TPU v7x, 128 devices: a whole 4x4x4 slice. The times are simulated.
128 devices in a mesh: dp: 4 (over z), gx: 4 (over x_lo, core), gy: 8 (over y, x_hi).
Axes of the slice: x: 4 (x_hi: 2, x_lo: 2; x = x_hi * 2 + x_lo), y: 4, z: 4, core: 2. Of those that a mesh axis runs over, the one named last changes fastest.
Arguments:
- tokens_in: bfloat16 [16384, 1600], P(('dp', 'gy'), 'gx'), may hold values from -6 to 6
- segments: int32 [16, 1024], P(('dp', 'gx'), 'gy'), may hold values from 0 to 2, as said below
- norm1_gain: float32 [1600], P('gx'), may hold values from 0.25 to 1.75
- norm1_bias: float32 [1600], P('gx'), may hold values from -4 to 4
- qkv_weight: bfloat16 [1600, 4800], P('gx', 'gy'), may hold values from -0.15625 to 0.15625
- query_bias: float32 [1600], replicated, may hold values from -6 to 6
- value_bias: float32 [1600], replicated, may hold values from -0.75 to 0.75
- proj_weight: bfloat16 [1600, 1600], P('gx', 'gy'), may hold values from -1.25 to 1.25
- proj_bias: float32 [1600], P('gx'), may hold values from -4 to 4
- norm2_gain: float32 [1600], P('gx'), may hold values from 0.25 to 1.75
- norm2_bias: float32 [1600], P('gx'), may hold values from -4 to 4
- fc_weight: bfloat16 [1600, 6400], P('gx', 'gy'), may hold values from -0.15625 to 0.15625
- fc_bias: float32 [6400], P('gy'), may hold values from -6 to 6
- out_weight: bfloat16 [1600, 6400], P('gx', 'gy'), may hold values from -0.078125 to 0.078125
- out_bias: float32 [1600], P('gx'), may hold values from -4 to 4
- out_grad: bfloat16 [16384, 1600], P(('dp', 'gy'), 'gx'), may hold values from -6 to 6
Outputs:
- layer_out: bfloat16 [16384, 1600], P(('dp', 'gy'), 'gx')
- input_grad: float32 [16384, 1600], P(('dp', 'gy'), 'gx')
- norm1_gain_grad: float32 [1600], P('gx')
- norm1_bias_grad: float32 [1600], P('gx')
- qkv_weight_grad: float32 [1600, 4800], P('gx', 'gy')
- query_bias_grad: float32 [1600], replicated
- value_bias_grad: float32 [1600], replicated
- proj_weight_grad: float32 [1600, 1600], P('gx', 'gy')
- proj_bias_grad: float32 [1600], P('gx')
- norm2_gain_grad: float32 [1600], P('gx')
- norm2_bias_grad: float32 [1600], P('gx')
- fc_weight_grad: float32 [1600, 6400], P('gx', 'gy')
- fc_bias_grad: float32 [6400], P('gy')
- out_weight_grad: float32 [1600, 6400], P('gx', 'gy')
- out_bias_grad: float32 [1600], P('gx')
Inputs may be any that keep to these rules, and one draw needn't show every extreme that they name: `segments`: each sequence of 1024 tokens holds three documents numbered 0, 1, 2 in order; document 1 has exactly 800 tokens and begins within the first eighth of the sequence.
All inputs are finite; a program needn't handle non-finite values.
Results may differ from a plain program's by a relative error of at most 0.014.
Values may be sent and summed in bfloat16 or wider, within the bound.
A program may use at most 192 MiB of HBM per device.

v0:
```python
import math

import jax
import jax.numpy as jnp
from jax import lax
from jax.sharding import PartitionSpec as P

HEADS = 25
HEAD_DIM = 64
FF = 6400
SEQ_LEN = 1024


NEG_FILL = -1e30


def gelu(value):
    return (
        0.5
        * value
        * (1.0 + jnp.tanh(0.7978845608028654 * (value + 0.044715 * value * value * value)))
    )


def row_totals(first, second):
    return lax.psum((jnp.sum(first, axis=1), jnp.sum(second, axis=1)), "gx")


def norm_forward(values, gain, shift):
    width = HEADS * HEAD_DIM
    total, squares = row_totals(values, values * values)
    mean = total / width
    spread = squares / width - mean * mean
    inverse = lax.rsqrt(spread + 1e-05)
    normed = (values - mean[:, None]) * inverse[:, None]
    return (normed * gain + shift, normed, inverse)


def norm_backward(grad, normed, inverse, gain):
    width = HEADS * HEAD_DIM
    scaled = grad * gain
    total, cross = row_totals(scaled, scaled * normed)
    return inverse[:, None] * (scaled - total[:, None] / width - normed * (cross[:, None] / width))


def gather_gy(values):
    return lax.all_gather(values, "gy", axis=0, tiled=True)


def gather_gx(values):
    return lax.all_gather(values, "gx", axis=0, tiled=True)


def sum_gx(left, weight):

    def term(start, count):
        return jnp.dot(left, weight, preferred_element_type=jnp.float32)

    return lax.psum_scatter(
        term(jnp.int32(0), lax.axis_size("gx") * (left.shape[0] // lax.axis_size("gx"))),
        "gx",
        scatter_dimension=0,
        tiled=True,
    )


def sum_gy(left, weight):

    def term(start, count):
        return lax.dot_general(
            left, weight, (((1,), (1,)), ((), ())), preferred_element_type=jnp.float32
        )

    return lax.psum_scatter(
        term(jnp.int32(0), lax.axis_size("gy") * (left.shape[0] // lax.axis_size("gy"))),
        "gy",
        scatter_dimension=0,
        tiled=True,
    )


def to_heads(values):
    shaped = values.reshape(values.shape[0] // SEQ_LEN, SEQ_LEN, values.shape[1])
    return lax.all_to_all(shaped, "gy", split_axis=1, concat_axis=2, tiled=True)


def to_rows(values):
    moved = lax.all_to_all(values, "gy", split_axis=2, concat_axis=1, tiled=True)
    return moved.reshape(moved.shape[0] * moved.shape[1], moved.shape[2])


def contract_rows(left, right):
    return lax.dot_general(
        left, right, (((0,), (0,)), ((), ())), preferred_element_type=jnp.float32
    )


def blockwise(step, carry, pieces):
    length = pieces[0].shape[1]
    size = math.gcd(length, 512)

    def inner(index, acc):
        offset = index * size
        parts = tuple((lax.dynamic_slice_in_dim(piece, offset, size, 1) for piece in pieces))
        return step(acc, parts, offset)

    return lax.fori_loop(0, length // size, inner, carry)


def masked_scores(queries, query_pos, query_seg, keys, key_pos, key_seg, scale):
    raw = jnp.einsum("sahe,sbhe->shab", queries, keys, preferred_element_type=jnp.float32) * scale
    allowed = (key_pos[None, None, :] <= query_pos[None, :, None]) & (
        key_seg[:, None, :] == query_seg[:, :, None]
    )
    return jnp.where(allowed[:, None], raw, NEG_FILL)


def probs_of(scores, top, total):
    return jnp.exp(scores - top[..., None]) / total[..., None]


def flip_last(values):
    return jnp.transpose(values, (0, 2, 1))


def per_device(
    tokens_in,
    segments,
    norm1_gain,
    norm1_bias,
    qkv_weight,
    query_bias,
    value_bias,
    proj_weight,
    proj_bias,
    norm2_gain,
    norm2_bias,
    fc_weight,
    fc_bias,
    out_weight,
    out_bias,
    out_grad,
):
    heads = HEADS
    head_dim = HEAD_DIM
    width = heads * head_dim
    scale = 1.0 / math.sqrt(head_dim)
    inputs = tokens_in.astype(jnp.float32)
    first, normed_one, inverse_one = norm_forward(inputs, norm1_gain, norm1_bias)
    rows_one = gather_gy(first.astype(jnp.bfloat16))
    linear = sum_gx(rows_one, qkv_weight)
    columns = linear.shape[1]
    bias_full = jnp.concatenate([query_bias, jnp.zeros_like(query_bias), value_bias])
    linear = linear + lax.dynamic_slice_in_dim(bias_full, lax.axis_index("gy") * columns, columns)
    token_qkv = to_heads(linear.astype(jnp.bfloat16))
    seq_count = token_qkv.shape[0]
    count = token_qkv.shape[1]
    triple = token_qkv.reshape(seq_count, count, 3, heads, head_dim)
    queries = triple[:, :, 0]
    keys = triple[:, :, 1]
    values = triple[:, :, 2]
    query_pos = lax.axis_index("gy") * count + jnp.arange(count, dtype=jnp.int32)

    def stat_step(carry, parts, start):
        top, total = carry
        key_part, seg_part = parts
        key_pos = start + jnp.arange(key_part.shape[1], dtype=jnp.int32)
        scores = masked_scores(queries, query_pos, segments, key_part, key_pos, seg_part, scale)
        new_top = jnp.maximum(top, jnp.max(scores, axis=-1))
        total = total * jnp.exp(top - new_top) + jnp.sum(
            jnp.exp(scores - new_top[..., None]), axis=-1
        )
        return (new_top, total)

    stat_init = (
        jnp.full((seq_count, heads, count), NEG_FILL, jnp.float32),
        jnp.zeros((seq_count, heads, count), jnp.float32),
    )
    top, total = blockwise(
        stat_step,
        stat_init,
        (
            lax.all_gather(keys, "gy", axis=1, tiled=True),
            lax.all_gather(segments, "gy", axis=1, tiled=True),
        ),
    )

    def visit(step, init):
        return blockwise(
            step,
            init,
            (
                lax.all_gather(keys, "gy", axis=1, tiled=True),
                lax.all_gather(values, "gy", axis=1, tiled=True),
                lax.all_gather(segments, "gy", axis=1, tiled=True),
            ),
        )

    def out_step(acc, parts, start):
        key_part, value_part, seg_part = parts
        key_pos = start + jnp.arange(key_part.shape[1], dtype=jnp.int32)
        scores = masked_scores(queries, query_pos, segments, key_part, key_pos, seg_part, scale)
        weights = probs_of(scores, top, total).astype(jnp.bfloat16)
        return acc + jnp.einsum(
            "shab,sbhe->sahe", weights, value_part, preferred_element_type=jnp.float32
        )

    attended = visit(out_step, jnp.zeros((seq_count, count, heads, head_dim), jnp.float32))
    att_rows = to_rows(attended.astype(jnp.bfloat16).reshape(seq_count, count, width))
    att_all = gather_gx(att_rows)
    resid = inputs + sum_gy(att_all, proj_weight) + proj_bias
    second, normed_two, inverse_two = norm_forward(resid, norm2_gain, norm2_bias)
    rows_two = gather_gy(second.astype(jnp.bfloat16))
    pre = sum_gx(rows_two, fc_weight) + fc_bias
    activated, gelu_pull = jax.vjp(gelu, pre)
    hidden_all = gather_gx(activated.astype(jnp.bfloat16))
    layer_out = resid + sum_gy(hidden_all, out_weight) + out_bias
    upstream = out_grad.astype(jnp.float32)
    out_bias_local = jnp.sum(upstream, axis=0)
    grad_rows_two = gather_gy(out_grad)
    out_weight_local = contract_rows(grad_rows_two, hidden_all)
    grad_hidden = sum_gx(grad_rows_two, out_weight)
    grad_pre = gelu_pull(grad_hidden)[0].astype(jnp.bfloat16)
    fc_bias_local = jnp.sum(grad_pre.astype(jnp.float32), axis=0)
    grad_pre_all = gather_gx(grad_pre)
    fc_weight_local = contract_rows(rows_two, grad_pre_all)
    grad_second = sum_gy(grad_pre_all, fc_weight)
    norm2_gain_local = jnp.sum(grad_second * normed_two, axis=0)
    norm2_bias_local = jnp.sum(grad_second, axis=0)
    grad_resid = upstream + norm_backward(grad_second, normed_two, inverse_two, norm2_gain)
    grad_branch = grad_resid.astype(jnp.bfloat16)
    proj_bias_local = jnp.sum(grad_branch.astype(jnp.float32), axis=0)
    grad_rows_one = gather_gy(grad_branch)
    proj_weight_local = contract_rows(grad_rows_one, att_all)
    grad_att = sum_gx(grad_rows_one, proj_weight).astype(jnp.bfloat16)
    grad_heads = to_heads(grad_att).reshape(seq_count, count, heads, head_dim)

    def delta_step(acc, parts, start):
        key_part, value_part, seg_part = parts
        key_pos = start + jnp.arange(key_part.shape[1], dtype=jnp.int32)
        scores = masked_scores(queries, query_pos, segments, key_part, key_pos, seg_part, scale)
        weights = probs_of(scores, top, total)
        product = jnp.einsum(
            "sahe,sbhe->shab", grad_heads, value_part, preferred_element_type=jnp.float32
        )
        return acc + jnp.sum(product * weights, axis=-1)

    delta = visit(delta_step, jnp.zeros((seq_count, heads, count), jnp.float32))

    def query_step(acc, parts, start):
        key_part, value_part, seg_part = parts
        key_pos = start + jnp.arange(key_part.shape[1], dtype=jnp.int32)
        scores = masked_scores(queries, query_pos, segments, key_part, key_pos, seg_part, scale)
        weights = probs_of(scores, top, total)
        product = jnp.einsum(
            "sahe,sbhe->shab", grad_heads, value_part, preferred_element_type=jnp.float32
        )
        grad_scores = (weights * (product - delta[..., None])).astype(jnp.bfloat16)
        return acc + jnp.einsum(
            "shab,sbhe->sahe", grad_scores, key_part, preferred_element_type=jnp.float32
        )

    grad_queries = (
        visit(query_step, jnp.zeros((seq_count, count, heads, head_dim), jnp.float32)) * scale
    )
    stats_rows = jnp.concatenate([flip_last(top), flip_last(total), flip_last(delta)], axis=2)
    all_stats = lax.all_gather(stats_rows, "gy", axis=1, tiled=True)

    def key_step(acc, parts, start):
        grad_keys, grad_values = acc
        query_part, grad_part, seg_part = parts
        size = query_part.shape[1]
        part_pos = start + jnp.arange(size, dtype=jnp.int32)
        stats_part = lax.dynamic_slice_in_dim(all_stats, start, size, 1)
        part_top = flip_last(stats_part[:, :, :heads])
        part_total = flip_last(stats_part[:, :, heads : 2 * heads])
        part_delta = flip_last(stats_part[:, :, 2 * heads :])
        scores = masked_scores(query_part, part_pos, seg_part, keys, query_pos, segments, scale)
        weights = probs_of(scores, part_top, part_total)
        grad_values = grad_values + jnp.einsum(
            "shab,sahe->sbhe",
            weights.astype(jnp.bfloat16),
            grad_part,
            preferred_element_type=jnp.float32,
        )
        product = jnp.einsum(
            "sahe,sbhe->shab", grad_part, values, preferred_element_type=jnp.float32
        )
        grad_scores = (weights * (product - part_delta[..., None])).astype(jnp.bfloat16)
        grad_keys = grad_keys + jnp.einsum(
            "shab,sahe->sbhe", grad_scores, query_part, preferred_element_type=jnp.float32
        )
        return (grad_keys, grad_values)

    empty = jnp.zeros((seq_count, count, heads, head_dim), jnp.float32)
    grad_keys, grad_values = blockwise(
        key_step,
        (empty, empty),
        (
            lax.all_gather(queries, "gy", axis=1, tiled=True),
            lax.all_gather(grad_heads, "gy", axis=1, tiled=True),
            lax.all_gather(segments, "gy", axis=1, tiled=True),
        ),
    )
    grad_qkv = (
        jnp.stack([grad_queries, grad_keys * scale, grad_values], axis=2)
        .reshape(seq_count, count, 3 * width)
        .astype(jnp.bfloat16)
    )
    qkv_bias_terms = jnp.sum(grad_qkv.astype(jnp.float32), axis=(0, 1))
    grad_qkv_all = gather_gx(to_rows(grad_qkv))
    qkv_weight_local = contract_rows(rows_one, grad_qkv_all)
    grad_first = sum_gy(grad_qkv_all, qkv_weight)
    norm1_gain_local = jnp.sum(grad_first * normed_one, axis=0)
    norm1_bias_local = jnp.sum(grad_first, axis=0)
    input_grad = grad_resid + norm_backward(grad_first, normed_one, inverse_one, norm1_gain)
    local_width = norm1_gain.shape[0]
    vectors = jnp.stack(
        [
            norm1_gain_local,
            norm1_bias_local,
            proj_bias_local,
            norm2_gain_local,
            norm2_bias_local,
            out_bias_local,
        ]
    )
    placed = lax.dynamic_update_slice(
        jnp.zeros((6, width), jnp.float32), vectors, (0, lax.axis_index("gx") * local_width)
    )
    fc_local_width = fc_bias.shape[0]
    fc_placed = lax.dynamic_update_slice(
        jnp.zeros((FF,), jnp.float32), fc_bias_local, (lax.axis_index("gy") * fc_local_width,)
    )
    query_value = jnp.stack([qkv_bias_terms[:width], qkv_bias_terms[2 * width :]])
    placed, fc_placed, query_value = lax.psum((placed, fc_placed, query_value), ("dp", "gx", "gy"))
    vectors = lax.dynamic_slice_in_dim(placed, lax.axis_index("gx") * local_width, local_width, 1)
    fc_bias_grad = lax.dynamic_slice_in_dim(
        fc_placed, lax.axis_index("gy") * fc_local_width, fc_local_width, 0
    )
    qkv_weight_grad, proj_weight_grad, fc_weight_grad, out_weight_grad = (
        lax.psum(qkv_weight_local.astype(jnp.bfloat16), "dp").astype(jnp.float32),
        lax.psum(proj_weight_local.astype(jnp.bfloat16), "dp").astype(jnp.float32),
        lax.psum(fc_weight_local.astype(jnp.bfloat16), "dp").astype(jnp.float32),
        lax.psum(out_weight_local.astype(jnp.bfloat16), "dp").astype(jnp.float32),
    )
    return (
        layer_out.astype(jnp.bfloat16),
        input_grad,
        vectors[0],
        vectors[1],
        qkv_weight_grad,
        query_value[0],
        query_value[1],
        proj_weight_grad,
        vectors[2],
        vectors[3],
        vectors[4],
        fc_weight_grad,
        fc_bias_grad,
        out_weight_grad,
        vectors[5],
    )


def solution(mesh):
    return jax.shard_map(
        per_device,
        mesh=mesh,
        in_specs=(
            P(("dp", "gy"), "gx"),
            P(("dp", "gx"), "gy"),
            P("gx"),
            P("gx"),
            P("gx", "gy"),
            P(),
            P(),
            P("gx", "gy"),
            P("gx"),
            P("gx"),
            P("gx"),
            P("gx", "gy"),
            P("gy"),
            P("gx", "gy"),
            P("gx"),
            P(("dp", "gy"), "gx"),
        ),
        out_specs=(
            P(("dp", "gy"), "gx"),
            P(("dp", "gy"), "gx"),
            P("gx"),
            P("gx"),
            P("gx", "gy"),
            P(),
            P(),
            P("gx", "gy"),
            P("gx"),
            P("gx"),
            P("gx"),
            P("gx", "gy"),
            P("gy"),
            P("gx", "gy"),
            P("gx"),
        ),
        check_vma=False,
    )
```

profile of v0, /device:TPU:27, one launch (start us, length us, event | category | flops | bytes accessed | tf_op | source)
XLA Modules:
  0.0 2014.3 jit_solution(17776053089696234846)
XLA Ops:
  16.8 64.8 %all-gather.16.cloned.1.call-done = bf16[4096,400]{0,1:T(8,128)(2,1)} async-done(((bf16[512,400]{0,1:T(8,128)(2,1)}), bf16[4096,400]{0,1:T(8,128)(2,1)}) %all-gather.16.cloned.1.call-update) | async-done | bytes 3276816 | tf_op jit(solution)/shard_map/all_gather | solution.py:47
  81.6 8.6 fusion.175
  91.0 90.5 %reduce-scatter.9.cloned.1.call-done = f32[1024,600]{0,1:T(8,128)} async-done(((f32[4096,600]{0,1:T(8,128)}), f32[1024,600]{0,1:T(8,128)}) %reduce-scatter.9.cloned.1.call-update) | async-done | bytes 2457616 | tf_op jit(solution)/shard_map/reduce_scatter | solution.py:59
  190.0 10.5 reduce.17
  205.1 22.5 %all_to_all.60 = bf16[8,2,38400]{2,1,0:T(2,128)(2,1)} all-to-all(bf16[8,2,38400]{2,1,0:T(2,128)(2,1)S(1)} %reshape.870), channel_id=1, replica_groups=mesh['dp'=4,'gx'=4,'gy'=8] {'gy'}, dimensions={0} | all-to-all | bytes 2457600 | tf_op jit(solution)/shard_map/all_to_all | solution.py:84
  239.1 14.6 all_gather.53
  253.8 48.0 %all-gather.36.cloned.1.call-done = bf16[1,1024,1,25,64]{1,4,3,2,0:T(8,128)(2,1)} async-done(((bf16[1,128,1,25,64]{1,4,3,2,0:T(8,128)(2,1)}), bf16[1,1024,1,25,64]{1,4,3,2,0:T(8,128)(2,1)}) %all-gather.36.cloned.1.call-update) | async-done | bytes 3276816 | tf_op jit(solution)/shard_map/all_gather | solution.py:193
  301.7 20.2 %while.74 = (s32[]{:T(128)}, f32[1,25,128]{2,1,0:T(8,128)S(1)}, f32[1,25,128]{2,1,0:T(8,128)S(1)}, s32[1,1024]{1,0:T(1,128)S(1)}, s32[1,128]{1,0:T(1,128)S(1)}, ...) while((s32[]{:T(128)}, f32[1,25,128]{2,1,0:T(8,128)S(1)}, ...), condition=%wide.region_8.9_spmd.clone, body=%wide.region_5.8_spmd.clone.sunk | while | flops 221397248 | bytes 15530174 | solution.py:107
  322.0 45.6 %all-gather.34.cloned.1.call-done = bf16[1,1024,1,25,64]{1,4,3,2,0:T(8,128)(2,1)} async-done(((bf16[1,128,1,25,64]{1,4,3,2,0:T(8,128)(2,1)}), bf16[1,1024,1,25,64]{1,4,3,2,0:T(8,128)(2,1)}) %all-gather.34.cloned.1.call-update) | async-done | bytes 3276816 | tf_op jit(solution)/shard_map/all_gather | solution.py:194
  367.5 9.6 while.75
  383.6 9.3 reduce.18
  393.1 12.2 all_to_all.61
  406.7 26.4 %all-gather.18.cloned.1.call-done = bf16[4096,200]{0,1:T(8,128)(2,1)} async-done(((bf16[1024,200]{0,1:T(8,128)(2,1)}), bf16[4096,200]{0,1:T(8,128)(2,1)}) %all-gather.18.cloned.1.call-update) | async-done | bytes 1638416 | tf_op jit(solution)/shard_map/all_gather | solution.py:51
  439.2 98.0 %reduce-scatter.11.cloned.1.call-done = f32[512,400]{0,1:T(8,128)} async-done(((f32[4096,400]{0,1:T(8,128)}), f32[512,400]{0,1:T(8,128)}) %reduce-scatter.11.cloned.1.call-update) | async-done | bytes 819216 | tf_op jit(solution)/shard_map/reduce_scatter | solution.py:74
  538.6 7.3 all-reduce.3
  547.0 55.9 %all-gather.24.cloned.1.call-done = bf16[4096,400]{0,1:T(8,128)(2,1)} async-done(((bf16[512,400]{0,1:T(8,128)(2,1)}), bf16[4096,400]{0,1:T(8,128)(2,1)}) %all-gather.24.cloned.1.call-update) | async-done | bytes 3276816 | tf_op jit(solution)/shard_map/all_gather | solution.py:47
  602.9 10.3 fusion.178
  613.6 55.0 %all-gather.20.cloned.1.call-done = bf16[4096,400]{0,1:T(8,128)(2,1)} async-done(((bf16[512,400]{0,1:T(8,128)(2,1)}), bf16[4096,400]{0,1:T(8,128)(2,1)}) %all-gather.20.cloned.1.call-update) | async-done | bytes 3276816 | tf_op jit(solution)/shard_map/all_gather | solution.py:47
  668.6 10.3 fusion.177
  679.0 109.9 %reduce-scatter.17.cloned.1.call-done = f32[1024,800]{0,1:T(8,128)} async-done(((f32[4096,800]{0,1:T(8,128)}), f32[1024,800]{0,1:T(8,128)}) %reduce-scatter.17.cloned.1.call-update) | async-done | bytes 3276816 | tf_op jit(solution)/shard_map/reduce_scatter | solution.py:59
  788.9 120.6 %reduce-scatter.13.cloned.1.call-done = f32[1024,800]{0,1:T(8,128)} async-done(((f32[4096,800]{0,1:T(8,128)}), f32[1024,800]{0,1:T(8,128)}) %reduce-scatter.13.cloned.1.call-update) | async-done | bytes 3276816 | tf_op jit(solution)/shard_map/reduce_scatter | solution.py:59
  916.7 67.4 %all-gather.26.cloned.1.call-done = bf16[4096,800]{0,1:T(8,128)(2,1)} async-done(((bf16[1024,800]{0,1:T(8,128)(2,1)}), bf16[4096,800]{0,1:T(8,128)(2,1)}) %all-gather.26.cloned.1.call-update) | async-done | bytes 6553616 | tf_op jit(solution)/shard_map/all_gather | solution.py:51
  984.0 8.4 fusion.182
  992.5 98.9 %reduce-scatter.19.cloned.1.call-done = f32[512,400]{0,1:T(8,128)} async-done(((f32[4096,400]{0,1:T(8,128)}), f32[512,400]{0,1:T(8,128)}) %reduce-scatter.19.cloned.1.call-update) | async-done | bytes 819216 | tf_op jit(solution)/shard_map/reduce_scatter | solution.py:74
  1103.6 62.1 %all-gather.28.cloned.1.call-done = bf16[4096,400]{0,1:T(8,128)(2,1)} async-done(((bf16[512,400]{0,1:T(8,128)(2,1)}), bf16[4096,400]{0,1:T(8,128)(2,1)}) %all-gather.28.cloned.1.call-update) | async-done | bytes 3276816 | tf_op jit(solution)/shard_map/all_gather | solution.py:47
  1171.1 37.9 %reduce-scatter.21.cloned.1.call-done = f32[1024,200]{0,1:T(8,128)} async-done(((f32[4096,200]{0,1:T(8,128)}), f32[1024,200]{0,1:T(8,128)}) %reduce-scatter.21.cloned.1.call-update) | async-done | bytes 819216 | tf_op jit(solution)/shard_map/reduce_scatter | solution.py:59
  1223.3 12.3 all-to-all-done.2
  1241.6 11.6 while.76
  1253.3 30.2 %all_gather.62 = f32[1,1024,75]{1,2,0:T(8,128)S(1)} all-gather(f32[1,128,75]{1,2,0:T(8,128)S(1)} %pad_maximum_fusion), channel_id=1, replica_groups=mesh['dp'=4,'gx'=4,'gy'=8] {'gy'}, dimensions={1}, use_global_device_ids=true | all-gather | bytes 345600 | tf_op jit(solution)/shard_map/all_gather | solution.py:267
  1283.4 26.9 %while.77 = (s32[]{:T(128)}, f32[1,128,25,64]{1,3,2,0:T(8,128)}, bf16[1,1024,25,64]{1,3,2,0:T(8,128)(2,1)}, s32[1,1024]{1,0:T(1,128)S(1)}, s32[1,128]{1,0:T(1,12...) while((s32[]{:T(128)}, f32[1,128,25,64]{1,3,2,0:T(8,128)}, ...), condition=%wide.region_29.30_spmd.clone, body=%wide.region_28.29_spmd.clone.sunk | while | flops 641221248 | bytes 22301432 | solution.py:107
  1289.0 7.7 fusion.255
  1302.4 7.9 fusion.255
  1311.6 37.8 %all-gather.30.cloned.1.call-done = bf16[1,1024,25,64]{1,3,2,0:T(8,128)(2,1)} async-done(((bf16[1,128,25,64]{1,3,2,0:T(8,128)(2,1)}), bf16[1,1024,25,64]{1,3,2,0:T(8,128)(2,1)}) %all-gather.30.cloned.1.call-update) | async-done | bytes 3276816 | tf_op jit(solution)/shard_map/all_gather | solution.py:301
  1349.4 37.5 %while.78 = (s32[]{:T(128)}, f32[1,128,25,64]{1,3,2,0:T(8,128)S(1)}, f32[1,128,25,64]{1,3,2,0:T(8,128)S(1)}, bf16[1,1024,25,64]{1,3,2,0:T(8,128)(2,1)}, s32[1,12...) while((s32[]{:T(128)}, ...), condition=%wide.region_31.0_spmd.clone, body=%wide.region_30.31_spmd.clone.sunk | while | flops 852984448 | bytes 30915852 | solution.py:107
  1349.8 7.2 exponential_divide_fusion.2
  1368.5 7.2 exponential_divide_fusion.2
  1387.7 20.0 copy.99
  1407.7 27.5 %reduce.20 = bf16[4800,128]{1,0:T(8,128)(2,1)} reduce(bf16[4800,1,128]{2,1,0:T(2,128)(2,1)S(1)} %bitcast.436, bf16[]{:T(256)} %broadcast.627), dimensions={1}, to_apply=%bitcast.319.reduce_sub_computation | reduce | bytes 2457602
  1438.4 21.1 %all_to_all.62 = bf16[8,2,38400]{2,1,0:T(2,128)(2,1)} all-to-all(bf16[8,2,38400]{2,1,0:T(2,128)(2,1)S(1)} %reshape.876), channel_id=1, replica_groups=mesh['dp'=4,'gx'=4,'gy'=8] {'gy'}, dimensions={0} | all-to-all | bytes 2457600 | tf_op jit(solution)/shard_map/all_to_all | solution.py:88
  1466.2 53.1 %all-gather.32.cloned.1.call-done = bf16[4096,600]{0,1:T(8,128)(2,1)} async-done(((bf16[1024,600]{0,1:T(8,128)(2,1)}), bf16[4096,600]{0,1:T(8,128)(2,1)}) %all-gather.32.cloned.1.call-update) | async-done | bytes 4915216 | tf_op jit(solution)/shard_map/all_gather | solution.py:51
  1526.4 61.5 %all-gather.22.cloned.1.call-done = bf16[4096,800]{0,1:T(8,128)(2,1)} async-done(((bf16[1024,800]{0,1:T(8,128)(2,1)}), bf16[4096,800]{0,1:T(8,128)(2,1)}) %all-gather.22.cloned.1.call-update) | async-done | bytes 6553616 | tf_op jit(solution)/shard_map/all_gather | solution.py:51
  1587.9 8.3 fusion.181
  1596.5 8.4 convolution_convert_fusion.1
  1618.5 72.7 %reduce-scatter.23.cloned.1.call-done = f32[512,400]{0,1:T(8,128)} async-done(((f32[4096,400]{0,1:T(8,128)}), f32[512,400]{0,1:T(8,128)}) %reduce-scatter.23.cloned.1.call-update) | async-done | bytes 819216 | tf_op jit(solution)/shard_map/reduce_scatter | solution.py:74
  1692.7 7.3 all-reduce.1
  1700.0 93.8 %reduce-scatter.15.cloned.1.call-done = f32[512,400]{0,1:T(8,128)} async-done(((f32[4096,400]{0,1:T(8,128)}), f32[512,400]{0,1:T(8,128)}) %reduce-scatter.15.cloned.1.call-update) | async-done | bytes 819216 | tf_op jit(solution)/shard_map/reduce_scatter | solution.py:74
  1798.1 61.9 %all-reduce.11.cloned.1.call-done = (bf16[400,600]{1,0:T(8,128)(2,1)}, bf16[400,200]{1,0:T(8,128)(2,1)}, bf16[400,800]{1,0:T(8,128)(2,1)}, bf16[400,800]{1,0:T(8,128)(2,1)}) async-done(((bf16[400,600]{1,0:T(8,128)(2,1)}, bf16[400,200]{1,0:T(8,128)(2,1)}, bf16[400,800]{1,0:T(8,128)(2,1)}, bf16[400,800]{1,0:T(8,128)(2,1)}), (bf16[400,600]{1,0:T(8,128)(2,1)}, bf16[400,200]{1,0:T(8,128)(2,1)}, ...) | async-done | bytes 1920016 | tf_op jit(solution)/shard_map/psum | solution.py:342
  1866.5 136.4 %all-reduce.9.cloned.1.call-done = (f32[6,1600]{1,0:T(8,128)}, f32[2,1600]{1,0:T(2,128)}, f32[6400]{0:T(1024)}) async-done(((f32[6,1600]{1,0:T(8,128)}, f32[2,1600]{1,0:T(2,128)}, f32[6400]{0:T(1024)}), (f32[6,1600]{1,0:T(8,128)}, f32[2,1600]{1,0:T(2,128)}, f32[6400]{0:T(1024)})) %all-reduce.9.cloned.1.call-update) | async-done | bytes 76816 | tf_op jit(solution)/shard_map/psum | solution.py:336
  (302 shorter events, 221.3 us)
Async XLA Ops:
  7.2 661.4 %copy-start = (bf16[400,800]{1,0:T(8,128)(2,1)S(1)}, bf16[400,800]{1,0:T(8,128)(2,1)}, u32[]{:S(2)}) copy-start(bf16[400,800]{1,0:T(8,128)(2,1)} %param.37) | copy-start | bytes 1920004
  7.2 74.4 %all-gather.16.cloned.1.call-start = ((), (), s32[]{:S(2)}) async-start(), calls=%async_computation.12 | async-start | bytes 3686400 | tf_op jit(solution)/shard_map/all_gather | solution.py:47
  16.7 164.8 %reduce-scatter.9.cloned.1.call-start = ((), (), s32[]{:S(2)}) async-start(), calls=%async_computation.13 | async-start | bytes 12288000 | tf_op jit(solution)/shard_map/reduce_scatter | solution.py:59
  90.2 211.5 %all-gather.36.cloned.1.call-start = ((), (), s32[]{:S(2)}) async-start(), calls=%async_computation.30 | async-start | bytes 3686400 | tf_op jit(solution)/shard_map/all_gather | solution.py:193
  238.5 129.0 %all-gather.34.cloned.1.call-start = ((), (), s32[]{:S(2)}) async-start(), calls=%async_computation.29 | async-start | bytes 3686400 | tf_op jit(solution)/shard_map/all_gather | solution.py:194
  239.1 194.1 %all-gather.18.cloned.1.call-start = ((), (), s32[]{:S(2)}) async-start(), calls=%async_computation.14 | async-start | bytes 2048000 | tf_op jit(solution)/shard_map/all_gather | solution.py:51
  406.6 130.5 %reduce-scatter.11.cloned.1.call-start = ((), (), s32[]{:S(2)}) async-start(), calls=%async_computation.15 | async-start | bytes 7372800 | tf_op jit(solution)/shard_map/reduce_scatter | solution.py:74
  438.3 98.9 %copy-start.7 = (bf16[512,400]{0,1:T(8,128)(2,1)S(1)}, bf16[512,400]{0,1:T(8,128)(2,1)}, u32[]{:S(2)}) copy-start(bf16[512,400]{0,1:T(8,128)(2,1)} %param.26) | copy-start | bytes 1228804
  438.3 98.9 %copy-start.42 = (f32[400]{0:T(512)S(1)}, f32[400]{0:T(512)}, u32[]{:S(2)}) copy-start(f32[400]{0:T(512)} %param.34) | copy-start | bytes 4804
  438.3 107.6 %copy-start.24 = (f32[400]{0:T(512)S(1)}, f32[400]{0:T(512)}, u32[]{:S(2)}) copy-start(f32[400]{0:T(512)} %param.35) | copy-start | bytes 4804
  438.3 107.6 %copy-start.43 = (f32[400]{0:T(512)S(1)}, f32[400]{0:T(512)}, u32[]{:S(2)}) copy-start(f32[400]{0:T(512)} %param.36) | copy-start | bytes 4804
  438.4 164.5 %copy-start.47 = (bf16[400,800]{1,0:T(8,128)(2,1)S(1)}, bf16[400,800]{1,0:T(8,128)(2,1)}, u32[]{:S(2)}) copy-start(bf16[400,800]{1,0:T(8,128)(2,1)} %param.39) | copy-start | bytes 1920004
  438.4 164.5 %all-gather.24.cloned.1.call-start = ((), (), s32[]{:S(2)}) async-start(), calls=%async_computation.20 | async-start | bytes 3686400 | tf_op jit(solution)/shard_map/all_gather | solution.py:47
  439.1 229.5 %all-gather.20.cloned.1.call-start = ((), (), s32[]{:S(2)}) async-start(), calls=%async_computation.16 | async-start | bytes 3686400 | tf_op jit(solution)/shard_map/all_gather | solution.py:47
  538.6 562.1 %copy-start.3 = (f32[512,400]{0,1:T(8,128)}, f32[512,400]{0,1:T(8,128)S(1)}, u32[]{:S(2)}) copy-start(f32[512,400]{0,1:T(8,128)S(1)} %get-tuple-element.1298) | copy-start | bytes 2457604
  545.9 554.8 %copy-start.20 = (f32[512]{0:T(512)}, f32[512]{0:T(512)S(1)}, u32[]{:S(2)}) copy-start(f32[512]{0:T(512)S(1)} %get-tuple-element.1322) | copy-start | bytes 6148
  545.9 554.8 %copy-start.22 = (f32[512]{0:T(512)}, f32[512]{0:T(512)S(1)}, u32[]{:S(2)}) copy-start(f32[512]{0:T(512)S(1)} %get-tuple-element.1323) | copy-start | bytes 6148
  546.9 241.9 %reduce-scatter.17.cloned.1.call-start = ((), (), s32[]{:S(2)}) async-start(), calls=%async_computation.21 | async-start | bytes 16384000 | tf_op jit(solution)/shard_map/reduce_scatter | solution.py:59
  613.2 296.2 %reduce-scatter.13.cloned.1.call-start = ((), (), s32[]{:S(2)}) async-start(), calls=%async_computation.17 | async-start | bytes 16384000 | tf_op jit(solution)/shard_map/reduce_scatter | solution.py:59
  678.9 230.5 %copy-start.41 = (f32[800]{0:T(1024)S(1)}, f32[800]{0:T(1024)}, u32[]{:S(2)}) copy-start(f32[800]{0:T(1024)} %param.38) | copy-start | bytes 9604
  678.9 305.1 %all-gather.26.cloned.1.call-start = ((), (), s32[]{:S(2)}) async-start(), calls=%async_computation.22 | async-start | bytes 8192000 | tf_op jit(solution)/shard_map/all_gather | solution.py:51
  916.6 174.7 %reduce-scatter.19.cloned.1.call-start = ((), (), s32[]{:S(2)}) async-start(), calls=%async_computation.23 | async-start | bytes 7372800 | tf_op jit(solution)/shard_map/reduce_scatter | solution.py:74
  992.4 108.3 %copy-start.11 = (bf16[512,400]{0,1:T(8,128)(2,1)S(1)}, bf16[512,400]{0,1:T(8,128)(2,1)}, u32[]{:S(2)}) copy-start(bf16[512,400]{0,1:T(8,128)(2,1)} %param.41) | copy-start | bytes 1228804
  992.5 173.2 %all-gather.28.cloned.1.call-start = ((), (), s32[]{:S(2)}) async-start(), calls=%async_computation.24 | async-start | bytes 3686400 | tf_op jit(solution)/shard_map/all_gather | solution.py:47
  1103.6 105.4 %reduce-scatter.21.cloned.1.call-start = ((), (), s32[]{:S(2)}) async-start(), calls=%async_computation.25 | async-start | bytes 4096000 | tf_op jit(solution)/shard_map/reduce_scatter | solution.py:59
  1170.5 141.1 %all-gather.38.cloned.1.call-start = ((), (), s32[]{:S(2)}) async-start(), calls=%async_computation.31 | async-start | bytes 3686400 | tf_op jit(solution)/shard_map/all_gather | solution.py:300
  1217.3 18.4 all-to-all-start.2
  1223.3 126.1 %all-gather.30.cloned.1.call-start = ((), (), s32[]{:S(2)}) async-start(), calls=%async_computation.26 | async-start | bytes 3686400 | tf_op jit(solution)/shard_map/all_gather | solution.py:301
  1241.6 277.6 %all-gather.32.cloned.1.call-start = ((), (), s32[]{:S(2)}) async-start(), calls=%async_computation.27 | async-start | bytes 6144000 | tf_op jit(solution)/shard_map/all_gather | solution.py:51
  1465.5 122.4 %all-gather.22.cloned.1.call-start = ((), (), s32[]{:S(2)}) async-start(), calls=%async_computation.18 | async-start | bytes 8192000 | tf_op jit(solution)/shard_map/all_gather | solution.py:51
  1466.1 225.1 %reduce-scatter.23.cloned.1.call-start = ((), (), s32[]{:S(2)}) async-start(), calls=%async_computation.28 | async-start | bytes 7372800 | tf_op jit(solution)/shard_map/reduce_scatter | solution.py:74
  1526.4 267.4 %reduce-scatter.15.cloned.1.call-start = ((), (), s32[]{:S(2)}) async-start(), calls=%async_computation.19 | async-start | bytes 7372800 | tf_op jit(solution)/shard_map/reduce_scatter | solution.py:74
  1596.2 263.7 %all-reduce.11.cloned.1.call-start = ((), (), s32[]{:S(2)}) async-start(), calls=%async_computation.33 | async-start | bytes 4300800 | tf_op jit(solution)/shard_map/psum | solution.py:342
  1617.2 176.6 %copy-start.4 = (f32[512,400]{0,1:T(8,128)S(1)}, f32[512,400]{0,1:T(8,128)}, u32[]{:S(2)}) copy-start(f32[512,400]{0,1:T(8,128)} %copy-done.3) | copy-start | bytes 2457604
  1617.2 176.6 %copy-start.9 = (f32[512,400]{0,1:T(8,128)S(1)}, f32[512,400]{0,1:T(8,128)}, u32[]{:S(2)}) copy-start(f32[512,400]{0,1:T(8,128)} %reduce-scatter.19.cloned.1.call-done) | copy-start | bytes 2457604
  1617.2 176.6 %copy-start.12 = (bf16[512,400]{0,1:T(8,128)(2,1)S(1)}, bf16[512,400]{0,1:T(8,128)(2,1)}, u32[]{:S(2)}) copy-start(bf16[512,400]{0,1:T(8,128)(2,1)} %param.41) | copy-start | bytes 1228804
  1617.2 176.6 %copy-start.21 = (f32[512]{0:T(512)S(1)}, f32[512]{0:T(512)}, u32[]{:S(2)}) copy-start(f32[512]{0:T(512)} %copy-done.20) | copy-start | bytes 6148
  1617.2 176.6 %copy-start.23 = (f32[512]{0:T(512)S(1)}, f32[512]{0:T(512)}, u32[]{:S(2)}) copy-start(f32[512]{0:T(512)} %copy-done.22) | copy-start | bytes 6148
  1617.2 176.6 %copy-start.25 = (f32[400]{0:T(512)S(1)}, f32[400]{0:T(512)}, u32[]{:S(2)}) copy-start(f32[400]{0:T(512)} %param.35) | copy-start | bytes 4804
  1617.2 176.6 %copy-start.32 = (f32[512]{0:T(512)S(1)}, f32[512]{0:T(512)}, u32[]{:S(2)}) copy-start(f32[512]{0:T(512)} %copy-done.31) | copy-start | bytes 6148
  1617.3 176.6 %copy-start.34 = (f32[512]{0:T(512)S(1)}, f32[512]{0:T(512)}, u32[]{:S(2)}) copy-start(f32[512]{0:T(512)} %copy-done.33) | copy-start | bytes 6148
  1617.3 176.6 %copy-start.44 = (f32[400]{0:T(512)S(1)}, f32[400]{0:T(512)}, u32[]{:S(2)}) copy-start(f32[400]{0:T(512)} %param.40) | copy-start | bytes 4804
  1617.3 385.6 %all-reduce.9.cloned.1.call-start = ((), (), s32[]{:S(2)}) async-start(), calls=%async_computation.32 | async-start | bytes 190464 | tf_op jit(solution)/shard_map/psum | solution.py:336
  1617.7 179.3 %copy-start.19 = (f32[6400]{0:T(1024)}, f32[6400]{0:T(1024)S(1)}, u32[]{:S(2)}) copy-start(f32[6400]{0:T(1024)S(1)} %dynamic_update_slice.7) | copy-start | bytes 76804
  1618.5 178.5 %copy-start.36 = (f32[400]{0:T(512)S(1)}, f32[400]{0:T(512)}, u32[]{:S(2)}) copy-start(f32[400]{0:T(512)} %get-tuple-element.1159) | copy-start | bytes 4804
  1618.5 178.5 %copy-start.37 = (f32[400]{0:T(512)S(1)}, f32[400]{0:T(512)}, u32[]{:S(2)}) copy-start(f32[400]{0:T(512)} %get-tuple-element.1165) | copy-start | bytes 4804
  1618.5 178.5 %copy-start.38 = (f32[400]{0:T(512)S(1)}, f32[400]{0:T(512)}, u32[]{:S(2)}) copy-start(f32[400]{0:T(512)} %get-tuple-element.1296) | copy-start | bytes 4804
  1860.0 147.3 %copy-start.1 = (bf16[400,800]{1,0:T(8,128)(2,1)S(1)}, bf16[400,800]{1,0:T(8,128)(2,1)}, u32[]{:S(2)}) copy-start(bf16[400,800]{1,0:T(8,128)(2,1)} %param.37) | copy-start | bytes 1920004
  (29 other events, 758.1 us)
Sparse Core Ops, SparseCore 0:
  16.9 64.7 all-gather.15
  90.3 91.1 reduce-scatter.8
  238.6 63.0 all-gather.35
  304.6 62.9 all-gather.33
  406.8 26.3 all-gather.17
  438.5 98.6 reduce-scatter.10
  539.4 63.4 all-gather.23
  605.6 62.9 all-gather.19
  671.1 117.7 reduce-scatter.16
  791.2 118.2 reduce-scatter.12
  916.7 67.2 all-gather.25
  992.6 98.7 reduce-scatter.18
  1103.7 61.9 all-gather.27
  1170.6 38.3 reduce-scatter.20
  1211.8 72.2 all-gather.37
  1287.0 62.4 all-gather.29
  1465.7 53.5 all-gather.31
  1520.9 66.9 all-gather.21
  1592.3 98.8 reduce-scatter.22
  1694.9 98.8 reduce-scatter.14
  1797.8 62.1 all-reduce.10
  1865.3 137.5 all-reduce.8
where the time goes:
time: 2020 us; the launch traced here: 2010 us
  waiting for transfers between devices  1510 us (75%)
  matrix products  178 us (9%)
  blocking collectives  128 us (6%)
  other arithmetic  97.8 us (5%)
  local copies, waits for them, and re-layouts  74 us (4%)
    reduce_scatter x4, waiting for transfers between devices, sum_gy(): lax.psum_scatter(term(jnp.int32(0), lax.axis_size('gy') * (left.shape[0]...  363 us
    reduce_scatter x4, waiting for transfers between devices, sum_gx(): lax.psum_scatter(term(jnp.int32(0), lax.axis_size('gx') * (left.shape[0]...  359 us
    all_gather x4, waiting for transfers between devices, gather_gy(): return lax.all_gather(values, 'gy', axis=0, tiled=True)  238 us
    all_gather x4, waiting for transfers between devices, gather_gx(): return lax.all_gather(values, 'gx', axis=0, tiled=True)  208 us
    psum x1, waiting for transfers between devices, per_device(): lax.psum((placed, fc_placed, query_value), ('dp', 'gx', 'gy'))  136 us
    psum x1, waiting for transfers between devices, per_device(): lax.psum(qkv_weight_local.astype(jnp.bfloat16), 'dp').astype(jnp.float32)  61.9 us
    unnamed x12, other arithmetic  51.6 us
    all_gather x1, waiting for transfers between devices, visit(): lax.all_gather(keys, 'gy', axis=1, tiled=True)  48 us
  transfers between devices with their start and end apart: 23, of which 22 were waited for; matrix products, arithmetic and copies ran while one was open for 7% of the time, Pallas kernels for 0%

commit v1 on v0

v1 whole, which is shorter than its diff:
```python
import math

import jax
import jax.numpy as jnp
from jax import lax
from jax.experimental import pallas as pl
from jax.experimental.pallas import tpu as pltpu
from jax.sharding import PartitionSpec as P

BF = jnp.bfloat16
F32 = jnp.float32
HEADS = 25
HEAD_DIM = 64
D = HEADS * HEAD_DIM
FF = 6400
SEQ = 1024
DOC = 800
ROWS = 128
QUARTER = 400
SUB = 200
FPAD = 208
FRAME = 256
TAIL = 64
NEG = -1e30
MESH = pl.DeviceIdType.MESH
VMEM = pl.BlockSpec(memory_space=pltpu.VMEM)
SMEM = pl.BlockSpec(memory_space=pltpu.SMEM)


def nt(a, b):
    return lax.dot_general(a, b, (((1,), (1,)), ((), ())), preferred_element_type=F32)


def nn(a, b):
    return lax.dot_general(a, b, (((1,), (0,)), ((), ())), preferred_element_type=F32)


def tn(a, b):
    return lax.dot_general(a, b, (((0,), (0,)), ((), ())), preferred_element_type=F32)


class Here:
    def __init__(self):
        self.z, self.gx, self.gy = (lax.axis_index(a) for a in ("dp", "gx", "gy"))
        self.y, self.xh = self.gy // 2, lax.rem(self.gy, 2)
        self.x = self.xh * 2 + self.gx // 2
        self.c = lax.rem(self.gx, 2)
        self.p = self.x * 2 + self.c

    def at(self, x, c, y, z):
        return (z, lax.rem(x, 2) * 2 + c, y * 2 + x // 2)

    def rel(self, dx=0, flip=0, dy=0, dz=0):
        c = 1 - self.c if flip else self.c
        return self.at(
            lax.rem(self.x + 4 + dx, 4), c, lax.rem(self.y + 4 + dy, 4), lax.rem(self.z + 4 + dz, 4)
        )

    def ring(self):
        return [self.rel(dx, f) for dx in range(4) for f in (0, 1) if dx or f]

    def gxd(self, d):
        return (self.z, self.gx ^ d, self.gy)

    def unit(self, i):
        if i == 3:
            return self.gy, 3
        t = 3 * self.gy + i
        return lax.rem(t, 8), t // 8

    def block(self, kind, p):
        if kind == 3:
            return p, 3
        t = kind * 8 + p
        return t // 3, lax.rem(t, 3)

    def holds(self, kind):
        return self.block(kind, self.p)[0] // 2 == self.y


def meet(peers):
    sem = pltpu.get_barrier_semaphore()
    for d in peers:
        pl.semaphore_signal(sem, inc=1, device_id=d, device_id_type=MESH)
    pl.semaphore_wait(sem, len(peers))


def push(src, dst, ss, rs, d):
    return pltpu.make_async_remote_copy(
        src_ref=src, dst_ref=dst, send_sem=ss, recv_sem=rs, device_id=d, device_id_type=MESH
    )


def stats(v):
    mean = jnp.sum(v, axis=1, keepdims=True) / D
    spread = jnp.sum(v * v, axis=1, keepdims=True) / D - mean * mean
    inv = lax.rsqrt(spread + 1e-5)
    return (v - mean) * inv, inv


def norm_back(u, gain, normed, inv):
    w = u * gain
    a = jnp.sum(w, axis=1, keepdims=True) / D
    b = jnp.sum(w * normed, axis=1, keepdims=True) / D
    return inv * (w - a - normed * b)


def rows_of(v):
    return jnp.sum(v, axis=0, keepdims=True)


class Gather:
    SEMS = 9

    def __init__(self, here, buf, ss, rs, base):
        self.h, self.buf, self.ss, self.rs, self.base = here, buf, ss, rs, base

    def slot(self, dx):
        return lax.rem(self.h.x + 4 + dx, 4) * 2 + self.h.c

    def go(self, k, slot, d, half=None):
        ref = self.buf.at[slot] if half is None else self.buf.at[slot, pl.ds(half * 64, 64)]
        i = self.base + k
        copy = push(ref, ref, self.ss.at[i], self.rs.at[i], d)
        copy.start()
        return copy

    def start(self):
        h = self.h
        self.right, self.left, self.sib = h.rel(1), h.rel(-1), h.rel(0, 1)
        self.a0 = self.go(0, self.slot(0), self.right)
        self.a1 = self.go(1, self.slot(0), self.left)
        self.f0 = self.go(2, self.slot(0), self.sib)

    def ready(self, s):
        h = self.h
        if s == 0:
            self.f0.wait_recv()
            return h.x
        if s == 1:
            self.a0.wait_recv()
            self.r0 = self.go(3, self.slot(-1), self.right, 0)
            self.f1 = self.go(5, self.slot(-1), self.sib)
            self.a1.wait_recv()
            self.r1 = self.go(4, self.slot(1), self.left, 1)
            self.f2 = self.go(6, self.slot(1), self.sib)
            self.f1.wait_recv()
            return lax.rem(h.x + 3, 4)
        if s == 2:
            self.f2.wait_recv()
            return lax.rem(h.x + 1, 4)
        self.r0.wait_recv()
        self.f3 = self.go(7, self.slot(2), self.sib, 0)
        self.r1.wait_recv()
        self.f4 = self.go(8, self.slot(2), self.sib, 1)
        self.f3.wait_recv()
        self.f4.wait_recv()
        return lax.rem(h.x + 2, 4)

    def finish(self):
        for c in (self.a0, self.a1, self.r0, self.r1, self.f0, self.f1, self.f2, self.f3, self.f4):
            c.wait_send()


class Scatter:
    SEMS = 7

    @staticmethod
    def scratch():
        return [
            pltpu.VMEM((2, ROWS, D), F32),
            pltpu.VMEM((4, ROWS, D), F32),
            pltpu.VMEM((4, ROWS, D), BF),
            pltpu.VMEM((4, ROWS, D), BF),
            pltpu.VMEM((3, ROWS, D), BF),
            pltpu.VMEM((3, ROWS, D), BF),
        ]

    def __init__(self, here, refs, ss, rs, base):
        self.h, self.ss, self.rs, self.base = here, ss, rs, base
        self.both, self.own, self.give, self.got, self.sums, self.far = refs
        self.steps = (2, 1, -1, 0)
        self.copies = {}

    def part(self, j, term):
        h = self.h
        chip = lax.rem(h.x + 4 + self.steps[j], 4)
        self.both[...] = term(chip).reshape(2, ROWS, D)
        self.own[j] = self.both[h.c]
        self.give[j] = self.both[1 - h.c].astype(BF)
        i = self.base + j
        c = push(self.give.at[j], self.got.at[j], self.ss.at[i], self.rs.at[i], h.rel(0, 1))
        c.start()
        self.copies[j] = c

    def combine(self, j):
        self.copies[j].wait_recv()
        if j == 3:
            return
        self.sums[j] = (self.own[j] + self.got[j].astype(F32)).astype(BF)
        i = self.base + 4 + j
        c = push(
            self.sums.at[j], self.far.at[j], self.ss.at[i], self.rs.at[i], self.h.rel(self.steps[j])
        )
        c.start()
        self.copies[4 + j] = c

    def run(self, term):
        self.part(0, term)
        self.part(1, term)
        self.combine(0)
        self.part(2, term)
        self.combine(1)
        self.part(3, term)
        self.combine(2)
        self.combine(3)

    def result(self):
        total = self.own[3] + self.got[3].astype(F32)
        for j in range(3):
            self.copies[4 + j].wait_recv()
            total = total + self.far[j].astype(F32)
        for c in self.copies.values():
            c.wait_send()
        return total


def join(blocks):
    return jnp.concatenate(blocks, axis=1)


def entry_kernel(
    tok, grd, wa, ff, vec, rows, grads, units, hidden, vecs,
    rt, rg, rwa, rff, rv, tsend, trecv, scr, frames, ss, rs, rsw,
):
    h = Here()
    nxt = lax.rem(h.gy + 1, 8)
    prv = lax.rem(h.gy + 7, 8)
    meet(h.ring() + [(h.z, h.gx, nxt), (h.z, h.gx, prv)])
    for k, i in enumerate((2, 3)):
        tsend[k] = wa[i].astype(F32)[SUB - TAIL :].astype(BF)
    tail = push(tsend, trecv, ss.at[0], rs.at[0], (h.z, h.gx, nxt))
    tail.start()
    copies = []
    for d in (1, 2, 3):
        for k, (src, dst) in enumerate(((tok, rt), (ff, rff), (grd, rg))):
            i = 3 * d + k
            copies.append(push(src.at[h.gx ^ d], dst.at[h.gx], ss.at[i], rs.at[i], h.gxd(d)))
        copies.append(push(vec, rv.at[h.gx], ss.at[12 + d], rs.at[12 + d], h.gxd(d)))
    for c in copies:
        c.start()
    rt[h.gx] = tok[h.gx]
    rg[h.gx] = grd[h.gx]
    rff[h.gx] = ff[h.gx]
    rv[h.gx] = vec[...]

    sends = []
    row = lax.broadcasted_iota(jnp.int32, (FRAME, QUARTER), 0)
    for i in (1, 2, 0, 3):
        p, kind = h.unit(i)
        if i == 0:
            tail.wait_recv()
        before = wa[i - 1].astype(F32)[SUB - TAIL :] if i in (1, 2) else trecv[i // 3].astype(F32)
        scr[pl.ds(pl.multiple_of(8 * p, 8), TAIL)] = before
        scr[pl.ds(pl.multiple_of(8 * p + TAIL, 8), SUB)] = wa[i].astype(F32)
        frame = jnp.where((row < 192) | (p == 7), scr[TAIL : TAIL + FRAME], 0.0)
        frames[i] = frame.astype(BF)
        c = push(
            frames.at[i], rwa.at[kind, h.gx], ss.at[16 + i], rsw.at[kind, h.gx],
            h.at(p // 2, lax.rem(p, 2), h.y, h.z),
        )
        mine = p == h.p

        @pl.when(mine)
        def _(i=i, kind=kind):
            rwa[kind, h.gx] = frames[i]

        @pl.when(jnp.logical_not(mine))
        def _(c=c):
            c.start()

        sends.append((c, mine))
    for c in copies:
        c.wait_recv()
    rows[...] = join([rt[g] for g in range(4)])
    grads[...] = join([rg[g] for g in range(4)])
    vecs[...] = join([rv[g] for g in range(4)])
    for k in range(2):
        hidden[k] = join([rff[g, k] for g in range(4)])
    for kind in range(4):
        gy, _ = h.block(kind, h.p)
        xh = lax.rem(gy, 2)
        for g in range(4):
            other = jnp.logical_not((g == h.gx) & (xh == h.xh))

            @pl.when(h.holds(kind) & other)
            def _(kind=kind, g=g):
                push(
                    frames.at[0], rwa.at[kind, g], ss.at[16], rsw.at[kind, g], h.rel(0, 1)
                ).wait_recv()

        @pl.when(h.holds(kind))
        def _(kind=kind):
            units[kind] = join([rwa[kind, g] for g in range(4)])

    tail.wait_send()
    for c in copies:
        c.wait_send()
    for c, mine in sends:

        @pl.when(jnp.logical_not(mine))
        def _(c=c):
            c.wait_send()


def entry(tok, grd, wa, ff, vec):
    return pl.pallas_call(
        entry_kernel,
        out_shape=[
            jax.ShapeDtypeStruct((ROWS, D), BF),
            jax.ShapeDtypeStruct((ROWS, D), BF),
            jax.ShapeDtypeStruct((4, FRAME, D), BF),
            jax.ShapeDtypeStruct((2, FPAD, D), BF),
            jax.ShapeDtypeStruct((8, D), F32),
        ],
        in_specs=[VMEM] * 5,
        out_specs=[VMEM] * 5,
        scratch_shapes=[
            pltpu.VMEM((4, ROWS, QUARTER), BF),
            pltpu.VMEM((4, ROWS, QUARTER), BF),
            pltpu.VMEM((4, 4, FRAME, QUARTER), BF),
            pltpu.VMEM((4, 2, FPAD, QUARTER), BF),
            pltpu.VMEM((4, 8, QUARTER), F32),
            pltpu.VMEM((2, TAIL, QUARTER), BF),
            pltpu.VMEM((2, TAIL, QUARTER), BF),
            pltpu.VMEM((336, QUARTER), F32),
            pltpu.VMEM((4, FRAME, QUARTER), BF),
            pltpu.SemaphoreType.DMA((20,)),
            pltpu.SemaphoreType.DMA((16,)),
            pltpu.SemaphoreType.DMA((4, 4)),
        ],
        compiler_params=pltpu.CompilerParams(
            collective_id=0, has_side_effects=True, vmem_limit_bytes=60 * 2**20
        ),
        name="entry",
    )(tok, grd, wa, ff, vec)


def set_masks(masks, begin):
    for i in range(4):
        n = 256 * (i + 1)
        b = lax.broadcasted_iota(jnp.int32, (n, 256), 0)
        a = lax.broadcasted_iota(jnp.int32, (n, 256), 1) + 256 * i

        def doc(t):
            return (t >= begin).astype(jnp.int32) + (t >= begin + DOC).astype(jnp.int32)

        masks[i, :n] = jnp.where((b <= a) & (doc(a) == doc(b)), 0.0, NEG)


def probs_t(key, query, mask):
    s = nt(key, query) + mask
    e = jnp.exp(s - jnp.max(s, axis=0, keepdims=True))
    return e * (1.0 / jnp.sum(e, axis=0, keepdims=True))


def halves(v):
    return v[:, :HEAD_DIM], v[:, HEAD_DIM:]


def attend_kernel(
    begin, rows, units, hidden, vecs, qkvb, fcb,
    firsts, weights, ffw, fcbs, qkv, att, resid, second,
    masks, *rest,
):
    scat_refs, (ss, rs, rsw) = rest[:6], rest[6:]
    h = Here()
    ys = [h.rel(dy=d) for d in (1, 2, 3)]
    meet(h.ring() + ys)
    x = rows[...].astype(F32)
    normed, _ = stats(x)
    firsts[h.p] = (normed * vecs[0:1] + vecs[1:2]).astype(BF)
    gather = Gather(h, firsts, ss, rs, 0)
    gather.start()
    wsend = []
    for kind in range(4):
        held = h.holds(kind)
        for d in (1, 2, 3):
            c = push(
                units.at[kind], weights.at[kind], ss.at[16 + 3 * kind + d - 1], rsw.at[kind], ys[d - 1]
            )
            wsend.append((c, held))

            @pl.when(held)
            def _(c=c):
                c.start()

        @pl.when(held)
        def _(kind=kind):
            weights[kind] = units[kind]

    fsend = []
    for d in (1, 2, 3):
        i = 28 + 2 * (d - 1)
        fsend.append(push(hidden, ffw.at[h.y], ss.at[i], rs.at[i], ys[d - 1]))
        fsend.append(push(fcb, fcbs.at[h.y], ss.at[i + 1], rs.at[i + 1], ys[d - 1]))
    for c in fsend:
        c.start()
    ffw[h.y] = hidden[...]
    fcbs[h.y] = fcb[...]
    set_masks(masks, begin[0])

    def wait_unit(kind):
        @pl.when(jnp.logical_not(h.holds(kind)))
        def _():
            push(units.at[0], weights.at[kind], ss.at[16], rsw.at[kind], ys[0]).wait_recv()

    for kind in range(3):
        wait_unit(kind)
    for s in range(4):
        chip = gather.ready(s)
        block = firsts[pl.ds(2 * chip, 2)].reshape(256, D)
        for kind in range(3):
            term = nt(block, weights[kind]) + qkvb[kind : kind + 1]
            qkv[kind, pl.ds(pl.multiple_of(256 * chip, 256), 256)] = term.astype(BF)
    gather.finish()

    @pl.loop(0, 2)
    def _(pair):
        lanes = pl.ds(pl.multiple_of(128 * pair, 128), 128)
        for i in range(4):
            n = 256 * (i + 1)
            queries = halves(qkv[0, 256 * i : n, lanes])
            keys = halves(qkv[1, 0:n, lanes])
            values = halves(qkv[2, 0:n, lanes])
            outs = []
            for q, k, v in zip(queries, keys, values):
                probs = probs_t(k, q * 0.125, masks[i, :n])
                outs.append(tn(probs.astype(BF), v))
            att[256 * i : n, lanes] = join(outs).astype(BF)

    wait_unit(3)
    scatter = Scatter(h, scat_refs, ss, rs, 9)

    def term(chip):
        return nn(att[pl.ds(pl.multiple_of(256 * chip, 256), 256)], weights[3])

    scatter.run(term)
    res = rows[...].astype(F32) + scatter.result() + vecs[2:3]
    resid[...] = res
    normed, _ = stats(res)
    second[...] = (normed * vecs[3:4] + vecs[4:5]).astype(BF)
    for c, held in wsend:

        @pl.when(held)
        def _(c=c):
            c.wait_send()

    for c in fsend:
        c.wait()


def attend(begin, rows, units, hidden, vecs, qkvb, fcb):
    return pl.pallas_call(
        attend_kernel,
        out_shape=[
            jax.ShapeDtypeStruct((8, ROWS, D), BF),
            jax.ShapeDtypeStruct((4, FRAME, D), BF),
            jax.ShapeDtypeStruct((4, 2, FPAD, D), BF),
            jax.ShapeDtypeStruct((4, 8, FPAD), F32),
            jax.ShapeDtypeStruct((3, SEQ, FRAME), BF),
            jax.ShapeDtypeStruct((SEQ, FRAME), BF),
            jax.ShapeDtypeStruct((ROWS, D), F32),
            jax.ShapeDtypeStruct((ROWS, D), BF),
        ],
        in_specs=[SMEM] + [VMEM] * 6,
        out_specs=[VMEM] * 8,
        scratch_shapes=[
            pltpu.VMEM((4, SEQ, 256), F32),
            *Scatter.scratch(),
            pltpu.SemaphoreType.DMA((34,)),
            pltpu.SemaphoreType.DMA((34,)),
            pltpu.SemaphoreType.DMA((4,)),
        ],
        compiler_params=pltpu.CompilerParams(
            collective_id=1, has_side_effects=True, vmem_limit_bytes=62 * 2**20
        ),
        name="attend",
    )(begin, rows, units, hidden, vecs, qkvb, fcb)


def feed_kernel(
    second, resid, grad, ffw, fcbs, vecs,
    layer_out, grad_resid, branch, dff, gvec, fcg,
    seconds, grads, hid, gpre, outs, *rest,
):
    s1, s2, (ss, rs) = rest[:6], rest[6:12], rest[12:]
    h = Here()
    meet(h.ring())
    seconds[h.p] = second[...]
    grads[h.p] = grad[...]
    g1 = Gather(h, seconds, ss, rs, 0)
    g2 = Gather(h, grads, ss, rs, 9)
    g1.start()
    g2.start()
    fcg[...] = jnp.zeros_like(fcg)
    for s in range(4):
        chip = g1.ready(s)
        g2.ready(s)
        span = pl.ds(pl.multiple_of(256 * chip, 256), 256)

        @pl.loop(0, 4)
        def _(y, chip=chip, span=span):
            a = seconds[pl.ds(2 * chip, 2)].reshape(256, D)
            b = grads[pl.ds(2 * chip, 2)].reshape(256, D)
            v = nt(a, ffw[y, 0]) + fcbs[y, 0:1]
            up = nt(b, ffw[y, 1])
            t = jnp.tanh(0.7978845608028654 * (v + 0.044715 * v * v * v))
            hid[y, span] = (0.5 * v * (1.0 + t)).astype(BF)
            slope = 0.5 * (1.0 + t) + 0.5 * v * (1.0 - t * t) * (
                0.7978845608028654 * (1.0 + 3 * 0.044715 * v * v)
            )
            low = (up * slope).astype(BF)
            gpre[y, span] = low
            fcg[y, 0:1] += rows_of(low.astype(F32))

    g1.finish()
    g2.finish()

    def total(src, k):
        def term(chip):
            span = pl.ds(pl.multiple_of(256 * chip, 256), 256)
            return sum(nn(src[y, span], ffw[y, k]) for y in range(4))

        return term

    back = Scatter(h, s2, ss, rs, 18)
    back.run(total(gpre, 0))
    forth = Scatter(h, s1, ss, rs, 25)
    forth.run(total(hid, 1))

    gs = back.result()
    normed, inv = stats(resid[...])
    up = grad[...].astype(F32)
    gres = up + norm_back(gs, vecs[3:4], normed, inv)
    grad_resid[...] = gres
    low = gres.astype(BF)
    branch[...] = low
    gvec[...] = jnp.zeros_like(gvec)
    gvec[0:1] = rows_of(gs * normed)
    gvec[1:2] = rows_of(gs)
    gvec[2:3] = rows_of(low.astype(F32))
    gvec[3:4] = rows_of(up)

    @pl.loop(0, 4)
    def _(y):
        dff[y, 0] = tn(gpre[y], seconds[...].reshape(SEQ, D)).astype(BF)
        dff[y, 1] = tn(hid[y], grads[...].reshape(SEQ, D)).astype(BF)

    out = (resid[...] + forth.result() + vecs[5:6]).astype(BF)
    for g in range(4):
        outs[g] = out[:, QUARTER * g : QUARTER * (g + 1)]
    spread(h, outs, layer_out, ss, rs, 32)


def spread(h, src, dst, ss, rs, base):
    copies = [
        push(src.at[h.gx ^ d], dst.at[h.gx], ss.at[base + d - 1], rs.at[base + d - 1], h.gxd(d))
        for d in (1, 2, 3)
    ]
    for c in copies:
        c.start()
    dst[h.gx] = src[h.gx]
    for c in copies:
        c.wait()


def feed(second, resid, grad, ffw, fcbs, vecs):
    return pl.pallas_call(
        feed_kernel,
        out_shape=[
            jax.ShapeDtypeStruct((4, ROWS, QUARTER), BF),
            jax.ShapeDtypeStruct((ROWS, D), F32),
            jax.ShapeDtypeStruct((ROWS, D), BF),
            jax.ShapeDtypeStruct((4, 2, FPAD, D), BF),
            jax.ShapeDtypeStruct((8, D), F32),
            jax.ShapeDtypeStruct((4, 8, FPAD), F32),
        ],
        in_specs=[VMEM] * 6,
        out_specs=[VMEM] * 6,
        scratch_shapes=[
            pltpu.VMEM((8, ROWS, D), BF),
            pltpu.VMEM((8, ROWS, D), BF),
            pltpu.VMEM((4, SEQ, FPAD), BF),
            pltpu.VMEM((4, SEQ, FPAD), BF),
            pltpu.VMEM((4, ROWS, QUARTER), BF),
            *Scatter.scratch(),
            *Scatter.scratch(),
            pltpu.SemaphoreType.DMA((35,)),
            pltpu.SemaphoreType.DMA((35,)),
        ],
        compiler_params=pltpu.CompilerParams(
            collective_id=2, has_side_effects=True, vmem_limit_bytes=62 * 2**20
        ),
        name="feed",
    )(second, resid, grad, ffw, fcbs, vecs)


def back_kernel(
    begin, branch, grad_resid, rows, firsts, weights, qkv, att, vecs,
    input_grad, dwa, gvec, qvg,
    masks, branches, gatt, dqkv, dk, dv, outs, got, *rest,
):
    scat_refs, (ss, rs) = rest[:6], rest[6:]
    h = Here()
    meet(h.ring())
    branches[h.p] = branch[...]
    gather = Gather(h, branches, ss, rs, 0)
    gather.start()
    set_masks(masks, begin[0])
    for s in range(4):
        chip = gather.ready(s)
        block = branches[pl.ds(2 * chip, 2)].reshape(256, D)
        gatt[pl.ds(pl.multiple_of(256 * chip, 256), 256)] = nt(block, weights[3]).astype(BF)
    gather.finish()

    @pl.loop(0, 2)
    def _(pair):
        lanes = pl.ds(pl.multiple_of(128 * pair, 128), 128)
        dk[...] = jnp.zeros_like(dk)
        dv[...] = jnp.zeros_like(dv)
        for i in range(4):
            n = 256 * (i + 1)
            queries = halves(qkv[0, 256 * i : n, lanes])
            keys = halves(qkv[1, 0:n, lanes])
            values = halves(qkv[2, 0:n, lanes])
            ups = halves(gatt[256 * i : n, lanes])
            dqs = []
            for s, (q, k, v, g) in enumerate(zip(queries, keys, values, ups)):
                q = q * 0.125
                probs = probs_t(k, q, masks[i, :n])
                dv[s, :n] += nn(probs.astype(BF), g)
                prod = probs * nt(v, g)
                ds = (prod - probs * jnp.sum(prod, axis=0, keepdims=True)).astype(BF)
                dk[s, :n] += nn(ds, q)
                dqs.append(tn(ds, k) * 0.125)
            dqkv[0, 256 * i : n, lanes] = join(dqs).astype(BF)
        dqkv[1, :, lanes] = join([dk[0], dk[1]]).astype(BF)
        dqkv[2, :, lanes] = join([dv[0], dv[1]]).astype(BF)

    scatter = Scatter(h, scat_refs, ss, rs, 9)

    def term(chip):
        span = pl.ds(pl.multiple_of(256 * chip, 256), 256)
        return sum(nn(dqkv[k, span], weights[k]) for k in range(3))

    scatter.run(term)
    qvg[...] = jnp.zeros_like(qvg)
    qvg[0:1] = rows_of(dqkv[0].astype(F32))
    qvg[1:2] = rows_of(dqkv[2].astype(F32))

    @pl.loop(0, 3)
    def _(kind):
        dwa[kind] = tn(dqkv[kind], firsts[...].reshape(SEQ, D)).astype(BF)

    dwa[3] = tn(att[...], branches[...].reshape(SEQ, D)).astype(BF)

    gf = scatter.result()
    normed, inv = stats(rows[...].astype(F32))
    out = grad_resid[...] + norm_back(gf, vecs[0:1], normed, inv)
    gvec[...] = jnp.zeros_like(gvec)
    gvec[0:1] = rows_of(gf * normed)
    gvec[1:2] = rows_of(gf)
    low = out.astype(BF)
    for g in range(4):
        outs[g] = low[:, QUARTER * g : QUARTER * (g + 1)]
    spread(h, outs, got, ss, rs, 16)
    input_grad[...] = got[...].astype(F32)


def back(begin, branch, grad_resid, rows, firsts, weights, qkv, att, vecs):
    return pl.pallas_call(
        back_kernel,
        out_shape=[
            jax.ShapeDtypeStruct((4, ROWS, QUARTER), F32),
            jax.ShapeDtypeStruct((4, FRAME, D), BF),
            jax.ShapeDtypeStruct((8, D), F32),
            jax.ShapeDtypeStruct((8, FRAME), F32),
        ],
        in_specs=[SMEM] + [VMEM] * 8,
        out_specs=[VMEM] * 4,
        scratch_shapes=[
            pltpu.VMEM((4, SEQ, 256), F32),
            pltpu.VMEM((8, ROWS, D), BF),
            pltpu.VMEM((SEQ, FRAME), BF),
            pltpu.VMEM((3, SEQ, FRAME), BF),
            pltpu.VMEM((2, SEQ, HEAD_DIM), F32),
            pltpu.VMEM((2, SEQ, HEAD_DIM), F32),
            pltpu.VMEM((4, ROWS, QUARTER), BF),
            pltpu.VMEM((4, ROWS, QUARTER), BF),
            *Scatter.scratch(),
            pltpu.SemaphoreType.DMA((19,)),
            pltpu.SemaphoreType.DMA((19,)),
        ],
        compiler_params=pltpu.CompilerParams(
            collective_id=3, has_side_effects=True, vmem_limit_bytes=62 * 2**20
        ),
        name="back",
    )(begin, branch, grad_resid, rows, firsts, weights, qkv, att, vecs)


ZF = 112
ZW = 64


def sums_kernel(
    dff, dwa, ffo, wao,
    ry, ryw, sf, sw, rz, rzw, zf, zw, ffs, was, main, tails, scr,
    ss, rs, ssw, rsw, rsm, rst,
):
    h = Here()
    ys = [h.rel(dy=d) for d in (1, 2, 3)]
    zs = [h.rel(dz=d) for d in (1, 2, 3)]
    plane = [h.rel(dx, f, dy) for dy in range(4) for dx in range(4) for f in (0, 1) if dx or f or dy]
    meet(plane + zs)
    n_ff = []
    for d in (1, 2, 3):
        to = lax.rem(h.y + d, 4)
        c = push(dff.at[to], ry.at[d - 1], ss.at[d - 1], rs.at[d - 1], ys[d - 1])
        c.start()
        n_ff.append(c)
    out_w = []
    for kind in range(4):
        home = h.block(kind, h.p)[0] // 2
        for d in (1, 2, 3):
            c = push(dwa.at[kind], ryw.at[d - 1, kind], ssw.at[kind], rsw.at[d - 1, kind], ys[d - 1])
            cond = lax.rem(h.y + d, 4) == home

            @pl.when(cond)
            def _(c=c):
                c.start()

            out_w.append((c, cond))
    for c in n_ff:
        c.wait_recv()
    for k in range(2):
        s = dff[h.y, k].astype(F32)
        for d in range(3):
            s = s + ry[d, k].astype(F32)
        sf[k] = s.astype(BF)
    zsend = []
    for d in (1, 2, 3):
        q = lax.rem(h.z + d, 4)
        src = sf.at[q // 2, pl.ds(pl.multiple_of(96 * lax.rem(q, 2), 16), ZF)]
        c = push(src, rz.at[d - 1], ss.at[2 + d], rs.at[2 + d], zs[d - 1])
        c.start()
        zsend.append(c)
    for kind in range(4):
        for d in (1, 2, 3):

            @pl.when(h.holds(kind))
            def _(kind=kind, d=d):
                push(
                    dwa.at[0], ryw.at[d - 1, kind], ssw.at[0], rsw.at[d - 1, kind], ys[0]
                ).wait_recv()

        @pl.when(h.holds(kind))
        def _(kind=kind):
            s = dwa[kind].astype(F32)
            for d in range(3):
                s = s + ryw[d, kind].astype(F32)
            sw[kind] = s.astype(BF)
            for d in (1, 2, 3):
                q = lax.rem(h.z + d, 4)
                src = sw.at[kind, pl.ds(pl.multiple_of(ZW * q, ZW), ZW)]
                push(
                    src, rzw.at[d - 1, kind], ssw.at[4 + 3 * kind + d - 1],
                    rsw.at[2 + d, kind], zs[d - 1],
                ).start()

    for c in zsend:
        c.wait_recv()
    s = sf[h.z // 2, pl.ds(pl.multiple_of(96 * lax.rem(h.z, 2), 16), ZF)].astype(F32)
    for d in range(3):
        s = s + rz[d].astype(F32)
    zf[h.z] = s.astype(BF)
    zback = []
    for d in (1, 2, 3):
        c = push(zf.at[h.z], zf.at[h.z], ss.at[5 + d], rs.at[5 + d], zs[d - 1])
        c.start()
        zback.append(c)
    for kind in range(4):

        @pl.when(h.holds(kind))
        def _(kind=kind):
            s = sw[kind, pl.ds(pl.multiple_of(ZW * h.z, ZW), ZW)].astype(F32)
            for d in (1, 2, 3):
                push(
                    dwa.at[0, pl.ds(0, ZW)], rzw.at[d - 1, kind], ssw.at[4],
                    rsw.at[2 + d, kind], zs[0],
                ).wait_recv()
                s = s + rzw[d - 1, kind].astype(F32)
            zw[kind, h.z] = s.astype(BF)
            for d in (1, 2, 3):
                push(
                    zw.at[kind, h.z], zw.at[kind, h.z], ssw.at[16 + 3 * kind + d - 1],
                    rsw.at[5 + d, kind], zs[d - 1],
                ).start()

    for c in zback:
        c.wait_recv()
    for k in range(2):
        full = jnp.concatenate([zf[2 * k], zf[2 * k + 1][16:]], axis=0)
        for g in range(4):
            ffs[g, k] = full[:, QUARTER * g : QUARTER * (g + 1)]
    spread_start = [
        push(ffs.at[h.gx ^ d], ffo.at[h.gx], ss.at[8 + d], rs.at[8 + d], h.gxd(d)) for d in (1, 2, 3)
    ]
    for c in spread_start:
        c.start()
    ffo[h.gx] = ffs[h.gx]

    for kind in range(4):
        gy, place = h.block(kind, h.p)
        gyt, placet = h.block(kind, h.p - 1)
        xh, xht, yt = lax.rem(gy, 2), lax.rem(gyt, 2), gyt // 2

        @pl.when(h.holds(kind))
        def _(kind=kind, gy=gy, place=place, gyt=gyt, placet=placet, xh=xh, xht=xht, yt=yt):
            for d in (1, 2, 3):
                push(
                    zw.at[0, 0], zw.at[kind, 0], ssw.at[4], rsw.at[5 + d, kind], zs[0]
                ).wait_recv()
            full = zw[kind].reshape(FRAME, D)
            for g in range(4):
                was[kind, g] = full[:, QUARTER * g : QUARTER * (g + 1)]
            for g in range(4):
                same = (g == h.gx) & (xh == h.xh)
                c = push(
                    was.at[kind, g], main.at[place], ssw.at[28 + 4 * kind + g], rsm.at[place],
                    (h.z, g, gy),
                )

                @pl.when(same)
                def _():
                    main[place] = was[kind, g]

                @pl.when(jnp.logical_not(same))
                def _():
                    c.start()

                @pl.when(h.p > 0)
                def _():
                    samet = (g == h.gx) & (xht == h.xh) & (yt == h.y)
                    t = push(
                        was.at[kind, g, pl.ds(0, TAIL)], tails.at[placet],
                        ssw.at[44 + 4 * kind + g], rst.at[placet], (h.z, g, gyt),
                    )

                    @pl.when(samet)
                    def _():
                        tails[placet] = was[kind, g, 0:TAIL]

                    @pl.when(jnp.logical_not(samet))
                    def _():
                        t.start()

    row = lax.broadcasted_iota(jnp.int32, (SUB, QUARTER), 0)
    for i in range(4):
        p, _ = h.unit(i)

        @pl.when(p != h.p)
        def _(i=i):
            push(main.at[0], main.at[i], ssw.at[28], rsm.at[i], ys[0]).wait_recv()

        nxt = p + 1
        kindv = h.unit(i)[1]
        if i == 3:
            ynext = nxt // 2
        else:
            ynext = (kindv * 8 + nxt) // 6

        @pl.when((p < 7) & jnp.logical_not((nxt == h.p) & (ynext == h.y)))
        def _(i=i):
            push(tails.at[0], tails.at[i], ssw.at[44], rst.at[i], ys[0]).wait_recv()

        scr[0:FRAME] = main[i].astype(F32)

        @pl.when(p < 7)
        def _(i=i):
            scr[192 : 192 + TAIL] = tails[i].astype(F32)

        wao[i] = scr[pl.ds(pl.multiple_of(8 * p, 8), SUB)]

    for c in n_ff + zsend + zback:
        c.wait_send()
    for c in spread_start:
        c.wait()
    for c, cond in out_w:

        @pl.when(cond)
        def _(c=c):
            c.wait_send()

    for kind in range(4):
        gy, place = h.block(kind, h.p)
        gyt, placet = h.block(kind, h.p - 1)
        xh, xht, yt = lax.rem(gy, 2), lax.rem(gyt, 2), gyt // 2

        @pl.when(h.holds(kind))
        def _(kind=kind, xh=xh, xht=xht, yt=yt):
            for d in (1, 2, 3):
                push(
                    sw.at[kind, pl.ds(0, ZW)], rzw.at[0, kind], ssw.at[4 + 3 * kind + d - 1],
                    rsw.at[3, kind], zs[0],
                ).wait_send()
                push(
                    zw.at[kind, 0], zw.at[kind, 0], ssw.at[16 + 3 * kind + d - 1], rsw.at[6, kind], zs[0]
                ).wait_send()
            for g in range(4):

                @pl.when(jnp.logical_not((g == h.gx) & (xh == h.xh)))
                def _():
                    push(
                        was.at[kind, g], main.at[0], ssw.at[28 + 4 * kind + g], rsm.at[0], ys[0]
                    ).wait_send()

                @pl.when((h.p > 0) & jnp.logical_not((g == h.gx) & (xht == h.xh) & (yt == h.y)))
                def _():
                    push(
                        was.at[kind, g, pl.ds(0, TAIL)], tails.at[0], ssw.at[44 + 4 * kind + g],
                        rst.at[0], ys[0],
                    ).wait_send()


def sums(dff, dwa):
    return pl.pallas_call(
        sums_kernel,
        out_shape=[
            jax.ShapeDtypeStruct((4, 2, FPAD, QUARTER), BF),
            jax.ShapeDtypeStruct((4, SUB, QUARTER), F32),
        ],
        in_specs=[VMEM] * 2,
        out_specs=[VMEM] * 2,
        scratch_shapes=[
            pltpu.VMEM((3, 2, FPAD, D), BF),
            pltpu.VMEM((3, 4, FRAME, D), BF),
            pltpu.VMEM((2, FPAD, D), BF),
            pltpu.VMEM((4, FRAME, D), BF),
            pltpu.VMEM((3, ZF, D), BF),
            pltpu.VMEM((3, 4, ZW, D), BF),
            pltpu.VMEM((4, ZF, D), BF),
            pltpu.VMEM((4, 4, ZW, D), BF),
            pltpu.VMEM((4, 2, FPAD, QUARTER), BF),
            pltpu.VMEM((4, 4, FRAME, QUARTER), BF),
            pltpu.VMEM((4, FRAME, QUARTER), BF),
            pltpu.VMEM((4, TAIL, QUARTER), BF),
            pltpu.VMEM((FRAME, QUARTER), F32),
            pltpu.SemaphoreType.DMA((12,)),
            pltpu.SemaphoreType.DMA((12,)),
            pltpu.SemaphoreType.DMA((60,)),
            pltpu.SemaphoreType.DMA((9, 4)),
            pltpu.SemaphoreType.DMA((4,)),
            pltpu.SemaphoreType.DMA((4,)),
        ],
        compiler_params=pltpu.CompilerParams(
            collective_id=4, has_side_effects=True, vmem_limit_bytes=62 * 2**20
        ),
        name="sums",
    )(dff, dwa)


def per_device(
    tokens_in, segments, norm1_gain, norm1_bias, qkv_weight, query_bias, value_bias, proj_weight,
    proj_bias, norm2_gain, norm2_bias, fc_weight, fc_bias, out_weight, out_bias, out_grad,
):
    gx, gy = lax.axis_index("gx"), lax.axis_index("gy")
    y, xh = gy // 2, lax.rem(gy, 2)
    p = xh * 4 + gx
    zeros = jnp.sum((segments == 0).astype(jnp.int32))
    begins = lax.psum(
        jnp.where((jnp.arange(4) == gx) & (gy == 0), zeros, 0).astype(jnp.int32), ("gx", "gy")
    )
    begin = lax.dynamic_slice_in_dim(begins, y, 1)

    wa = jnp.concatenate([qkv_weight.T.reshape(3, SUB, QUARTER), proj_weight.T[None]])
    ff = jnp.stack(
        [fc_weight.T.reshape(4, SUB, QUARTER), out_weight.T.reshape(4, SUB, QUARTER)], axis=1
    )
    ff = jnp.pad(ff, ((0, 0), (0, 0), (0, FPAD - SUB), (0, 0)))
    zero = jnp.zeros_like(norm1_gain)
    vec = jnp.stack(
        [norm1_gain, norm1_bias, proj_bias, norm2_gain, norm2_bias, out_bias, zero, zero]
    )
    rows, grads, units, hidden, vecs = entry(
        tokens_in.reshape(4, ROWS, QUARTER), out_grad.reshape(4, ROWS, QUARTER), wa, ff, vec
    )

    valid = (jnp.arange(FRAME) < 192) | (p == 7)
    qb = jnp.where(valid, lax.dynamic_slice_in_dim(query_bias, 192 * p, FRAME), 0.0)
    vb = jnp.where(valid, lax.dynamic_slice_in_dim(value_bias, 192 * p, FRAME), 0.0)
    nil = jnp.zeros_like(qb)
    qkvb = jnp.stack([qb, nil, vb, nil, nil, nil, nil, nil])
    fcb = jnp.pad(lax.dynamic_slice_in_dim(fc_bias, SUB * gx, SUB), (0, FPAD - SUB))
    fcb = jnp.broadcast_to(fcb, (8, FPAD))

    firsts, weights, ffw, fcbs, qkv, att, resid, second = attend(
        begin, rows, units, hidden, vecs, qkvb, fcb
    )
    layer_out, grad_resid, branch, dff, gvec2, fcg = feed(second, resid, grads, ffw, fcbs, vecs)
    input_grad, dwa, gvec1, qvg = back(
        begin, branch, grad_resid, rows, firsts, weights, qkv, att, vecs
    )
    ffo, wao = sums(dff, dwa)

    qv = jnp.zeros((2, D), F32)
    qv = lax.dynamic_update_slice(qv, qvg[0:2], (0, 192 * p))
    fcp = jnp.zeros((4, 2, 4, SUB), F32)
    fcp = lax.dynamic_update_slice(fcp, fcg[:, 0, :SUB][:, None, None], (0, xh, gx, 0))
    both = jnp.concatenate([gvec1[0:2], gvec2[0:4]])
    both, qv, fcp = lax.psum((both, qv, fcp), ("dp", "gx", "gy"))
    mine = lax.dynamic_slice_in_dim(both, QUARTER * gx, QUARTER, 1)
    fcp = lax.dynamic_slice(fcp, (y, xh, 0, 0), (1, 1, 4, SUB)).reshape(4 * SUB)

    def whole(v):
        return v[:, :SUB].reshape(4 * SUB, QUARTER).T.astype(F32)

    return (
        layer_out.reshape(4 * ROWS, QUARTER),
        input_grad.reshape(4 * ROWS, QUARTER),
        mine[0],
        mine[1],
        wao[0:3].reshape(3 * SUB, QUARTER).T,
        qv[0],
        qv[1],
        wao[3].T,
        mine[4],
        mine[2],
        mine[3],
        whole(ffo[:, 0]),
        fcp,
        whole(ffo[:, 1]),
        mine[5],
    )


def solution(mesh):
    return jax.shard_map(
        per_device,
        mesh=mesh,
        in_specs=(
            P(("dp", "gy"), "gx"), P(("dp", "gx"), "gy"), P("gx"), P("gx"), P("gx", "gy"), P(), P(),
            P("gx", "gy"), P("gx"), P("gx"), P("gx"), P("gx", "gy"), P("gy"), P("gx", "gy"), P("gx"),
            P(("dp", "gy"), "gx"),
        ),
        out_specs=(
            P(("dp", "gy"), "gx"), P(("dp", "gy"), "gx"), P("gx"), P("gx"), P("gx", "gy"), P(), P(),
            P("gx", "gy"), P("gx"), P("gx"), P("gx"), P("gx", "gy"), P("gy"), P("gx", "gy"), P("gx"),
        ),
        check_vma=False,
    )
```

time: 2020 us -> 683 us (0.34)
  waiting for transfers between devices: 1510 us -> 8.3 us
  Pallas kernels: 0 us -> 601 us
  matrix products: 178 us -> 0 us
  blocking collectives: 128 us -> 13.2 us
  other arithmetic: 97.8 us -> 6.41 us
  local copies, waits for them, and re-layouts: 74 us -> 28.6 us
    reduce_scatter x8 -> x0, waiting for transfers between devices: 722 us -> none  [the longest x4 363 us: sum_gy(): lax.psum_scatter(term(jnp.int32(0), lax.axis_size('gy') * (left.shape[0]...]
    pallas_call x0 -> x5, Pallas kernels: none -> 601 us  [the longest x1 225 us: sums(): pl.pallas_call(sums_kernel, out_shape=[jax.ShapeDtypeStruct((4, 2, FPAD,...]
    all_gather x12 -> x0, waiting for transfers between devices: 577 us -> none  [the longest x4 238 us: gather_gy(): return lax.all_gather(values, 'gy', axis=0, tiled=True)]
    psum x2 -> x1, waiting for transfers between devices: 198 us -> 8.29 us  [per_device(): both, qv, fcp = lax.psum((both, qv, fcp), ('dp', 'gx', 'gy'))]
    dot_general x30 -> x0, matrix products: 178 us -> none  [the longest x8 42 us: masked_scores(): jnp.einsum('sahe,sbhe->shab', queries, keys, preferred_element_type=jnp.f...]
    all_to_all x3 -> x0, blocking collectives: 55.9 us -> none  [the longest x2 33.4 us: to_rows(): lax.all_to_all(values, 'gy', split_axis=2, concat_axis=1, tiled=True)]
    unnamed x12 -> x0, other arithmetic: 51.6 us -> none
    all_gather x2 -> x0, blocking collectives: 44.8 us -> none  [the longest x1 30.2 us: per_device(): all_stats = lax.all_gather(stats_rows, 'gy', axis=1, tiled=True)]
  transfers between devices with their start and end apart: 23 -> 1, of which waited for: 22 -> 1; matrix products, arithmetic and copies ran while one was open for 7% -> 2% of each run, Pallas kernels for 0% -> 34%
where the time goes in v1:
time: 683 us; the launch traced here: 672 us
  Pallas kernels  601 us (88%)
  local copies, waits for them, and re-layouts  28.6 us (4%)
  between operations  14.8 us (2%)
  blocking collectives  13.2 us (2%)
  waiting for transfers between devices  8.3 us (1%)
    pallas_call x1, Pallas kernels, sums(): pl.pallas_call(sums_kernel, out_shape=[jax.ShapeDtypeStruct((4, 2, FPAD,...  225 us
    pallas_call x1, Pallas kernels, attend(): pl.pallas_call(attend_kernel, out_shape=[jax.ShapeDtypeStruct((8, ROWS, D...  138 us
    pallas_call x1, Pallas kernels, feed(): pl.pallas_call(feed_kernel, out_shape=[jax.ShapeDtypeStruct((4, ROWS, QUA...  113 us
    pallas_call x1, Pallas kernels, back(): pl.pallas_call(back_kernel, out_shape=[jax.ShapeDtypeStruct((4, ROWS, QUA...  74.9 us
    pallas_call x1, Pallas kernels, entry(): pl.pallas_call(entry_kernel, out_shape=[jax.ShapeDtypeStruct((ROWS, D), B...  49.6 us
  transfers between devices with their start and end apart: 1, of which 1 were waited for; matrix products, arithmetic and copies ran while one was open for 2% of the time, Pallas kernels for 34%

profile of v1, /device:TPU:27, one launch (start us, length us, event | category | flops | bytes accessed | tf_op | source)
XLA Modules:
  0.0 672.3 jit_solution(4564389764084740231)
XLA Ops:
  7.3 1.4 fusion.3
  8.7 0.6 and_select_fusion
  9.3 13.2 %psum.28 = s32[4]{0:T(128)S(1)} all-reduce(s32[4]{0:T(128)S(1)} %and_select_fusion), channel_id=1, replica_groups=mesh['dp'=4,'gx'=4,'gy'=8] {'gx','gy'}, use_global_device_ids=true, to_apply=%region_1.2 | all-reduce | flops 4 | bytes 32 | tf_op jit(solution)/shard_map/psum | solution.py:981
  22.5 1.4 copy.35
  23.9 0.3 copy.36
  24.2 0.2 copy.33
  24.5 0.3 copy-done.8
  24.8 0.1 copy.34
  25.0 0.1 copy-done.7
  25.0 1.0 copy.31
  26.0 2.0 copy.32
  28.0 0.6 dynamic_slice.18.begin
  28.6 0.8 dynamic_slice.21
  29.4 1.4 fusion.2.ff
  30.8 1.0 pad_maximum_fusion.wa
  31.8 0.8 dynamic-slice_select_fusion
  32.6 0.6 stack.51.qkvb
  33.3 0.6 stack.47.vec
  33.9 49.6 %entry.1 = (bf16[128,1600]{1,0:T(8,128)(2,1)}, bf16[128,1600]{1,0:T(8,128)(2,1)}, bf16[4,256,1600]{2,1,0:T(8,128)(2,1)}, bf16[2,208,1600]{2,1,0:T(8,128)(2,1)}, f32[8,1600]{1,0:T(8,128)}) custom-call(bf16[4,128,400]{2,1,0:T(8,128)(2,1)} %bitcast.51, bf16[4,128,400]{2,1,0:T(8,128)(2,1)} %bitcast.52, bf16[4,200,400]{2,1,0:T(8,128)(2,1)} %pad_maximum_fusion.wa, ...), custom_call_target="tpu_custom_call" | custom-call | tf_op jit(solution)/shard_map/entry/pallas_call | solution.py:317
  83.5 0.6 broadcast_in_dim.29.fcb
  84.1 138.1 %attend.1 = (bf16[8,128,1600]{2,1,0:T(8,128)(2,1)}, bf16[4,256,1600]{2,1,0:T(8,128)(2,1)}, bf16[4,2,208,1600]{3,2,1,0:T(8,128)(2,1)}, f32[4,8,208]{2,1,0:T(8,128...) custom-call(s32[1]{0:T(128)} %dynamic_slice.18.begin, ...), custom_call_target="tpu_custom_call" | custom-call | tf_op jit(solution)/shard_map/attend/pallas_call | solution.py:464
  222.3 112.9 %feed.1 = (bf16[4,128,400]{2,1,0:T(8,128)(2,1)}, f32[128,1600]{1,0:T(8,128)}, bf16[128,1600]{1,0:T(8,128)(2,1)}, bf16[4,2,208,1600]{3,2,1,0:T(8,128)(2,1)}, f32[8,1600]{1,0:T(8,128)}, /*index=5*/f32[4,8,208]{2,1,0:T(8,128)}) custom-call(bf16[128,1600]{1,0:T(8,128)(2,1)} %get-tuple-element.44.second, f32[128,1600]{1,0:T(8,128)} %get-tuple-element.45.resid, ...), custom_call_target="tpu_custom_call" | custom-call | tf_op jit(solution)/shard_map/feed/pallas_call | solution.py:579
  335.2 74.9 %back.1 = (f32[4,128,400]{2,1,0:T(8,128)}, bf16[4,256,1600]{2,1,0:T(8,128)(2,1)}, f32[8,1600]{1,0:T(8,128)}, f32[8,256]{1,0:T(8,128)}) custom-call(s32[1]{0:T(128)} %dynamic_slice.18.begin, bf16[128,1600]{1,0:T(8,128)(2,1)} %get-tuple-element.50.branch, f32[128,1600]{1,0:T(8,128)} %get-tuple-element.51.grad_resid, bf16[128,1600]{1,0:T(8,128)(2,1)} %get-tuple-element.40.rows, ...), custom_call_target="tpu_custom_call" | custom-call | tf_op jit(solution)/shard_map/back/pallas_call | solution.py:682
  410.1 0.8 slice.54
  410.9 0.7 slice.59
  411.6 0.8 slice_bitcast_fusion.3
  412.4 0.6 pad_maximum_fusion.1
  413.0 0.2 dynamic_update_slice.6
  413.3 0.5 copy-done.10
  413.8 0.1 copy-done.9
  414.0 225.5 %sums.1 = (bf16[4,2,208,400]{3,2,1,0:T(8,128)(2,1)}, f32[4,200,400]{2,1,0:T(8,128)}) custom-call(bf16[4,2,208,1600]{3,2,1,0:T(8,128)(2,1)} %get-tuple-element.59.dff, bf16[4,256,1600]{2,1,0:T(8,128)(2,1)} %get-tuple-element.60.dwa), custom_call_target="tpu_custom_call" | custom-call | tf_op jit(solution)/shard_map/sums/pallas_call | solution.py:937
  639.4 1.5 slice_bitcast_fusion
  641.0 0.3 bitcast_convert_fusion.1
  641.4 0.3 bitcast_convert_fusion
  641.7 1.1 copy-done.1
  642.8 0.8 slice_bitcast_fusion.2
  643.5 1.1 slice.58
  644.7 1.6 copy.38
  646.3 1.6 copy.39
  647.9 1.3 copy.37
  649.2 0.9 copy.42
  650.2 1.2 copy.41
  651.4 0.9 copy.40
  652.3 8.3 %all-reduce.5.cloned.1.call-done = (f32[6,1600]{1,0:T(8,128)}, f32[2,1600]{1,0:T(2,128)}, f32[4,2,4,200]{3,1,2,0:T(2,128)}) async-done(((f32[6,1600]{1,0:T(8,128)}, f32[2,1600]{1,0:T(2,128)}, f32[4,2,4,200]{3,1,2,0:T(2,128)}), (f32[6,1600]{1,0:T(8,128)}, f32[2,1600]{1,0:T(2,128)}, f32[4,2,4,200]{3,1,2,0:T(2,128)})) %all-reduce.5.cloned.1.call-update) | async-done | bytes 76816 | tf_op jit(solution)/shard_map/psum | solution.py:1021
  660.6 0.7 dynamic-slice_reduce_fusion
  661.3 0.7 reshape.63
  662.0 1.4 slice_reduce_fusion
  663.4 1.6 fusion.4
  (43 shorter events, 0.3 us)
Async XLA Ops:
  7.2 16.7 %copy-start.4 = (bf16[400,800]{1,0:T(8,128)(2,1)S(1)}, bf16[400,800]{1,0:T(8,128)(2,1)}, u32[]{:S(2)}) copy-start(bf16[400,800]{1,0:T(8,128)(2,1)} %param.29) | copy-start | bytes 1920004
  7.2 17.0 %copy-start.6 = (bf16[400,600]{1,0:T(8,128)(2,1)S(1)}, bf16[400,600]{1,0:T(8,128)(2,1)}, u32[]{:S(2)}) copy-start(bf16[400,600]{1,0:T(8,128)(2,1)} %param.20) | copy-start | bytes 1440004
  7.2 653.4 %all-reduce.5.cloned.1.call-start = ((), (), s32[]{:S(2)}) async-start(), calls=%async_computation | async-start | bytes 198656 | tf_op jit(solution)/shard_map/psum | solution.py:1021
  23.9 0.9 copy-start.8
  23.9 1.1 copy-start.7
  29.4 3.9 copy-start.12
  29.4 3.9 copy-start.13
  29.4 3.9 copy-start.14
  29.4 3.9 copy-start.15
  29.4 3.9 copy-start.16
  29.4 3.9 copy-start.17
  335.2 75.8 %copy-start.11 = (f32[8,1600]{1,0:T(8,128)S(1)}, f32[8,1600]{1,0:T(8,128)}, u32[]{:S(2)}) copy-start(f32[8,1600]{1,0:T(8,128)} %get-tuple-element.58) | copy-start | bytes 153604
  413.2 0.6 copy-start.10
  413.3 0.6 copy-start.9
  641.3 1.4 copy-start.1
  646.3 1.6 copy-start
  647.9 1.3 copy-start.2
  647.9 2.3 copy-start.3
  649.2 2.1 copy-start.5
Sparse Core Ops, SparseCore 0:
  414.1 246.4 all-reduce.4

commit v2 on v0

v2 whole, which is shorter than its diff:
```python
import math

import jax
import jax.numpy as jnp
from jax import lax
from jax.experimental import pallas as pl
from jax.experimental.pallas import tpu as pltpu
from jax.sharding import PartitionSpec as P

BF = jnp.bfloat16
F32 = jnp.float32
HEADS = 25
HEAD_DIM = 64
D = HEADS * HEAD_DIM
FF = 6400
SEQ = 1024
DOC = 800
ROWS = 128
QUARTER = 400
SUB = 200
FPAD = 208
FRAME = 256
TAIL = 64
NEG = -1e30
MESH = pl.DeviceIdType.MESH
VMEM = pl.BlockSpec(memory_space=pltpu.VMEM)
SMEM = pl.BlockSpec(memory_space=pltpu.SMEM)


def nt(a, b):
    return lax.dot_general(a, b, (((1,), (1,)), ((), ())), preferred_element_type=F32)


def nn(a, b):
    return lax.dot_general(a, b, (((1,), (0,)), ((), ())), preferred_element_type=F32)


def tn(a, b):
    return lax.dot_general(a, b, (((0,), (0,)), ((), ())), preferred_element_type=F32)


class Here:
    def __init__(self):
        self.z, self.gx, self.gy = (lax.axis_index(a) for a in ("dp", "gx", "gy"))
        self.y, self.xh = self.gy // 2, lax.rem(self.gy, 2)
        self.x = self.xh * 2 + self.gx // 2
        self.c = lax.rem(self.gx, 2)
        self.p = self.x * 2 + self.c

    def at(self, x, c, y, z):
        return (z, lax.rem(x, 2) * 2 + c, y * 2 + x // 2)

    def rel(self, dx=0, flip=0, dy=0, dz=0):
        c = 1 - self.c if flip else self.c
        return self.at(
            lax.rem(self.x + 4 + dx, 4), c, lax.rem(self.y + 4 + dy, 4), lax.rem(self.z + 4 + dz, 4)
        )

    def ring(self):
        return [self.rel(dx, f) for dx in range(4) for f in (0, 1) if dx or f]

    def gxd(self, d):
        return (self.z, self.gx ^ d, self.gy)

    def unit(self, i):
        if i == 3:
            return self.gy, 3
        t = 3 * self.gy + i
        return lax.rem(t, 8), t // 8

    def block(self, kind, p):
        if kind == 3:
            return p, 3
        t = kind * 8 + p
        return t // 3, lax.rem(t, 3)

    def holds(self, kind):
        return self.block(kind, self.p)[0] // 2 == self.y


def meet(peers):
    sem = pltpu.get_barrier_semaphore()
    for d in peers:
        pl.semaphore_signal(sem, inc=1, device_id=d, device_id_type=MESH)
    pl.semaphore_wait(sem, len(peers))


def push(src, dst, ss, rs, d):
    return pltpu.make_async_remote_copy(
        src_ref=src, dst_ref=dst, send_sem=ss, recv_sem=rs, device_id=d, device_id_type=MESH
    )


def stats(v):
    mean = jnp.sum(v, axis=1, keepdims=True) / D
    spread = jnp.sum(v * v, axis=1, keepdims=True) / D - mean * mean
    inv = lax.rsqrt(spread + 1e-5)
    return (v - mean) * inv, inv


def norm_back(u, gain, normed, inv):
    w = u * gain
    a = jnp.sum(w, axis=1, keepdims=True) / D
    b = jnp.sum(w * normed, axis=1, keepdims=True) / D
    return inv * (w - a - normed * b)


def cut(start, size):
    return pl.ds(start if isinstance(start, int) else pl.multiple_of(start, 16), size)


def rows_of(v):
    return jnp.sum(v, axis=0, keepdims=True)


class Copy:
    def __init__(self, desc, send_if=None, recv_if=None):
        self.desc, self.send_if, self.recv_if = desc, send_if, recv_if
        self.is_got = self.is_gone = False

    def on(self, cond, do):
        if cond is None:
            do()
        else:
            pl.when(cond)(do)

    def start(self):
        self.on(self.send_if, self.desc.start)

    def got(self):
        if not self.is_got:
            self.is_got = True
            self.on(self.recv_if, self.desc.wait_recv)

    def gone(self):
        if not self.is_gone:
            self.is_gone = True
            self.on(self.send_if, self.desc.wait_send)


class Net:
    SIZE = 360

    def __init__(self, ss, rs):
        self.ss, self.rs, self.n, self.copies = ss, rs, 0, []

    def make(self, src, dst, d, send_if=None, recv_if=None, rs=None):
        i = self.n
        self.n += 1
        assert i < self.SIZE
        c = Copy(push(src, dst, self.ss.at[i], self.rs.at[i] if rs is None else rs, d), send_if, recv_if)
        if rs is not None:
            c.is_got = True
        self.copies.append(c)
        return c

    def send(self, *args, **kw):
        c = self.make(*args, **kw)
        c.start()
        return c

    def finish(self):
        for c in self.copies:
            c.got()
            c.gone()


class Gather:
    def __init__(self, here, net, buf):
        self.h, self.net, self.buf = here, net, buf

    def row(self, dx):
        return (lax.rem(self.h.x + 4 + dx, 4) * 2 + self.h.c) * ROWS

    def go(self, dx, d, half=None):
        ref = self.buf.at[cut(self.row(dx), ROWS) if half is None else cut(self.row(dx) + 64 * half, 64)]
        return self.net.send(ref, ref, d)

    def start(self):
        h = self.h
        self.right, self.left, self.sib = h.rel(1), h.rel(-1), h.rel(0, 1)
        self.r = [self.go(0, self.right, 0), None]
        self.l = [None, self.go(0, self.left, 1)]
        self.r[1] = self.go(0, self.right, 1)
        self.l[0] = self.go(0, self.left, 0)
        self.own = self.go(0, self.sib)

    def ready(self, s):
        h = self.h
        if s == 0:
            self.own.got()
            return h.x
        if s == 1:
            self.r[0].got()
            self.rr = self.go(-1, self.right, 0)
            self.l[1].got()
            self.ll = self.go(1, self.left, 1)
            self.r[1].got()
            self.f1 = self.go(-1, self.sib)
            self.l[0].got()
            self.f2 = self.go(1, self.sib)
            self.f1.got()
            return lax.rem(h.x + 3, 4)
        if s == 2:
            self.f2.got()
            return lax.rem(h.x + 1, 4)
        self.rr.got()
        f3 = self.go(2, self.sib, 0)
        self.ll.got()
        f4 = self.go(2, self.sib, 1)
        f3.got()
        f4.got()
        for c in (*self.r, *self.l, self.own, self.rr, self.ll, self.f1, self.f2, f3, f4):
            c.gone()
        return lax.rem(h.x + 2, 4)


class Scatter:
    @staticmethod
    def scratch():
        return [
            pltpu.VMEM((4, 2, ROWS, D), BF),
            pltpu.VMEM((4, ROWS, D), BF),
            pltpu.VMEM((2, ROWS, D), BF),
            pltpu.VMEM((ROWS, D), BF),
        ]

    STEPS = (2, 1, -1, 0)

    def __init__(self, here, net, refs):
        self.h, self.net = here, net
        self.part, self.mate, self.far, self.relay = refs
        self.pair, self.out = {}, []

    def term(self, j, f):
        h = self.h
        chip = lax.rem(h.x + 4 + self.STEPS[j], 4)
        self.part[j] = f(chip).astype(BF).reshape(2, ROWS, D)
        self.pair[j] = self.net.send(self.part.at[j, 1 - h.c], self.mate.at[j], h.rel(0, 1))

    def total(self, j):
        self.pair[j].got()
        return self.part[j, self.h.c].astype(F32) + self.mate[j].astype(F32)

    def link(self, j, half, dst, dx):
        src = self.part.at[j, self.h.c, pl.ds(64 * half, 64)]
        c = self.net.send(src, dst, self.h.rel(dx))
        self.out.append(c)
        return c

    def first(self):
        self.part[0, self.h.c] = self.total(0).astype(BF)
        self.in_r = self.link(0, 0, self.relay.at[pl.ds(0, 64)], 1)
        self.in_l = self.link(0, 1, self.relay.at[pl.ds(64, 64)], -1)

    def side(self, j):
        half = 1 if j == 1 else 0
        self.part[j, self.h.c] = self.total(j).astype(BF)
        c = self.link(j, half, self.far.at[j - 1, pl.ds(64 * half, 64)], self.STEPS[j])
        self.ends = getattr(self, "ends", []) + [c]

    def relayed(self):
        for j, half, c in ((1, 0, self.in_r), (2, 1, self.in_l)):
            c.got()
            span = pl.ds(64 * half, 64)
            s = self.part[j, self.h.c, span].astype(F32) + self.relay[span].astype(F32)
            self.part[j, self.h.c, span] = s.astype(BF)
            self.ends.append(self.link(j, half, self.far.at[j - 1, span], self.STEPS[j]))

    def run(self, f):
        self.term(0, f)
        self.term(1, f)
        self.first()
        self.term(2, f)
        self.side(1)
        self.term(3, f)
        self.side(2)
        self.relayed()

    def result(self):
        t = self.total(3)
        for c in self.ends:
            c.got()
        t = t + self.far[0].astype(F32) + self.far[1].astype(F32)
        for c in list(self.pair.values()) + self.out:
            c.gone()
        return t


def join(blocks):
    return jnp.concatenate(blocks, axis=1)


def set_masks(masks, begin):
    for i in range(4):
        n = 256 * (i + 1)
        b = lax.broadcasted_iota(jnp.int32, (n, 256), 0)
        a = lax.broadcasted_iota(jnp.int32, (n, 256), 1) + 256 * i

        def doc(t):
            return (t >= begin).astype(jnp.int32) + (t >= begin + DOC).astype(jnp.int32)

        masks[MASK_AT[i] : MASK_AT[i] + n] = jnp.where((b <= a) & (doc(a) == doc(b)), 0.0, NEG)


def probs_t(key, query, mask):
    s = nt(key, query) + mask
    e = jnp.exp(s - jnp.max(s, axis=0, keepdims=True))
    return e * (1.0 / jnp.sum(e, axis=0, keepdims=True))


def halves(v):
    return v[:, :HEAD_DIM], v[:, HEAD_DIM:]


MASK_AT = (0, 256, 768, 1536)
A_ROWS, B_ROWS = 112, 96
HALF = 96
EXTRA = 32
VW = 1664 + 256


def layer_kernel(
    segs, tok, grd, wa, ff, vec, qkvb, fcb,
    layer_out, input_grad, ffo, wao, vsum, qf, saved,
    *refs,
):
    (
        fs, ga, ba, wt, fw, qkv, att, gat, masks, hid, gpre, dk, dv,
        a0, a1, a2, a3, b0, b1, b2, b3,
        rt, rg, rwa, rff, frames, tsend, trecv, scr, rv, vecs, seg, fcbs,
        res, gsave, rows, gown, yr, x2, s2, wx, tl, igot, v0, vy, vz, vx,
        ss, rs, rsw, rsx, rseg, rsm, rsn, rst, loc, hz, hb, hy,
    ) = refs
    h = Here()
    net = Net(ss, rs)
    par = lax.rem(h.z, 2)
    last = h.p == 7
    ys = [h.rel(dy=d) for d in (1, 2, 3)]
    zp, zm, zo = h.rel(dz=1), h.rel(dz=-1), h.rel(dz=2)
    plane = [h.rel(dx, f, dy) for dy in range(4) for dx in range(4) for f in (0, 1) if dx or f or dy]
    meet(plane + [zp, zm, zo])

    for k, i in enumerate((2, 3)):
        tsend[k] = wa[i].astype(F32)[SUB - TAIL :].astype(BF)
    tail = net.send(tsend, trecv, (h.z, h.gx, lax.rem(h.gy + 1, 8)))

    def by_gx(src, dst):
        out = [net.send(src.at[h.gx ^ d], dst.at[h.gx], h.gxd(d)) for d in (1, 2, 3)]
        return out

    toks = by_gx(tok, rt)
    vgot = [net.send(vec, rv.at[h.gx], h.gxd(d)) for d in (1, 2, 3)]
    rt[h.gx] = tok[h.gx]
    rv[h.gx] = vec[...]
    at_zero = h.gy == 0
    alone = at_zero & (h.gx == 0)
    for j in range(8):
        me = (h.gx == 0) if j == 0 else False
        cond = at_zero & jnp.logical_not(me)
        net.send(segs, seg, h.at(j // 2, j % 2, h.gx, h.z), send_if=cond, rs=rseg.at[0])

    @pl.when(alone)
    def _():
        seg[...] = segs[...]

    fgot = [net.send(fcb, fcbs.at[h.y], d) for d in ys]
    fcbs[h.y] = fcb[...]

    row = lax.broadcasted_iota(jnp.int32, (FRAME, QUARTER), 0)
    half_own = cut(HALF * par, HALF)
    extra_own = cut(192 + EXTRA * par, EXTRA)
    fsends = []
    for i in (1, 2, 0, 3):
        p, kind = h.unit(i)
        slot = i // 3
        if i == 0:
            tail.got()
        before = wa[i - 1].astype(F32)[SUB - TAIL :] if i in (1, 2) else trecv[i // 3].astype(F32)
        scr[pl.ds(pl.multiple_of(8 * p, 8), TAIL)] = before
        scr[pl.ds(pl.multiple_of(8 * p + TAIL, 8), SUB)] = wa[i].astype(F32)
        frames[i] = jnp.where((row < 192) | (p == 7), scr[TAIL : TAIL + FRAME], 0.0).astype(BF)
        dest = h.at(p // 2, lax.rem(p, 2), h.y, h.z)
        mine = p == h.p
        far = jnp.logical_not(mine)
        fsends.append(net.send(
            frames.at[i, half_own], rwa.at[slot, h.gx, pl.ds(0, HALF)], dest,
            send_if=far, rs=rsw.at[slot, h.gx],
        ))
        fsends.append(net.send(
            frames.at[i, extra_own], rwa.at[slot, h.gx, pl.ds(HALF, EXTRA)], dest,
            send_if=far & (p == 7), rs=rsx.at[slot, h.gx],
        ))

        @pl.when(mine)
        def _(i=i, slot=slot):
            rwa[slot, h.gx, 0:HALF] = frames[i, half_own]
            rwa[slot, h.gx, HALF : HALF + EXTRA] = frames[i, extra_own]

    for c in vgot:
        c.got()
    vecs[...] = join([rv[g] for g in range(4)])
    for c in toks:
        c.got()
    x = join([rt[g] for g in range(4)])
    rows[...] = x
    normed, _ = stats(x.astype(F32))
    my_rows = cut(ROWS * h.p, ROWS)
    fs[my_rows] = (normed * vecs[0:1] + vecs[1:2]).astype(BF)
    gather = Gather(h, net, fs)
    gather.start()
    ffs = [
        net.send(ff.at[h.gx ^ d, par], rff.at[h.gx], h.gxd(d)) for d in (1, 2, 3)
    ]
    ff_own = pltpu.make_async_copy(ff.at[h.gx, par], rff.at[h.gx], loc.at[0])
    ff_own.start()
    grds = by_gx(grd, rg)
    rg[h.gx] = grd[h.gx]

    by_y = {}
    for kind in range(4):
        slot = kind // 3
        held = h.holds(kind)
        gy, _ = h.block(kind, h.p)
        xh = lax.rem(gy, 2)
        for g in range(4):
            other = held & jnp.logical_not((g == h.gx) & (xh == h.xh))

            @pl.when(other)
            def _(slot=slot, g=g):
                push(
                    frames.at[0, pl.ds(0, HALF)], rwa.at[slot, g, pl.ds(0, HALF)], ss.at[0],
                    rsw.at[slot, g], ys[0],
                ).wait_recv()

            @pl.when(other & last)
            def _(slot=slot, g=g):
                push(
                    frames.at[0, pl.ds(0, EXTRA)], rwa.at[slot, g, pl.ds(HALF, EXTRA)], ss.at[0],
                    rsx.at[slot, g], ys[0],
                ).wait_recv()

        @pl.when(held)
        def _(kind=kind, slot=slot):
            wt[kind, half_own] = join([rwa[slot, g, 0:HALF] for g in range(4)])

        @pl.when(held & last)
        def _(kind=kind, slot=slot):
            wt[kind, extra_own] = join([rwa[slot, g, HALF : HALF + EXTRA] for g in range(4)])

        @pl.when(jnp.logical_not(last))
        def _(kind=kind):
            wt[kind, 192:FRAME] = jnp.zeros((64, D), BF)

        free = jnp.logical_not(held)
        for d in (1, 2, 3):
            comes = h.block(kind, h.p)[0] // 2 == lax.rem(h.y + 4 - d, 4)
            for what, cond in ((half_own, None), (extra_own, last)):
                s_if = held if cond is None else held & cond
                r_if = comes if cond is None else comes & cond
                ref = wt.at[kind, what]
                by_y.setdefault(kind, []).append(
                    net.send(ref, ref, ys[d - 1], send_if=s_if, recv_if=r_if)
                )

    by_z = {}

    def pass_z(kind):
        for c in by_y[kind]:
            c.got()
        for base, size, cond in ((HALF * par, 48, None), (192 + EXTRA * par, 16, last)):
            for off, d in ((0, zm), (size, zp)):
                ref = wt.at[kind, cut(base + off, size)]
                by_z.setdefault(kind, []).append(net.send(ref, ref, d, send_if=cond, recv_if=cond))

    gather.ready(0)
    gather.ready(1)
    for kind in range(3):
        pass_z(kind)
    gather.ready(2)
    gather.ready(3)

    ff_own.wait()
    for c in ffs:
        c.got()
    fslab = lambda y, k: cut((2 * y + k) * FPAD, FPAD)
    mine_ff = fslab(h.y, par)
    fw[mine_ff] = join([rff[g] for g in range(4)])
    ff_y = [net.send(fw.at[mine_ff], fw.at[mine_ff], d) for d in ys]
    ff_z = []

    def ff_pass(d):
        if d:
            ff_y[d - 1].got()
        base = (2 * lax.rem(h.y + 4 - d, 4) + par) * FPAD
        for off, size, to in ((0, A_ROWS, zm), (A_ROWS, B_ROWS, zp)):
            ref = fw.at[cut(base + off, size)]
            ff_z.append(net.send(ref, ref, to))

    ff_pass(0)
    for c in grds:
        c.got()
    gown[...] = join([rg[g] for g in range(4)])
    ga[my_rows] = gown[...]
    ggather = Gather(h, net, ga)
    ggather.start()

    @pl.when(jnp.logical_not(alone))
    def _():
        push(segs, seg, ss.at[0], rseg.at[0], ys[0]).wait_recv()

    begin = jnp.sum((seg[0:1] == 0).astype(F32), axis=1, keepdims=True).astype(jnp.int32)
    set_masks(masks, begin)
    for kind in range(3):
        for c in by_z[kind]:
            c.got()

    @pl.loop(0, 4)
    def _(chip):
        span = cut(256 * chip, 256)
        for kind in range(3):
            qkv[kind, span] = (nt(fs[span], wt[kind]) + qkvb[kind : kind + 1]).astype(BF)

    save = pltpu.make_async_copy(fs, saved, loc.at[1])
    save.start()
    for c in fsends:
        c.gone()
    pass_z(3)
    ggather.ready(0)
    ggather.ready(1)

    def attend(pair):
        lanes = pl.ds(128 * pair, 128)
        for i in range(4):
            n = 256 * (i + 1)
            mask = masks[MASK_AT[i] : MASK_AT[i] + n]
            outs = []
            for q, k, v in zip(
                halves(qkv[0, 256 * i : n, lanes]), halves(qkv[1, 0:n, lanes]), halves(qkv[2, 0:n, lanes])
            ):
                outs.append(tn(probs_t(k, q * 0.125, mask).astype(BF), v))
            att[256 * i : n, lanes] = join(outs).astype(BF)

    attend(0)
    ff_pass(1)
    ff_pass(3)
    ggather.ready(2)
    ggather.ready(3)
    attend(1)
    ff_pass(2)
    save.wait()
    for c in by_z[3]:
        c.got()

    sa = Scatter(h, net, (a0, a1, a2, a3))
    sa.run(lambda chip: nn(att[cut(256 * chip, 256)], wt[3]))
    r = rows[...].astype(F32) + sa.result() + vecs[2:3]
    res[...] = r
    normed, _ = stats(r)

    fs[my_rows] = (normed * vecs[3:4] + vecs[4:5]).astype(BF)
    gather = Gather(h, net, fs)
    gather.start()
    for c in ff_z + fgot:
        c.got()
    v0[...] = jnp.zeros_like(v0)
    for s in range(4):
        chip = gather.ready(s)

        @pl.loop(0, 4)
        def _(y, chip=chip):
            span = cut(256 * chip, 256)
            v = nt(fs[span], fw[fslab(y, 0)]) + fcbs[y, 0:1]
            up = nt(ga[span], fw[fslab(y, 1)])
            t = jnp.tanh(0.7978845608028654 * (v + 0.044715 * v * v * v))
            hid[y, span] = (0.5 * v * (1.0 + t)).astype(BF)
            slope = 0.5 * (1.0 + t) + 0.5 * v * (1.0 - t * t) * (
                0.7978845608028654 * (1.0 + 3 * 0.044715 * v * v)
            )
            gpre[y, span] = (up * slope).astype(BF)

    def total(src, k):
        def f(chip):
            return sum(nn(src[y, cut(256 * chip, 256)], fw[fslab(y, k)]) for y in range(4))

        return f

    sb = Scatter(h, net, (b0, b1, b2, b3))
    sb.run(total(gpre, 0))
    for c in ff_y + ff_z:
        c.gone()
    sa = Scatter(h, net, (a0, a1, a2, a3))
    for j in range(4):
        sa.term(j, total(hid, 1))

    @pl.loop(0, 4)
    def _(y):
        fw[fslab(y, 0)] = tn(gpre[y], fs[...]).astype(BF)
        fw[fslab(y, 1)] = tn(hid[y], ga[...]).astype(BF)

    for y in range(4):
        v0[2 + y : 3 + y, 1664 : 1664 + FPAD] = rows_of(gpre[y].astype(F32))
    for d in (zm, zp):
        pl.semaphore_signal(hz, inc=1, device_id=d, device_id_type=MESH)
    load = pltpu.make_async_copy(saved, fs, loc.at[1])
    load.start()

    gs = sb.result()
    normed, inv = stats(res[...])
    up = gown[...].astype(F32)
    gres = up + norm_back(gs, vecs[3:4], normed, inv)
    gsave[...] = gres
    low = gres.astype(BF)
    ba[my_rows] = low
    gather = Gather(h, net, ba)
    gather.start()
    v0[2:3, 0:D] = rows_of(gs * normed)
    v0[3:4, 0:D] = rows_of(gs)
    v0[4:5, 0:D] = rows_of(low.astype(F32))
    v0[5:6, 0:D] = rows_of(up)

    pl.semaphore_wait(hz, 2)
    one = {}
    for d in (2, 1, 3, 0):
        y = lax.rem(h.y + d, 4)
        base = (2 * y + 1 - par) * FPAD
        one[d] = [
            net.send(fw.at[cut(base + off, size)], ga.at[cut(FPAD * y + off, size)], to)
            for off, size, to in ((0, A_ROWS, zm), (A_ROWS, B_ROWS, zp))
        ]

    for s in range(4):
        chip = gather.ready(s)
        span = cut(256 * chip, 256)
        gat[span] = nt(ba[span], wt[3]).astype(BF)
    for j in (1, 2):
        if j == 1:
            sa.first()
        sa.side(j)
    for kind in range(4):
        for c in by_y[kind] + by_z[kind]:
            c.gone()
    wt[3] = tn(att[...], ba[...]).astype(BF)
    for d in (zm, zp):
        pl.semaphore_signal(hb, inc=1, device_id=d, device_id_type=MESH)

    two = {}

    def collect(d):
        for c in one[d]:
            c.got()
        y = lax.rem(h.y + d, 4)
        span = fslab(y, par)
        fw[span] = (fw[span].astype(F32) + ga[cut(FPAD * y, FPAD)].astype(F32)).astype(BF)
        if d:
            two[d] = net.send(fw.at[span], yr.at[d - 1, pl.ds(0, FPAD)], ys[d - 1])

    def attend_back(pair):
        lanes = pl.ds(128 * pair, 128)
        dk[...] = jnp.zeros_like(dk)
        dv[...] = jnp.zeros_like(dv)
        for i in range(4):
            n = 256 * (i + 1)
            mask = masks[MASK_AT[i] : MASK_AT[i] + n]
            dqs, dks, dvs = [], [], []
            for q, k, v, g in zip(
                halves(qkv[0, 256 * i : n, lanes]), halves(qkv[1, 0:n, lanes]),
                halves(qkv[2, 0:n, lanes]), halves(gat[256 * i : n, lanes]),
            ):
                q = q * 0.125
                probs = probs_t(k, q, mask)
                dvs.append(nn(probs.astype(BF), g))
                prod = probs * nt(v, g)
                ds = (prod - probs * jnp.sum(prod, axis=0, keepdims=True)).astype(BF)
                dks.append(nn(ds, q))
                dqs.append(tn(ds, k) * 0.125)
            dv[:n] += join(dvs)
            dk[:n] += join(dks)
            qkv[0, 256 * i : n, lanes] = join(dqs).astype(BF)
        qkv[1, :, lanes] = dk[...].astype(BF)
        qkv[2, :, lanes] = dv[...].astype(BF)

    attend_back(0)
    sa.relayed()
    collect(2)
    collect(1)
    attend_back(1)
    collect(3)
    collect(0)

    for c in toks:
        c.gone()
    out = (res[...] + sa.result() + vecs[5:6]).astype(BF)
    for g in range(4):
        rt[g] = out[:, QUARTER * g : QUARTER * (g + 1)]
    by_gx(rt, layer_out)
    lo_own = pltpu.make_async_copy(rt.at[h.gx], layer_out.at[h.gx], loc.at[2])
    lo_own.start()

    sb = Scatter(h, net, (b0, b1, b2, b3))
    sb.run(lambda chip: sum(nn(qkv[k, cut(256 * chip, 256)], wt[k]) for k in range(3)))
    load.wait()

    @pl.loop(0, 3)
    def _(kind):
        wt[kind] = tn(qkv[kind], fs[...]).astype(BF)

    pl.semaphore_wait(hb, 2)
    wone = {}
    for kind in (3, 0, 1, 2):
        for base, at, size, cond in (
            (HALF * (1 - par), 0, 48, None), (192 + EXTRA * (1 - par), HALF, 16, last),
        ):
            for k, to in ((0, zm), (1, zp)):
                wone.setdefault(kind, []).append(
                    net.send(
                        wt.at[kind, cut(base + size * k, size)],
                        ba.at[pl.ds(128 * kind + at + size * k, size)], to, send_if=cond, recv_if=cond,
                    )
                )
    v0[0:1, 1664:VW] = rows_of(qkv[0].astype(F32))
    v0[1:2, 1664:VW] = rows_of(qkv[2].astype(F32))

    s = fw[fslab(h.y, par)].astype(F32)
    for d in (1, 2, 3):
        two[d].got()
        s = s + yr[d - 1, 0:FPAD].astype(F32)
    s2[0:FPAD] = s.astype(BF)
    for d in ys:
        pl.semaphore_signal(hy, inc=1, device_id=d, device_id_type=MESH)
    three = net.send(s2.at[pl.ds(0, FPAD)], x2, zo)

    gf = sb.result()
    normed, inv = stats(rows[...].astype(F32))
    low = (gsave[...] + norm_back(gf, vecs[0:1], normed, inv)).astype(BF)
    v0[0:1, 0:D] = rows_of(gf * normed)
    v0[1:2, 0:D] = rows_of(gf)
    for c in grds:
        c.gone()
    for g in range(4):
        rg[g] = low[:, QUARTER * g : QUARTER * (g + 1)]
    igs = by_gx(rg, igot)
    igot[h.gx] = rg[h.gx]
    vys = [net.send(v0, vy.at[h.y], d) for d in ys]
    vy[h.y] = v0[...]

    three.got()
    full = (s2[0:FPAD].astype(F32) + x2[...].astype(F32)).astype(BF)
    for c in ffs:
        c.gone()
    for g in range(4):
        rff[g] = full[:, QUARTER * g : QUARTER * (g + 1)]
    four = [net.send(rff.at[h.gx ^ d], ffo.at[par, h.gx], h.gxd(d)) for d in (1, 2, 3)]
    ffo_own = pltpu.make_async_copy(rff.at[h.gx], ffo.at[par, h.gx], loc.at[3])
    ffo_own.start()
    three.gone()

    pl.semaphore_wait(hy, 3)
    wtwo = {}
    spans = ((half_own, 0, HALF, None), (extra_own, HALF, EXTRA, last))
    for kind in range(4):
        slot, held = kind // 3, h.holds(kind)
        home = h.block(kind, h.p)[0] // 2
        for c in wone[kind]:
            c.got()
        for mine, at, size, cond in spans:

            def add(mine=mine, at=at, size=size, kind=kind):
                s = wt[kind, mine].astype(F32) + ba[128 * kind + at : 128 * kind + at + size].astype(F32)
                wt[kind, mine] = s.astype(BF)

            if cond is None:
                add()
            else:
                pl.when(cond)(add)
            for d in (1, 2, 3):
                goes, comes = lax.rem(h.y + d, 4) == home, held
                if cond is not None:
                    goes, comes = goes & cond, comes & cond
                wtwo.setdefault(kind, []).append(
                    net.send(
                        wt.at[kind, mine], yr.at[d - 1, pl.ds(128 * slot + at, size)], ys[d - 1],
                        send_if=goes, recv_if=comes,
                    )
                )

    for c in igs:
        c.got()
    input_grad[...] = igot[...].astype(F32)
    for c in vys:
        c.got()
    vz[h.z] = (vy[0] + vy[1]) + (vy[2] + vy[3])
    vzs = [net.send(vz.at[h.z], vz.at[h.z], h.rel(dz=d)) for d in (1, 2, 3)]

    ffo_own.wait()
    for c in four:
        c.got()
    for at, size, to in ((0, A_ROWS, zm), (A_ROWS, B_ROWS, zp)):
        ref = ffo.at[par, :, pl.ds(at, size)]
        net.send(ref, ref, to)

    wthree = {}
    for kind in range(4):
        slot, held = kind // 3, h.holds(kind)
        for c in wtwo[kind]:
            c.got()
        for mine, at, size, cond in spans:
            ok = held if cond is None else held & cond
            low_at = 128 * slot + at

            @pl.when(ok)
            def _(kind=kind, mine=mine, size=size, low_at=low_at):
                s = wt[kind, mine].astype(F32)
                for d in range(3):
                    s = s + yr[d, low_at : low_at + size].astype(F32)
                s2[low_at : low_at + size] = s.astype(BF)

            wthree.setdefault(kind, []).append(
                net.send(
                    s2.at[pl.ds(low_at, size)], wx.at[pl.ds(low_at, size)], zo, send_if=ok, recv_if=ok
                )
            )

    for c in vzs:
        c.got()
    vx[h.p] = (vz[0] + vz[1]) + (vz[2] + vz[3])
    vxs = [net.send(vx.at[h.p], vx.at[h.p], d) for d in h.ring()]

    for kind in range(4):
        slot, held = kind // 3, h.holds(kind)
        gy, place = h.block(kind, h.p)
        gyt, placet = h.block(kind, h.p - 1)
        xh, xht, yt = lax.rem(gy, 2), lax.rem(gyt, 2), gyt // 2
        for c in wthree[kind]:
            c.got()
        for mine, at, size, cond in spans:
            ok = held if cond is None else held & cond
            low_at = 128 * slot + at

            @pl.when(ok)
            def _(slot=slot, at=at, size=size, low_at=low_at):
                span = slice(low_at, low_at + size)
                full = (s2[span].astype(F32) + wx[span].astype(F32)).astype(BF)
                for g in range(4):
                    rwa[slot, g, at : at + size] = full[:, QUARTER * g : QUARTER * (g + 1)]

            for g in range(4):
                same = (g == h.gx) & (xh == h.xh)
                net.send(
                    rwa.at[slot, g, pl.ds(at, size)], frames.at[place, mine], (h.z, g, gy),
                    send_if=ok & jnp.logical_not(same), rs=(rsm if cond is None else rsn).at[place],
                )

                @pl.when(ok & same)
                def _(slot=slot, g=g, place=place, mine=mine, at=at, size=size):
                    frames[place, mine] = rwa[slot, g, at : at + size]

        for g in range(4):
            same = (g == h.gx) & (xht == h.xh) & (yt == h.y)
            ok = held & (h.p > 0) & (par == 0)
            net.send(
                rwa.at[slot, g, pl.ds(0, TAIL)], tl.at[placet], (h.z, g, gyt),
                send_if=ok & jnp.logical_not(same), rs=rst.at[placet],
            )

            @pl.when(ok & same)
            def _(slot=slot, g=g, placet=placet):
                tl[placet] = rwa[slot, g, 0:TAIL]

    wfive = {}
    for i in range(4):
        p, kind = h.unit(i)
        four_heads = p == 7
        far = p != h.p

        @pl.when(far)
        def _(i=i):
            push(
                frames.at[0, pl.ds(0, HALF)], frames.at[i, pl.ds(0, HALF)], ss.at[0], rsm.at[i], ys[0]
            ).wait_recv()

        @pl.when(far & four_heads)
        def _(i=i):
            push(
                frames.at[0, pl.ds(0, EXTRA)], frames.at[i, pl.ds(0, EXTRA)], ss.at[0], rsn.at[i], ys[0]
            ).wait_recv()

        follow = (p + 1) // 2 if i == 3 else (kind * 8 + p + 1) // 6
        has_tail = jnp.logical_not(four_heads)

        @pl.when(has_tail & (par == 0) & jnp.logical_not((p + 1 == h.p) & (follow == h.y)))
        def _(i=i):
            push(tl.at[0], tl.at[i], ss.at[0], rst.at[i], ys[0]).wait_recv()

        for base, size, cond in (
            (HALF * par, 48, None), (192 + EXTRA * par, 16, four_heads),
        ):
            for k, to in ((0, zm), (1, zp)):
                ref = frames.at[i, cut(base + size * k, size)]
                wfive.setdefault(i, []).append(net.send(ref, ref, to, send_if=cond, recv_if=cond))
        for k, to in ((0, zm), (1, zp)):
            ref = tl.at[i, pl.ds(32 * k, 32)]
            wfive[i].append(
                net.send(
                    ref, ref, to, send_if=has_tail & (par == 0), recv_if=has_tail & (par == 1)
                )
            )

    for c in vxs:
        c.got()
    total_v = vx[0]
    for p in range(1, 8):
        total_v = total_v + vx[p]
    vsum[...] = total_v[:, 0:D]
    qf[...] = vx[:, :, 1664:VW]
    for i in range(4):
        p, _ = h.unit(i)
        for c in wfive[i]:
            c.got()
        scr[0:FRAME] = frames[i].astype(F32)

        @pl.when(p < 7)
        def _(i=i):
            scr[192 : 192 + TAIL] = tl[i].astype(F32)

        wao[i] = scr[pl.ds(pl.multiple_of(8 * p, 8), SUB)].astype(BF)

    lo_own.wait()
    net.finish()


def layer(segs, tok, grd, wa, ff, vec, qkvb, fcb):
    any_ = pl.BlockSpec(memory_space=pl.ANY)
    scratch = [
        pltpu.VMEM((SEQ, D), BF),
        pltpu.VMEM((SEQ, D), BF),
        pltpu.VMEM((SEQ, D), BF),
        pltpu.VMEM((4, FRAME, D), BF),
        pltpu.VMEM((8 * FPAD, D), BF),
        pltpu.VMEM((3, SEQ, FRAME), BF),
        pltpu.VMEM((SEQ, FRAME), BF),
        pltpu.VMEM((SEQ, FRAME), BF),
        pltpu.VMEM((2560, 256), F32),
        pltpu.VMEM((4, SEQ, FPAD), BF),
        pltpu.VMEM((4, SEQ, FPAD), BF),
        pltpu.VMEM((SEQ, 2 * HEAD_DIM), F32),
        pltpu.VMEM((SEQ, 2 * HEAD_DIM), F32),
        *Scatter.scratch(),
        *Scatter.scratch(),
        pltpu.VMEM((4, ROWS, QUARTER), BF),
        pltpu.VMEM((4, ROWS, QUARTER), BF),
        pltpu.VMEM((2, 4, HALF + EXTRA, QUARTER), BF),
        pltpu.VMEM((4, FPAD, QUARTER), BF),
        pltpu.VMEM((4, FRAME, QUARTER), BF),
        pltpu.VMEM((2, TAIL, QUARTER), BF),
        pltpu.VMEM((2, TAIL, QUARTER), BF),
        pltpu.VMEM((336, QUARTER), F32),
        pltpu.VMEM((4, 8, QUARTER), F32),
        pltpu.VMEM((8, D), F32),
        pltpu.VMEM((8, 128), jnp.int32),
        pltpu.VMEM((4, 8, FPAD), F32),
        pltpu.VMEM((ROWS, D), F32),
        pltpu.VMEM((ROWS, D), F32),
        pltpu.VMEM((ROWS, D), BF),
        pltpu.VMEM((ROWS, D), BF),
        pltpu.VMEM((3, FRAME, D), BF),
        pltpu.VMEM((FPAD, D), BF),
        pltpu.VMEM((FRAME, D), BF),
        pltpu.VMEM((FRAME, D), BF),
        pltpu.VMEM((4, TAIL, QUARTER), BF),
        pltpu.VMEM((4, ROWS, QUARTER), BF),
        pltpu.VMEM((8, VW), F32),
        pltpu.VMEM((4, 8, VW), F32),
        pltpu.VMEM((4, 8, VW), F32),
        pltpu.VMEM((8, 8, VW), F32),
        pltpu.SemaphoreType.DMA((Net.SIZE,)),
        pltpu.SemaphoreType.DMA((Net.SIZE,)),
        pltpu.SemaphoreType.DMA((2, 4)),
        pltpu.SemaphoreType.DMA((2, 4)),
        pltpu.SemaphoreType.DMA((1,)),
        pltpu.SemaphoreType.DMA((4,)),
        pltpu.SemaphoreType.DMA((4,)),
        pltpu.SemaphoreType.DMA((4,)),
        pltpu.SemaphoreType.DMA((4,)),
        pltpu.SemaphoreType.REGULAR,
        pltpu.SemaphoreType.REGULAR,
        pltpu.SemaphoreType.REGULAR,
    ]
    return pl.pallas_call(
        layer_kernel,
        out_shape=[
            jax.ShapeDtypeStruct((4, ROWS, QUARTER), BF),
            jax.ShapeDtypeStruct((4, ROWS, QUARTER), F32),
            jax.ShapeDtypeStruct((2, 4, FPAD, QUARTER), BF),
            jax.ShapeDtypeStruct((4, SUB, QUARTER), BF),
            jax.ShapeDtypeStruct((8, D), F32),
            jax.ShapeDtypeStruct((8, 8, 256), F32),
            jax.ShapeDtypeStruct((SEQ, D), BF),
        ],
        in_specs=[VMEM, VMEM, VMEM, VMEM, any_, VMEM, VMEM, VMEM],
        out_specs=[any_, VMEM, any_, VMEM, VMEM, VMEM, any_],
        scratch_shapes=scratch,
        compiler_params=pltpu.CompilerParams(
            collective_id=0, has_side_effects=True, vmem_limit_bytes=64 * 2**20 - 2**16
        ),
        name="layer",
    )(segs, tok, grd, wa, ff, vec, qkvb, fcb)


def per_device(
    tokens_in, segments, norm1_gain, norm1_bias, qkv_weight, query_bias, value_bias, proj_weight,
    proj_bias, norm2_gain, norm2_bias, fc_weight, fc_bias, out_weight, out_bias, out_grad,
):
    gx, gy = lax.axis_index("gx"), lax.axis_index("gy")
    y, xh = gy // 2, lax.rem(gy, 2)
    p = xh * 4 + gx
    wa = jnp.concatenate([qkv_weight.T.reshape(3, SUB, QUARTER), proj_weight.T[None]])
    ff = jnp.stack(
        [fc_weight.T.reshape(4, SUB, QUARTER), out_weight.T.reshape(4, SUB, QUARTER)], axis=1
    )
    ff = jnp.pad(ff, ((0, 0), (0, 0), (0, FPAD - SUB), (0, 0)))
    zero = jnp.zeros_like(norm1_gain)
    vec = jnp.stack(
        [norm1_gain, norm1_bias, proj_bias, norm2_gain, norm2_bias, out_bias, zero, zero]
    )
    valid = (jnp.arange(FRAME) < 192) | (p == 7)
    qb = jnp.where(valid, lax.dynamic_slice_in_dim(query_bias, 192 * p, FRAME), 0.0)
    vb = jnp.where(valid, lax.dynamic_slice_in_dim(value_bias, 192 * p, FRAME), 0.0)
    nil = jnp.zeros_like(qb)
    qkvb = jnp.stack([qb, nil, vb, nil, nil, nil, nil, nil])
    fcb = jnp.pad(lax.dynamic_slice_in_dim(fc_bias, SUB * gx, SUB), (0, FPAD - SUB))
    fcb = jnp.broadcast_to(fcb, (8, FPAD))
    layer_out, input_grad, ffo, wao, vsum, qf, _ = layer(
        jnp.broadcast_to(segments, (8, ROWS)),
        tokens_in.reshape(4, ROWS, QUARTER), out_grad.reshape(4, ROWS, QUARTER),
        wa, ff, vec, qkvb, fcb,
    )
    mine = lax.dynamic_slice_in_dim(vsum, QUARTER * gx, QUARTER, 1)

    def heads(v):
        return jnp.concatenate([v[:, :192].reshape(8 * 192), v[7, 192:]])

    fcp = lax.dynamic_slice(qf, (4 * xh, 2 + y, 0), (4, 1, SUB)).reshape(4 * SUB)

    def whole(v):
        return v[:, :SUB].reshape(4 * SUB, QUARTER).T.astype(F32)

    return (
        layer_out.reshape(4 * ROWS, QUARTER),
        input_grad.reshape(4 * ROWS, QUARTER),
        mine[0],
        mine[1],
        wao[0:3].reshape(3 * SUB, QUARTER).T.astype(F32),
        heads(qf[:, 0]),
        heads(qf[:, 1]),
        wao[3].T.astype(F32),
        mine[4],
        mine[2],
        mine[3],
        whole(ffo[0]),
        fcp,
        whole(ffo[1]),
        mine[5],
    )


def solution(mesh):
    return jax.shard_map(
        per_device,
        mesh=mesh,
        in_specs=(
            P(("dp", "gy"), "gx"), P(("dp", "gx"), "gy"), P("gx"), P("gx"), P("gx", "gy"), P(), P(),
            P("gx", "gy"), P("gx"), P("gx"), P("gx"), P("gx", "gy"), P("gy"), P("gx", "gy"), P("gx"),
            P(("dp", "gy"), "gx"),
        ),
        out_specs=(
            P(("dp", "gy"), "gx"), P(("dp", "gy"), "gx"), P("gx"), P("gx"), P("gx", "gy"), P(), P(),
            P("gx", "gy"), P("gx"), P("gx"), P("gx"), P("gx", "gy"), P("gy"), P("gx", "gy"), P("gx"),
        ),
        check_vma=False,
    )
```

time: 2020 us -> 344 us (0.17)
  waiting for transfers between devices: 1510 us -> 0 us
  Pallas kernels: 0 us -> 311 us
  matrix products: 178 us -> 0 us
  blocking collectives: 128 us -> 0 us
  other arithmetic: 97.8 us -> 5.25 us
  local copies, waits for them, and re-layouts: 74 us -> 20.9 us
    reduce_scatter x8 -> x0, waiting for transfers between devices: 722 us -> none  [the longest x4 363 us: sum_gy(): lax.psum_scatter(term(jnp.int32(0), lax.axis_size('gy') * (left.shape[0]...]
    all_gather x12 -> x0, waiting for transfers between devices: 577 us -> none  [the longest x4 238 us: gather_gy(): return lax.all_gather(values, 'gy', axis=0, tiled=True)]
    pallas_call x0 -> x1, Pallas kernels: none -> 311 us  [layer(): pl.pallas_call(layer_kernel, out_shape=[jax.ShapeDtypeStruct((4, ROWS, QU...]
    psum x2 -> x0, waiting for transfers between devices: 198 us -> none  [the longest x1 136 us: per_device(): lax.psum((placed, fc_placed, query_value), ('dp', 'gx', 'gy'))]
    dot_general x30 -> x0, matrix products: 178 us -> none  [the longest x8 42 us: masked_scores(): jnp.einsum('sahe,sbhe->shab', queries, keys, preferred_element_type=jnp.f...]
    all_to_all x3 -> x0, blocking collectives: 55.9 us -> none  [the longest x2 33.4 us: to_rows(): lax.all_to_all(values, 'gy', split_axis=2, concat_axis=1, tiled=True)]
    unnamed x12 -> x0, other arithmetic: 51.6 us -> none
    all_gather x2 -> x0, blocking collectives: 44.8 us -> none  [the longest x1 30.2 us: per_device(): all_stats = lax.all_gather(stats_rows, 'gy', axis=1, tiled=True)]
  transfers between devices with their start and end apart: 23 -> 0, of which waited for: 22 -> 0; matrix products, arithmetic and copies ran while one was open for 7% -> 0% of each run, Pallas kernels for 0% -> 0%
where the time goes in v2:
time: 344 us; the launch traced here: 338 us
  Pallas kernels  311 us (90%)
  local copies, waits for them, and re-layouts  20.9 us (6%)
  other arithmetic  5.25 us (2%)
    pallas_call x1, Pallas kernels, layer(): pl.pallas_call(layer_kernel, out_shape=[jax.ShapeDtypeStruct((4, ROWS, QU...  311 us

profile of v2, /device:TPU:27, one launch (start us, length us, event | category | flops | bytes accessed | tf_op | source)
XLA Modules:
  0.0 338.0 jit_solution(4701607126488470875)
XLA Ops:
  0.6 0.0 copy-start.2
  0.7 0.9 dynamic-slice_select_fusion
  1.5 0.6 stack.51.qkvb
  2.2 0.8 dynamic_slice.17
  2.9 0.6 broadcast_in_dim.22.fcb
  3.5 1.4 copy.36
  4.9 0.3 copy.35
  5.2 0.0 copy-start.4
  5.2 0.0 copy-start.7
  5.3 1.4 fusion.2.ff
  6.7 0.2 copy.33
  6.9 0.0 copy-start.6
  7.0 0.1 copy.34
  7.1 0.0 copy-start.8
  7.1 0.0 copy-start.9
  7.1 0.0 copy-start.10
  7.1 0.0 copy-start.11
  7.1 0.0 copy-start.12
  7.1 0.0 copy-start.13
  7.2 0.0 copy-start.14
  7.2 1.0 pad_maximum_fusion.wa
  8.2 1.0 copy.31
  9.2 1.0 copy.32
  10.2 0.6 stack.47.vec
  10.8 0.6 broadcast_in_dim.19.segs
  11.4 310.7 %layer.1 = (bf16[4,128,400]{2,1,0:T(8,128)(2,1)}, f32[4,128,400]{2,1,0:T(8,128)}, bf16[2,4,208,400]{3,2,1,0:T(8,128)(2,1)}, bf16[4,200,400]{2,1,0:T(8,128)(2,1)}...) custom-call(s32[8,128]{1,0:T(8,128)} %broadcast_in_dim.19.segs, ...), custom_call_target="tpu_custom_call" | custom-call | tf_op jit(solution)/shard_map/layer/pallas_call | solution.py:989
  322.2 1.5 slice_bitcast_fusion
  323.7 0.1 slice.76
  323.7 0.3 bitcast_convert_fusion.1
  324.0 1.6 copy.38
  325.6 0.1 slice.77
  325.7 0.3 bitcast_convert_fusion
  326.0 1.6 copy.39
  327.6 0.9 fusion.3
  328.5 0.1 reshape.71
  328.6 0.1 slice_bitcast_fusion.2
  328.7 0.6 pad_maximum_fusion.2
  329.3 0.1 reshape.70
  329.4 0.1 slice_bitcast_fusion.3
  329.4 0.6 pad_maximum_fusion.1
  330.1 0.2 bitcast_convert_fusion.2
  330.3 1.3 copy.37
  331.6 1.2 copy.41
  332.9 0.9 copy.42
  333.8 0.9 copy.40
  334.7 0.8 dynamic-slice_reduce_fusion
  335.5 0.7 reshape.72
  336.2 1.6 fusion.4
  (27 shorter events, 0.1 us)
Async XLA Ops:
  0.6 4.3 %copy-start.2 = (bf16[400,800]{1,0:T(8,128)(2,1)S(1)}, bf16[400,800]{1,0:T(8,128)(2,1)}, u32[]{:S(2)}) copy-start(bf16[400,800]{1,0:T(8,128)(2,1)} %param.27) | copy-start | bytes 1920004
  5.2 1.5 copy-start.4
  5.2 1.7 copy-start.7
  6.7 1.5 copy-start.5
  6.9 2.2 copy-start.6
  7.1 3.1 copy-start.8
  7.1 3.1 copy-start.9
  7.1 3.1 copy-start.10
  7.1 3.1 copy-start.11
  7.1 3.1 copy-start.12
  7.1 3.1 copy-start.13
  7.2 3.7 %copy-start.14 = (s32[1,128]{1,0:T(1,128)S(1)}, s32[1,128]{1,0:T(1,128)}, u32[]{:S(2)}) copy-start(s32[1,128]{1,0:T(1,128)} %param.17) | copy-start | bytes 1540
  326.0 4.1 %copy-start.1 = (bf16[4,200,400]{2,1,0:T(8,128)(2,1)S(1)}, bf16[4,200,400]{2,1,0:T(8,128)(2,1)}, u32[]{:S(2)}) copy-start(bf16[4,200,400]{2,1,0:T(8,128)(2,1)} %get-tuple-element.24) | copy-start | bytes 1920004
  330.1 1.6 copy-start
  331.6 2.2 copy-start.3

commit v3 on v2

--- a/solution.py
+++ b/solution.py
@@ -139,7 +139,7 @@
 
 
 class Net:
-    SIZE = 360
+    SIZE = 424
 
     def __init__(self, ss, rs):
         self.ss, self.rs, self.n, self.copies = ss, rs, 0, []
@@ -184,6 +184,9 @@
         self.r[1] = self.go(0, self.right, 1)
         self.l[0] = self.go(0, self.left, 0)
         self.own = self.go(0, self.sib)
+
+    def chip(self, s):
+        return lax.rem(self.h.x + (0, 3, 1, 2)[s], 4)
 
     def ready(self, s):
         h = self.h
@@ -219,7 +222,7 @@
     @staticmethod
     def scratch():
         return [
-            pltpu.VMEM((4, 2, ROWS, D), BF),
+            pltpu.VMEM((SEQ, D), BF),
             pltpu.VMEM((4, ROWS, D), BF),
             pltpu.VMEM((2, ROWS, D), BF),
             pltpu.VMEM((ROWS, D), BF),
@@ -230,44 +233,48 @@
     def __init__(self, here, net, refs):
         self.h, self.net = here, net
         self.part, self.mate, self.far, self.relay = refs
-        self.pair, self.out = {}, []
+        self.pair, self.out, self.ends = {}, [], []
+
+    def at(self, j, c, half=None):
+        base = 256 * j + ROWS * c
+        return cut(base, ROWS) if half is None else cut(base + 64 * half, 64)
 
     def term(self, j, f):
         h = self.h
         chip = lax.rem(h.x + 4 + self.STEPS[j], 4)
-        self.part[j] = f(chip).astype(BF).reshape(2, ROWS, D)
-        self.pair[j] = self.net.send(self.part.at[j, 1 - h.c], self.mate.at[j], h.rel(0, 1))
+        self.part[256 * j : 256 * (j + 1)] = f(chip).astype(BF)
+        self.pair[j] = self.net.send(
+            self.part.at[self.at(j, 1 - h.c)], self.mate.at[j], h.rel(0, 1)
+        )
 
     def total(self, j):
         self.pair[j].got()
-        return self.part[j, self.h.c].astype(F32) + self.mate[j].astype(F32)
+        return self.part[self.at(j, self.h.c)].astype(F32) + self.mate[j].astype(F32)
 
     def link(self, j, half, dst, dx):
-        src = self.part.at[j, self.h.c, pl.ds(64 * half, 64)]
-        c = self.net.send(src, dst, self.h.rel(dx))
+        c = self.net.send(self.part.at[self.at(j, self.h.c, half)], dst, self.h.rel(dx))
         self.out.append(c)
         return c
 
     def first(self):
-        self.part[0, self.h.c] = self.total(0).astype(BF)
+        self.part[self.at(0, self.h.c)] = self.total(0).astype(BF)
         self.in_r = self.link(0, 0, self.relay.at[pl.ds(0, 64)], 1)
         self.in_l = self.link(0, 1, self.relay.at[pl.ds(64, 64)], -1)
 
     def side(self, j):
         half = 1 if j == 1 else 0
-        self.part[j, self.h.c] = self.total(j).astype(BF)
-        c = self.link(j, half, self.far.at[j - 1, pl.ds(64 * half, 64)], self.STEPS[j])
-        self.ends = getattr(self, "ends", []) + [c]
+        self.part[self.at(j, self.h.c)] = self.total(j).astype(BF)
+        self.ends.append(self.link(j, half, self.far.at[j - 1, pl.ds(64 * half, 64)], self.STEPS[j]))
 
     def relayed(self):
         for j, half, c in ((1, 0, self.in_r), (2, 1, self.in_l)):
             c.got()
-            span = pl.ds(64 * half, 64)
-            s = self.part[j, self.h.c, span].astype(F32) + self.relay[span].astype(F32)
-            self.part[j, self.h.c, span] = s.astype(BF)
+            span, mine = pl.ds(64 * half, 64), self.at(j, self.h.c, half)
+            s = self.part[mine].astype(F32) + self.relay[span].astype(F32)
+            self.part[mine] = s.astype(BF)
             self.ends.append(self.link(j, half, self.far.at[j - 1, span], self.STEPS[j]))
 
-    def run(self, f):
+    def begin(self, f):
         self.term(0, f)
         self.term(1, f)
         self.first()
@@ -275,6 +282,9 @@
         self.side(1)
         self.term(3, f)
         self.side(2)
+
+    def run(self, f):
+        self.begin(f)
         self.relayed()
 
     def result(self):
@@ -300,11 +310,13 @@
         def doc(t):
             return (t >= begin).astype(jnp.int32) + (t >= begin + DOC).astype(jnp.int32)
 
-        masks[MASK_AT[i] : MASK_AT[i] + n] = jnp.where((b <= a) & (doc(a) == doc(b)), 0.0, NEG)
+        masks[MASK_AT[i] : MASK_AT[i] + n] = jnp.where(
+            (b <= a) & (doc(a) == doc(b)), 0.0, NEG
+        ).astype(BF)
 
 
 def probs_t(key, query, mask):
-    s = nt(key, query) + mask
+    s = nt(key, query) + mask.astype(F32)
     e = jnp.exp(s - jnp.max(s, axis=0, keepdims=True))
     return e * (1.0 / jnp.sum(e, axis=0, keepdims=True))
 
@@ -321,16 +333,16 @@
 
 
 def layer_kernel(
-    segs, tok, grd, wa, ff, vec, qkvb, fcb,
-    layer_out, input_grad, ffo, wao, vsum, qf, saved,
+    segs, tok, grd, wq, wp, fcw, otw, vec, bias,
+    layer_out, input_grad, gwa, gfc, got_, vsum, qsum, fsum, ffo, saved,
     *refs,
 ):
     (
         fs, ga, ba, wt, fw, qkv, att, gat, masks, hid, gpre, dk, dv,
         a0, a1, a2, a3, b0, b1, b2, b3,
-        rt, rg, rwa, rff, frames, tsend, trecv, scr, rv, vecs, seg, fcbs,
-        res, gsave, rows, gown, yr, x2, s2, wx, tl, igot, v0, vy, vz, vx,
-        ss, rs, rsw, rsx, rseg, rsm, rsn, rst, loc, hz, hb, hy,
+        rt, rg, rwa, rff, frames, tsend, trecv, scr, t32, stage, fbuf, rv, vecs, seg, fcb, fcbs,
+        res, gsave, rows, yr, s2, wx, tl, v0, vy, vz, vx,
+        ss, rs, rsw, rsx, rseg, rsm, rsn, rst, loc, hz, hb, hy, ho,
     ) = refs
     h = Here()
     net = Net(ss, rs)
@@ -339,19 +351,78 @@
     ys = [h.rel(dy=d) for d in (1, 2, 3)]
     zp, zm, zo = h.rel(dz=1), h.rel(dz=-1), h.rel(dz=2)
     plane = [h.rel(dx, f, dy) for dy in range(4) for dx in range(4) for f in (0, 1) if dx or f or dy]
-    meet(plane + [zp, zm, zo])
+    everyone = plane + [zp, zm, zo]
+    barrier = pltpu.get_barrier_semaphore()
+    for d in everyone:
+        pl.semaphore_signal(barrier, inc=1, device_id=d, device_id_type=MESH)
+
+    @pl.when(par == 0)
+    def _():
+        pltpu.make_async_copy(fcw, stage, loc.at[0]).start()
+
+    @pl.when(par == 1)
+    def _():
+        pltpu.make_async_copy(otw, stage, loc.at[0]).start()
+
+    t32[0 : 3 * SUB] = jnp.transpose(wq[...]).astype(F32)
+    t32[3 * SUB : 4 * SUB] = jnp.transpose(wp[...]).astype(F32)
+
+    def sub_tail(i):
+        return t32[SUB * (i + 1) - TAIL : SUB * (i + 1)]
 
     for k, i in enumerate((2, 3)):
-        tsend[k] = wa[i].astype(F32)[SUB - TAIL :].astype(BF)
+        tsend[k] = sub_tail(i).astype(BF)
+    row = lax.broadcasted_iota(jnp.int32, (FRAME, QUARTER), 0)
+    half_own = cut(HALF * par, HALF)
+    extra_own = cut(192 + EXTRA * par, EXTRA)
+
+    def frame(i, before):
+        p, _ = h.unit(i)
+        scr[pl.ds(pl.multiple_of(8 * p, 8), TAIL), 0:QUARTER] = before
+        scr[pl.ds(pl.multiple_of(8 * p + TAIL, 8), SUB), 0:QUARTER] = t32[SUB * i : SUB * (i + 1)]
+        frames[i] = jnp.where((row < 192) | (p == 7), scr[TAIL : TAIL + FRAME, 0:QUARTER], 0.0).astype(BF)
+
+    fsends = []
+
+    def send_frame(i):
+        p, _ = h.unit(i)
+        slot = i // 3
+        dest = h.at(p // 2, lax.rem(p, 2), h.y, h.z)
+        mine = p == h.p
+        far = jnp.logical_not(mine)
+        for src, at, size, cond, sem in (
+            (half_own, 0, HALF, far, rsw), (extra_own, HALF, EXTRA, far & (p == 7), rsx),
+        ):
+            fsends.append(
+                net.send(
+                    frames.at[i, src], rwa.at[slot, h.gx, pl.ds(at, size)], dest,
+                    send_if=cond, rs=sem.at[slot, h.gx],
+                )
+            )
+
+        @pl.when(mine)
+        def _():
+            rwa[slot, h.gx, 0:HALF] = frames[i, half_own]
+            rwa[slot, h.gx, HALF : HALF + EXTRA] = frames[i, extra_own]
+
+    for i in (1, 2):
+        frame(i, sub_tail(i - 1))
+    pl.semaphore_wait(barrier, len(everyone))
+
     tail = net.send(tsend, trecv, (h.z, h.gx, lax.rem(h.gy + 1, 8)))
 
+    def lanes_of(g):
+        return pl.ds(pl.multiple_of(ROWS * g, ROWS), ROWS)
+
     def by_gx(src, dst):
-        out = [net.send(src.at[h.gx ^ d], dst.at[h.gx], h.gxd(d)) for d in (1, 2, 3)]
-        return out
-
-    toks = by_gx(tok, rt)
+        return [net.send(src(h.gx ^ d), dst(h.gx), h.gxd(d)) for d in (1, 2, 3)]
+
+    toks = by_gx(lambda g: tok.at[:, lanes_of(g)], lambda g: rt.at[g])
+    for i in (1, 2):
+        send_frame(i)
     vgot = [net.send(vec, rv.at[h.gx], h.gxd(d)) for d in (1, 2, 3)]
-    rt[h.gx] = tok[h.gx]
+    tok_own = pltpu.make_async_copy(tok.at[:, lanes_of(h.gx)], rt.at[h.gx], loc.at[2])
+    tok_own.start()
     rv[h.gx] = vec[...]
     at_zero = h.gy == 0
     alone = at_zero & (h.gx == 0)
@@ -364,61 +435,73 @@
     def _():
         seg[...] = segs[...]
 
-    fgot = [net.send(fcb, fcbs.at[h.y], d) for d in ys]
-    fcbs[h.y] = fcb[...]
-
-    row = lax.broadcasted_iota(jnp.int32, (FRAME, QUARTER), 0)
-    half_own = cut(HALF * par, HALF)
-    extra_own = cut(192 + EXTRA * par, EXTRA)
-    fsends = []
-    for i in (1, 2, 0, 3):
-        p, kind = h.unit(i)
-        slot = i // 3
-        if i == 0:
-            tail.got()
-        before = wa[i - 1].astype(F32)[SUB - TAIL :] if i in (1, 2) else trecv[i // 3].astype(F32)
-        scr[pl.ds(pl.multiple_of(8 * p, 8), TAIL)] = before
-        scr[pl.ds(pl.multiple_of(8 * p + TAIL, 8), SUB)] = wa[i].astype(F32)
-        frames[i] = jnp.where((row < 192) | (p == 7), scr[TAIL : TAIL + FRAME], 0.0).astype(BF)
-        dest = h.at(p // 2, lax.rem(p, 2), h.y, h.z)
-        mine = p == h.p
-        far = jnp.logical_not(mine)
-        fsends.append(net.send(
-            frames.at[i, half_own], rwa.at[slot, h.gx, pl.ds(0, HALF)], dest,
-            send_if=far, rs=rsw.at[slot, h.gx],
-        ))
-        fsends.append(net.send(
-            frames.at[i, extra_own], rwa.at[slot, h.gx, pl.ds(HALF, EXTRA)], dest,
-            send_if=far & (p == 7), rs=rsx.at[slot, h.gx],
-        ))
-
-        @pl.when(mine)
-        def _(i=i, slot=slot):
-            rwa[slot, h.gx, 0:HALF] = frames[i, half_own]
-            rwa[slot, h.gx, HALF : HALF + EXTRA] = frames[i, extra_own]
+    def pick(values, index):
+        out = values[0]
+        for k, v in enumerate(values[1:]):
+            out = jnp.where(index == k + 1, v, out)
+        return out
 
     for c in vgot:
         c.got()
     vecs[...] = join([rv[g] for g in range(4)])
     for c in toks:
         c.got()
-    x = join([rt[g] for g in range(4)])
+    tok_own.wait()
+
+    def turn(ref):
+        return jnp.transpose(jnp.concatenate([ref[g] for g in range(4)], axis=0))
+
+    x = turn(rt)
     rows[...] = x
     normed, _ = stats(x.astype(F32))
     my_rows = cut(ROWS * h.p, ROWS)
     fs[my_rows] = (normed * vecs[0:1] + vecs[1:2]).astype(BF)
+    tail.got()
+    for i in (0, 3):
+        frame(i, trecv[i // 3].astype(F32))
+        send_frame(i)
+
     gather = Gather(h, net, fs)
     gather.start()
-    ffs = [
-        net.send(ff.at[h.gx ^ d, par], rff.at[h.gx], h.gxd(d)) for d in (1, 2, 3)
-    ]
-    ff_own = pltpu.make_async_copy(ff.at[h.gx, par], rff.at[h.gx], loc.at[0])
-    ff_own.start()
-    grds = by_gx(grd, rg)
-    rg[h.gx] = grd[h.gx]
-
-    by_y = {}
-    for kind in range(4):
+
+    @pl.when(par == 0)
+    def _():
+        pltpu.make_async_copy(fcw, stage, loc.at[0]).wait()
+
+    @pl.when(par == 1)
+    def _():
+        pltpu.make_async_copy(otw, stage, loc.at[0]).wait()
+
+    t32[...] = jnp.transpose(stage[...]).astype(F32)
+    blank = jnp.zeros((FPAD - SUB, QUARTER), F32)
+    for g in range(4):
+        fbuf[g] = jnp.concatenate([t32[SUB * g : SUB * (g + 1)], blank], axis=0).astype(BF)
+    ffs = by_gx(lambda g: fbuf.at[g], lambda g: rff.at[g])
+    rff[h.gx] = fbuf[h.gx]
+
+    low_bias = pick([bias[2:3, SUB * g : SUB * (g + 1)] for g in range(4)], h.gx)
+    fcb[...] = jnp.broadcast_to(join([low_bias, jnp.zeros((1, FPAD - SUB), F32)]), (8, FPAD))
+    fgot = [net.send(fcb, fcbs.at[h.y], d) for d in ys]
+    fcbs[h.y] = fcb[...]
+    lane = lax.broadcasted_iota(jnp.int32, (1, FRAME), 1)
+    qb, vb = (
+        jnp.where(
+            (lane < 192) | last, pick([bias[k : k + 1, 192 * p : 192 * p + FRAME] for p in range(8)], h.p), 0.0
+        )
+        for k in (0, 1)
+    )
+    qkvb = (qb, jnp.zeros_like(qb), vb)
+
+    def wrow(kind, start, size):
+        return cut(FRAME * kind + start, size)
+
+    w_half = lambda kind: wrow(kind, HALF * par, HALF)
+    w_extra = lambda kind: wrow(kind, 192 + EXTRA * par, EXTRA)
+
+    def wspan(kind):
+        return slice(FRAME * kind, FRAME * (kind + 1))
+
+    def take_frames(kind):
         slot = kind // 3
         held = h.holds(kind)
         gy, _ = h.block(kind, h.p)
@@ -441,48 +524,63 @@
                 ).wait_recv()
 
         @pl.when(held)
-        def _(kind=kind, slot=slot):
-            wt[kind, half_own] = join([rwa[slot, g, 0:HALF] for g in range(4)])
+        def _():
+            wt[w_half(kind)] = join([rwa[slot, g, 0:HALF] for g in range(4)])
 
         @pl.when(held & last)
-        def _(kind=kind, slot=slot):
-            wt[kind, extra_own] = join([rwa[slot, g, HALF : HALF + EXTRA] for g in range(4)])
+        def _():
+            wt[w_extra(kind)] = join([rwa[slot, g, HALF : HALF + EXTRA] for g in range(4)])
 
         @pl.when(jnp.logical_not(last))
-        def _(kind=kind):
-            wt[kind, 192:FRAME] = jnp.zeros((64, D), BF)
-
-        free = jnp.logical_not(held)
-        for d in (1, 2, 3):
-            comes = h.block(kind, h.p)[0] // 2 == lax.rem(h.y + 4 - d, 4)
-            for what, cond in ((half_own, None), (extra_own, last)):
+        def _():
+            wt[wrow(kind, 192, 64)] = jnp.zeros((64, D), BF)
+
+    by_y, by_z = {}, {}
+
+    chunks = lambda q: (
+        (HALF * q, 0, 64, None), (HALF * q + 64, 64, 32, None), (192 + EXTRA * q, HALF, EXTRA, last),
+    )
+
+    def pass_y(kind):
+        held = h.holds(kind)
+        for k, (start, _, size, cond) in enumerate(chunks(par)):
+            by_y[kind, k] = []
+            for d in (2, 1, 3):
+                comes = h.block(kind, h.p)[0] // 2 == lax.rem(h.y + 4 - d, 4)
                 s_if = held if cond is None else held & cond
                 r_if = comes if cond is None else comes & cond
-                ref = wt.at[kind, what]
-                by_y.setdefault(kind, []).append(
-                    net.send(ref, ref, ys[d - 1], send_if=s_if, recv_if=r_if)
-                )
-
-    by_z = {}
-
-    def pass_z(kind):
-        for c in by_y[kind]:
+                ref = wt.at[wrow(kind, start, size)]
+                by_y[kind, k].append(net.send(ref, ref, ys[d - 1], send_if=s_if, recv_if=r_if))
+
+    def pass_z(kind, k):
+        start, _, size, cond = chunks(par)[k]
+        for c in by_y[kind, k]:
             c.got()
-        for base, size, cond in ((HALF * par, 48, None), (192 + EXTRA * par, 16, last)):
-            for off, d in ((0, zm), (size, zp)):
-                ref = wt.at[kind, cut(base + off, size)]
-                by_z.setdefault(kind, []).append(net.send(ref, ref, d, send_if=cond, recv_if=cond))
-
+        for off, d in ((0, zm), (size // 2, zp)):
+            ref = wt.at[wrow(kind, start + off, size // 2)]
+            by_z.setdefault(kind, []).append(net.send(ref, ref, d, send_if=cond, recv_if=cond))
+
+    for kind in range(3):
+        take_frames(kind)
+        pass_y(kind)
     gather.ready(0)
     gather.ready(1)
     for kind in range(3):
-        pass_z(kind)
+        pass_z(kind, 0)
+    grds = by_gx(lambda g: grd.at[:, lanes_of(g)], lambda g: rg.at[g])
+    grd_own = pltpu.make_async_copy(grd.at[:, lanes_of(h.gx)], rg.at[h.gx], loc.at[3])
+    grd_own.start()
+    for k in (1, 2):
+        for kind in range(3):
+            pass_z(kind, k)
     gather.ready(2)
     gather.ready(3)
-
-    ff_own.wait()
+    take_frames(3)
+    pass_y(3)
+
     for c in ffs:
         c.got()
+        c.gone()
     fslab = lambda y, k: cut((2 * y + k) * FPAD, FPAD)
     mine_ff = fslab(h.y, par)
     fw[mine_ff] = join([rff[g] for g in range(4)])
@@ -497,35 +595,34 @@
             ref = fw.at[cut(base + off, size)]
             ff_z.append(net.send(ref, ref, to))
 
-    ff_pass(0)
-    for c in grds:
-        c.got()
-    gown[...] = join([rg[g] for g in range(4)])
-    ga[my_rows] = gown[...]
-    ggather = Gather(h, net, ga)
-    ggather.start()
-
     @pl.when(jnp.logical_not(alone))
     def _():
         push(segs, seg, ss.at[0], rseg.at[0], ys[0]).wait_recv()
 
-    begin = jnp.sum((seg[0:1] == 0).astype(F32), axis=1, keepdims=True).astype(jnp.int32)
+    begin = jnp.sum((seg[...] == 0).astype(F32), axis=1, keepdims=True).astype(jnp.int32)
     set_masks(masks, begin)
+    for c in grds:
+        c.got()
+    grd_own.wait()
+    ga[my_rows] = turn(rg)
+    ggather = Gather(h, net, ga)
+    ggather.start()
     for kind in range(3):
         for c in by_z[kind]:
             c.got()
+
+    ff_pass(0)
 
     @pl.loop(0, 4)
     def _(chip):
         span = cut(256 * chip, 256)
         for kind in range(3):
-            qkv[kind, span] = (nt(fs[span], wt[kind]) + qkvb[kind : kind + 1]).astype(BF)
+            qkv[kind, span] = (nt(fs[span], wt[wspan(kind)]) + qkvb[kind]).astype(BF)
 
     save = pltpu.make_async_copy(fs, saved, loc.at[1])
     save.start()
     for c in fsends:
         c.gone()
-    pass_z(3)
     ggather.ready(0)
     ggather.ready(1)
 
@@ -542,18 +639,19 @@
             att[256 * i : n, lanes] = join(outs).astype(BF)
 
     attend(0)
-    ff_pass(1)
-    ff_pass(3)
     ggather.ready(2)
     ggather.ready(3)
+    for k in range(3):
+        pass_z(3, k)
     attend(1)
-    ff_pass(2)
     save.wait()
     for c in by_z[3]:
         c.got()
 
     sa = Scatter(h, net, (a0, a1, a2, a3))
-    sa.run(lambda chip: nn(att[cut(256 * chip, 256)], wt[3]))
+    sa.run(lambda chip: nn(att[cut(256 * chip, 256)], wt[wspan(3)]))
+    ff_pass(1)
+    ff_pass(3)
     r = rows[...].astype(F32) + sa.result() + vecs[2:3]
     res[...] = r
     normed, _ = stats(r)
@@ -561,6 +659,7 @@
     fs[my_rows] = (normed * vecs[3:4] + vecs[4:5]).astype(BF)
     gather = Gather(h, net, fs)
     gather.start()
+    ff_pass(2)
     for c in ff_z + fgot:
         c.got()
     v0[...] = jnp.zeros_like(v0)
@@ -586,28 +685,31 @@
         return f
 
     sb = Scatter(h, net, (b0, b1, b2, b3))
-    sb.run(total(gpre, 0))
+    sb.begin(total(gpre, 0))
     for c in ff_y + ff_z:
         c.gone()
     sa = Scatter(h, net, (a0, a1, a2, a3))
     for j in range(4):
         sa.term(j, total(hid, 1))
-
-    @pl.loop(0, 4)
-    def _(y):
+    sb.relayed()
+
+    one = {}
+    for d in (2, 1, 3, 0):
+        y = lax.rem(h.y + d, 4)
         fw[fslab(y, 0)] = tn(gpre[y], fs[...]).astype(BF)
         fw[fslab(y, 1)] = tn(hid[y], ga[...]).astype(BF)
-
-    for y in range(4):
-        v0[2 + y : 3 + y, 1664 : 1664 + FPAD] = rows_of(gpre[y].astype(F32))
-    for d in (zm, zp):
-        pl.semaphore_signal(hz, inc=1, device_id=d, device_id_type=MESH)
+        base = (2 * y + 1 - par) * FPAD
+        land = yr.at[d - 1] if d else wx
+        one[d] = [
+            net.send(fw.at[cut(base + off, size)], land.at[pl.ds(off, size)], to)
+            for off, size, to in ((0, A_ROWS, zm), (A_ROWS, B_ROWS, zp))
+        ]
+
     load = pltpu.make_async_copy(saved, fs, loc.at[1])
     load.start()
-
     gs = sb.result()
     normed, inv = stats(res[...])
-    up = gown[...].astype(F32)
+    up = ga[my_rows].astype(F32)
     gres = up + norm_back(gs, vecs[3:4], normed, inv)
     gsave[...] = gres
     low = gres.astype(BF)
@@ -618,29 +720,25 @@
     v0[3:4, 0:D] = rows_of(gs)
     v0[4:5, 0:D] = rows_of(low.astype(F32))
     v0[5:6, 0:D] = rows_of(up)
-
-    pl.semaphore_wait(hz, 2)
-    one = {}
-    for d in (2, 1, 3, 0):
-        y = lax.rem(h.y + d, 4)
-        base = (2 * y + 1 - par) * FPAD
-        one[d] = [
-            net.send(fw.at[cut(base + off, size)], ga.at[cut(FPAD * y + off, size)], to)
-            for off, size, to in ((0, A_ROWS, zm), (A_ROWS, B_ROWS, zp))
-        ]
+    for d in ys:
+        pl.semaphore_signal(hz, inc=1, device_id=d, device_id_type=MESH)
+    gather.ready(0)
+    gather.ready(1)
+    for y in range(4):
+        v0[2 + y : 3 + y, 1664 : 1664 + FPAD] = rows_of(gpre[y].astype(F32))
 
     for s in range(4):
-        chip = gather.ready(s)
-        span = cut(256 * chip, 256)
-        gat[span] = nt(ba[span], wt[3]).astype(BF)
-    for j in (1, 2):
-        if j == 1:
-            sa.first()
-        sa.side(j)
+        if s > 1:
+            gather.ready(s)
+        span = cut(256 * gather.chip(s), 256)
+        gat[span] = nt(ba[span], wt[wspan(3)]).astype(BF)
+    sa.first()
+    sa.side(1)
+    sa.side(2)
     for kind in range(4):
-        for c in by_y[kind] + by_z[kind]:
+        for c in by_y[kind, 0] + by_y[kind, 1] + by_y[kind, 2] + by_z[kind]:
             c.gone()
-    wt[3] = tn(att[...], ba[...]).astype(BF)
+    wt[wspan(3)] = tn(att[...], ba[...]).astype(BF)
     for d in (zm, zp):
         pl.semaphore_signal(hb, inc=1, device_id=d, device_id_type=MESH)
 
@@ -651,9 +749,10 @@
             c.got()
         y = lax.rem(h.y + d, 4)
         span = fslab(y, par)
-        fw[span] = (fw[span].astype(F32) + ga[cut(FPAD * y, FPAD)].astype(F32)).astype(BF)
+        other = yr[d - 1, 0:FPAD] if d else wx[0:FPAD]
+        fw[span] = (fw[span].astype(F32) + other.astype(F32)).astype(BF)
         if d:
-            two[d] = net.send(fw.at[span], yr.at[d - 1, pl.ds(0, FPAD)], ys[d - 1])
+            two[d] = net.send(fw.at[span], ga.at[pl.ds(FPAD * (d - 1), FPAD)], ys[d - 1])
 
     def attend_back(pair):
         lanes = pl.ds(128 * pair, 128)
@@ -680,113 +779,134 @@
         qkv[1, :, lanes] = dk[...].astype(BF)
         qkv[2, :, lanes] = dv[...].astype(BF)
 
-    attend_back(0)
-    sa.relayed()
+    pl.semaphore_wait(hz, 3)
     collect(2)
     collect(1)
-    attend_back(1)
+    sa.relayed()
+    attend_back(0)
     collect(3)
     collect(0)
-
-    for c in toks:
-        c.gone()
-    out = (res[...] + sa.result() + vecs[5:6]).astype(BF)
-    for g in range(4):
-        rt[g] = out[:, QUARTER * g : QUARTER * (g + 1)]
-    by_gx(rt, layer_out)
-    lo_own = pltpu.make_async_copy(rt.at[h.gx], layer_out.at[h.gx], loc.at[2])
+    pl.semaphore_signal(ho, inc=1, device_id=zo, device_id_type=MESH)
+    for d in ys:
+        pl.semaphore_signal(hy, inc=1, device_id=d, device_id_type=MESH)
+
+    def turn_back(v, dst):
+        t = jnp.transpose(v.astype(BF))
+        for g in range(4):
+            dst[g] = t[QUARTER * g : QUARTER * (g + 1)]
+
+    turn_back(res[...] + sa.result() + vecs[5:6], rt)
+    by_gx(lambda g: rt.at[g], lambda g: layer_out.at[:, lanes_of(g)])
+    lo_own = pltpu.make_async_copy(rt.at[h.gx], layer_out.at[:, lanes_of(h.gx)], loc.at[2])
     lo_own.start()
 
-    sb = Scatter(h, net, (b0, b1, b2, b3))
-    sb.run(lambda chip: sum(nn(qkv[k, cut(256 * chip, 256)], wt[k]) for k in range(3)))
+    def dw(kind):
+        return wt if kind == 3 else a0
+
+    wone = {}
+
+    def send_one(kind, k):
+        start, at, size, cond = chunks(1 - par)[k]
+        half = size // 2
+        wone[kind, k] = [
+            net.send(
+                dw(kind).at[wrow(kind, start + half * i, half)],
+                ba.at[pl.ds(128 * kind + at + half * i, half)], to, send_if=cond, recv_if=cond,
+            )
+            for i, to in ((0, zm), (1, zp))
+        ]
+
+    pl.semaphore_wait(hb, 2)
+    for k in range(3):
+        send_one(3, k)
+    attend_back(1)
     load.wait()
 
     @pl.loop(0, 3)
     def _(kind):
-        wt[kind] = tn(qkv[kind], fs[...]).astype(BF)
-
-    pl.semaphore_wait(hb, 2)
-    wone = {}
-    for kind in (3, 0, 1, 2):
-        for base, at, size, cond in (
-            (HALF * (1 - par), 0, 48, None), (192 + EXTRA * (1 - par), HALF, 16, last),
-        ):
-            for k, to in ((0, zm), (1, zp)):
-                wone.setdefault(kind, []).append(
-                    net.send(
-                        wt.at[kind, cut(base + size * k, size)],
-                        ba.at[pl.ds(128 * kind + at + size * k, size)], to, send_if=cond, recv_if=cond,
-                    )
+        a0[cut(FRAME * kind, FRAME)] = tn(qkv[kind], fs[...]).astype(BF)
+
+    for k in range(3):
+        for kind in range(3):
+            send_one(kind, k)
+    sb = Scatter(h, net, (b0, b1, b2, b3))
+    sb.begin(lambda chip: sum(nn(qkv[k, cut(256 * chip, 256)], wt[wspan(k)]) for k in range(3)))
+
+    wtwo = {}
+
+    def send_two(kind, k):
+        slot, held = kind // 3, h.holds(kind)
+        home = h.block(kind, h.p)[0] // 2
+        start, at, size, cond = chunks(par)[k]
+        mine = wrow(kind, start, size)
+        for c in wone[kind, k]:
+            c.got()
+
+        def add():
+            ref = dw(kind)
+            s = ref[mine].astype(F32) + ba[128 * kind + at : 128 * kind + at + size].astype(F32)
+            ref[mine] = s.astype(BF)
+
+        if cond is None:
+            add()
+        else:
+            pl.when(cond)(add)
+        for d in (2, 1, 3):
+            goes, comes = lax.rem(h.y + d, 4) == home, held
+            if cond is not None:
+                goes, comes = goes & cond, comes & cond
+            wtwo.setdefault(kind, []).append(
+                net.send(
+                    dw(kind).at[mine], yr.at[d - 1, pl.ds(128 * slot + at, size)], ys[d - 1],
+                    send_if=goes, recv_if=comes,
                 )
+            )
+
+    pl.semaphore_wait(hy, 3)
+    for k in range(3):
+        send_two(3, k)
+    for kind in range(3):
+        send_two(kind, 0)
+    sb.relayed()
+    for k in (1, 2):
+        for kind in range(3):
+            send_two(kind, k)
     v0[0:1, 1664:VW] = rows_of(qkv[0].astype(F32))
     v0[1:2, 1664:VW] = rows_of(qkv[2].astype(F32))
 
     s = fw[fslab(h.y, par)].astype(F32)
     for d in (1, 2, 3):
         two[d].got()
-        s = s + yr[d - 1, 0:FPAD].astype(F32)
+        s = s + ga[FPAD * (d - 1) : FPAD * d].astype(F32)
     s2[0:FPAD] = s.astype(BF)
-    for d in ys:
-        pl.semaphore_signal(hy, inc=1, device_id=d, device_id_type=MESH)
-    three = net.send(s2.at[pl.ds(0, FPAD)], x2, zo)
+    pl.semaphore_wait(ho, 1)
+    three = net.send(s2.at[pl.ds(0, FPAD)], wx.at[pl.ds(0, FPAD)], zo)
 
     gf = sb.result()
     normed, inv = stats(rows[...].astype(F32))
-    low = (gsave[...] + norm_back(gf, vecs[0:1], normed, inv)).astype(BF)
+    low = gsave[...] + norm_back(gf, vecs[0:1], normed, inv)
     v0[0:1, 0:D] = rows_of(gf * normed)
     v0[1:2, 0:D] = rows_of(gf)
     for c in grds:
         c.gone()
-    for g in range(4):
-        rg[g] = low[:, QUARTER * g : QUARTER * (g + 1)]
-    igs = by_gx(rg, igot)
-    igot[h.gx] = rg[h.gx]
+    turn_back(low, rg)
+    by_gx(lambda g: rg.at[g], lambda g: input_grad.at[:, lanes_of(g)])
+    ig_own = pltpu.make_async_copy(rg.at[h.gx], input_grad.at[:, lanes_of(h.gx)], loc.at[0])
+    ig_own.start()
     vys = [net.send(v0, vy.at[h.y], d) for d in ys]
     vy[h.y] = v0[...]
 
     three.got()
-    full = (s2[0:FPAD].astype(F32) + x2[...].astype(F32)).astype(BF)
-    for c in ffs:
-        c.gone()
+    full = (s2[0:FPAD].astype(F32) + wx[0:FPAD].astype(F32)).astype(BF)
+    pl.semaphore_signal(ho, inc=1, device_id=zo, device_id_type=MESH)
     for g in range(4):
         rff[g] = full[:, QUARTER * g : QUARTER * (g + 1)]
-    four = [net.send(rff.at[h.gx ^ d], ffo.at[par, h.gx], h.gxd(d)) for d in (1, 2, 3)]
+    four = by_gx(lambda g: rff.at[g], lambda g: ffo.at[par, g])
     ffo_own = pltpu.make_async_copy(rff.at[h.gx], ffo.at[par, h.gx], loc.at[3])
     ffo_own.start()
     three.gone()
 
-    pl.semaphore_wait(hy, 3)
-    wtwo = {}
-    spans = ((half_own, 0, HALF, None), (extra_own, HALF, EXTRA, last))
-    for kind in range(4):
-        slot, held = kind // 3, h.holds(kind)
-        home = h.block(kind, h.p)[0] // 2
-        for c in wone[kind]:
-            c.got()
-        for mine, at, size, cond in spans:
-
-            def add(mine=mine, at=at, size=size, kind=kind):
-                s = wt[kind, mine].astype(F32) + ba[128 * kind + at : 128 * kind + at + size].astype(F32)
-                wt[kind, mine] = s.astype(BF)
-
-            if cond is None:
-                add()
-            else:
-                pl.when(cond)(add)
-            for d in (1, 2, 3):
-                goes, comes = lax.rem(h.y + d, 4) == home, held
-                if cond is not None:
-                    goes, comes = goes & cond, comes & cond
-                wtwo.setdefault(kind, []).append(
-                    net.send(
-                        wt.at[kind, mine], yr.at[d - 1, pl.ds(128 * slot + at, size)], ys[d - 1],
-                        send_if=goes, recv_if=comes,
-                    )
-                )
-
-    for c in igs:
-        c.got()
-    input_grad[...] = igot[...].astype(F32)
+    spans = ((HALF * par, half_own, 0, HALF, None), (192 + EXTRA * par, extra_own, HALF, EXTRA, last))
     for c in vys:
         c.got()
     vz[h.z] = (vy[0] + vy[1]) + (vy[2] + vy[3])
@@ -795,22 +915,24 @@
     ffo_own.wait()
     for c in four:
         c.got()
+    five = []
     for at, size, to in ((0, A_ROWS, zm), (A_ROWS, B_ROWS, zp)):
         ref = ffo.at[par, :, pl.ds(at, size)]
-        net.send(ref, ref, to)
-
+        five.append(net.send(ref, ref, to))
+
+    pl.semaphore_wait(ho, 1)
     wthree = {}
     for kind in range(4):
         slot, held = kind // 3, h.holds(kind)
         for c in wtwo[kind]:
             c.got()
-        for mine, at, size, cond in spans:
+        for start, _, at, size, cond in spans:
             ok = held if cond is None else held & cond
             low_at = 128 * slot + at
 
             @pl.when(ok)
-            def _(kind=kind, mine=mine, size=size, low_at=low_at):
-                s = wt[kind, mine].astype(F32)
+            def _(kind=kind, start=start, size=size, low_at=low_at):
+                s = dw(kind)[wrow(kind, start, size)].astype(F32)
                 for d in range(3):
                     s = s + yr[d, low_at : low_at + size].astype(F32)
                 s2[low_at : low_at + size] = s.astype(BF)
@@ -833,7 +955,7 @@
         xh, xht, yt = lax.rem(gy, 2), lax.rem(gyt, 2), gyt // 2
         for c in wthree[kind]:
             c.got()
-        for mine, at, size, cond in spans:
+        for _, mine, at, size, cond in spans:
             ok = held if cond is None else held & cond
             low_at = 128 * slot + at
 
@@ -906,69 +1028,93 @@
                 )
             )
 
+    for c in four + five:
+        c.got()
+        c.gone()
+    for k, dst in ((0, gfc), (1, got_)):
+        fetch = pltpu.make_async_copy(ffo.at[k], rff, loc.at[3])
+        fetch.start()
+        fetch.wait()
+        for g in range(4):
+            t32[SUB * g : SUB * (g + 1)] = rff[g].astype(F32)[0:SUB]
+        if k:
+            out_copy.wait()
+        stage[...] = jnp.transpose(t32[...]).astype(BF)
+        out_copy = pltpu.make_async_copy(stage, dst, loc.at[1])
+        out_copy.start()
+
+    out_copy.wait()
     for c in vxs:
         c.got()
     total_v = vx[0]
     for p in range(1, 8):
         total_v = total_v + vx[p]
-    vsum[...] = total_v[:, 0:D]
-    qf[...] = vx[:, :, 1664:VW]
+    vsum[...] = pick([total_v[:, QUARTER * g : QUARTER * (g + 1)] for g in range(4)], h.gx)
+    for k in (0, 1):
+        parts = [vx[p, k : k + 1, 1664 : 1664 + (FRAME if p == 7 else 192)] for p in range(8)]
+        qsum[k : k + 1] = join(parts)
+    fsum[...] = join([vx[4 * h.xh + g, pl.ds(2 + h.y, 1), 1664 : 1664 + SUB] for g in range(4)])
     for i in range(4):
         p, _ = h.unit(i)
         for c in wfive[i]:
             c.got()
-        scr[0:FRAME] = frames[i].astype(F32)
+        scr[0:FRAME, 0:QUARTER] = frames[i].astype(F32)
 
         @pl.when(p < 7)
         def _(i=i):
-            scr[192 : 192 + TAIL] = tl[i].astype(F32)
-
-        wao[i] = scr[pl.ds(pl.multiple_of(8 * p, 8), SUB)].astype(BF)
-
+            scr[192 : 192 + TAIL, 0:QUARTER] = tl[i].astype(F32)
+
+        t32[SUB * i : SUB * (i + 1)] = scr[pl.ds(pl.multiple_of(8 * p, 8), SUB), 0:QUARTER]
+    stage[...] = jnp.transpose(t32[...]).astype(BF)
+    out_copy = pltpu.make_async_copy(stage, gwa, loc.at[1])
+    out_copy.start()
+    out_copy.wait()
     lo_own.wait()
+    ig_own.wait()
     net.finish()
 
 
-def layer(segs, tok, grd, wa, ff, vec, qkvb, fcb):
+def layer(segs, tok, grd, wq, wp, fcw, otw, vec, bias):
     any_ = pl.BlockSpec(memory_space=pl.ANY)
     scratch = [
         pltpu.VMEM((SEQ, D), BF),
         pltpu.VMEM((SEQ, D), BF),
         pltpu.VMEM((SEQ, D), BF),
-        pltpu.VMEM((4, FRAME, D), BF),
+        pltpu.VMEM((SEQ, D), BF),
         pltpu.VMEM((8 * FPAD, D), BF),
         pltpu.VMEM((3, SEQ, FRAME), BF),
         pltpu.VMEM((SEQ, FRAME), BF),
         pltpu.VMEM((SEQ, FRAME), BF),
-        pltpu.VMEM((2560, 256), F32),
+        pltpu.VMEM((2560, 256), BF),
         pltpu.VMEM((4, SEQ, FPAD), BF),
         pltpu.VMEM((4, SEQ, FPAD), BF),
         pltpu.VMEM((SEQ, 2 * HEAD_DIM), F32),
         pltpu.VMEM((SEQ, 2 * HEAD_DIM), F32),
         *Scatter.scratch(),
         *Scatter.scratch(),
-        pltpu.VMEM((4, ROWS, QUARTER), BF),
-        pltpu.VMEM((4, ROWS, QUARTER), BF),
+        pltpu.VMEM((4, QUARTER, ROWS), BF),
+        pltpu.VMEM((4, QUARTER, ROWS), BF),
         pltpu.VMEM((2, 4, HALF + EXTRA, QUARTER), BF),
         pltpu.VMEM((4, FPAD, QUARTER), BF),
         pltpu.VMEM((4, FRAME, QUARTER), BF),
         pltpu.VMEM((2, TAIL, QUARTER), BF),
         pltpu.VMEM((2, TAIL, QUARTER), BF),
         pltpu.VMEM((336, QUARTER), F32),
+        pltpu.VMEM((4 * SUB, QUARTER), F32),
+        pltpu.VMEM((QUARTER, 4 * SUB), BF),
+        pltpu.VMEM((4, FPAD, QUARTER), BF),
         pltpu.VMEM((4, 8, QUARTER), F32),
         pltpu.VMEM((8, D), F32),
-        pltpu.VMEM((8, 128), jnp.int32),
+        pltpu.VMEM((1, 128), jnp.int32),
+        pltpu.VMEM((8, FPAD), F32),
         pltpu.VMEM((4, 8, FPAD), F32),
         pltpu.VMEM((ROWS, D), F32),
         pltpu.VMEM((ROWS, D), F32),
         pltpu.VMEM((ROWS, D), BF),
-        pltpu.VMEM((ROWS, D), BF),
         pltpu.VMEM((3, FRAME, D), BF),
-        pltpu.VMEM((FPAD, D), BF),
         pltpu.VMEM((FRAME, D), BF),
         pltpu.VMEM((FRAME, D), BF),
         pltpu.VMEM((4, TAIL, QUARTER), BF),
-        pltpu.VMEM((4, ROWS, QUARTER), BF),
         pltpu.VMEM((8, VW), F32),
         pltpu.VMEM((4, 8, VW), F32),
         pltpu.VMEM((4, 8, VW), F32),
@@ -985,82 +1131,60 @@
         pltpu.SemaphoreType.REGULAR,
         pltpu.SemaphoreType.REGULAR,
         pltpu.SemaphoreType.REGULAR,
+        pltpu.SemaphoreType.REGULAR,
     ]
     return pl.pallas_call(
         layer_kernel,
         out_shape=[
-            jax.ShapeDtypeStruct((4, ROWS, QUARTER), BF),
-            jax.ShapeDtypeStruct((4, ROWS, QUARTER), F32),
+            jax.ShapeDtypeStruct((QUARTER, 4 * ROWS), BF),
+            jax.ShapeDtypeStruct((QUARTER, 4 * ROWS), BF),
+            jax.ShapeDtypeStruct((QUARTER, 4 * SUB), BF),
+            jax.ShapeDtypeStruct((QUARTER, 4 * SUB), BF),
+            jax.ShapeDtypeStruct((QUARTER, 4 * SUB), BF),
+            jax.ShapeDtypeStruct((8, QUARTER), F32),
+            jax.ShapeDtypeStruct((2, D), F32),
+            jax.ShapeDtypeStruct((1, 4 * SUB), F32),
             jax.ShapeDtypeStruct((2, 4, FPAD, QUARTER), BF),
-            jax.ShapeDtypeStruct((4, SUB, QUARTER), BF),
-            jax.ShapeDtypeStruct((8, D), F32),
-            jax.ShapeDtypeStruct((8, 8, 256), F32),
             jax.ShapeDtypeStruct((SEQ, D), BF),
         ],
-        in_specs=[VMEM, VMEM, VMEM, VMEM, any_, VMEM, VMEM, VMEM],
-        out_specs=[any_, VMEM, any_, VMEM, VMEM, VMEM, any_],
+        in_specs=[VMEM, any_, any_, VMEM, VMEM, any_, any_, VMEM, VMEM],
+        out_specs=[any_, any_, any_, any_, any_, VMEM, VMEM, VMEM, any_, any_],
         scratch_shapes=scratch,
         compiler_params=pltpu.CompilerParams(
             collective_id=0, has_side_effects=True, vmem_limit_bytes=64 * 2**20 - 2**16
         ),
         name="layer",
-    )(segs, tok, grd, wa, ff, vec, qkvb, fcb)
+    )(segs, tok, grd, wq, wp, fcw, otw, vec, bias)
 
 
 def per_device(
     tokens_in, segments, norm1_gain, norm1_bias, qkv_weight, query_bias, value_bias, proj_weight,
     proj_bias, norm2_gain, norm2_bias, fc_weight, fc_bias, out_weight, out_bias, out_grad,
 ):
-    gx, gy = lax.axis_index("gx"), lax.axis_index("gy")
-    y, xh = gy // 2, lax.rem(gy, 2)
-    p = xh * 4 + gx
-    wa = jnp.concatenate([qkv_weight.T.reshape(3, SUB, QUARTER), proj_weight.T[None]])
-    ff = jnp.stack(
-        [fc_weight.T.reshape(4, SUB, QUARTER), out_weight.T.reshape(4, SUB, QUARTER)], axis=1
-    )
-    ff = jnp.pad(ff, ((0, 0), (0, 0), (0, FPAD - SUB), (0, 0)))
     zero = jnp.zeros_like(norm1_gain)
     vec = jnp.stack(
         [norm1_gain, norm1_bias, proj_bias, norm2_gain, norm2_bias, out_bias, zero, zero]
     )
-    valid = (jnp.arange(FRAME) < 192) | (p == 7)
-    qb = jnp.where(valid, lax.dynamic_slice_in_dim(query_bias, 192 * p, FRAME), 0.0)
-    vb = jnp.where(valid, lax.dynamic_slice_in_dim(value_bias, 192 * p, FRAME), 0.0)
-    nil = jnp.zeros_like(qb)
-    qkvb = jnp.stack([qb, nil, vb, nil, nil, nil, nil, nil])
-    fcb = jnp.pad(lax.dynamic_slice_in_dim(fc_bias, SUB * gx, SUB), (0, FPAD - SUB))
-    fcb = jnp.broadcast_to(fcb, (8, FPAD))
-    layer_out, input_grad, ffo, wao, vsum, qf, _ = layer(
-        jnp.broadcast_to(segments, (8, ROWS)),
-        tokens_in.reshape(4, ROWS, QUARTER), out_grad.reshape(4, ROWS, QUARTER),
-        wa, ff, vec, qkvb, fcb,
+    bias = jnp.stack([query_bias, value_bias, jnp.pad(fc_bias, (0, D - 4 * SUB))])
+    layer_out, input_grad, gwa, gfc, got, vsum, qsum, fsum, _, _ = layer(
+        segments, tokens_in.T, out_grad.T, qkv_weight, proj_weight, fc_weight, out_weight, vec, bias
     )
-    mine = lax.dynamic_slice_in_dim(vsum, QUARTER * gx, QUARTER, 1)
-
-    def heads(v):
-        return jnp.concatenate([v[:, :192].reshape(8 * 192), v[7, 192:]])
-
-    fcp = lax.dynamic_slice(qf, (4 * xh, 2 + y, 0), (4, 1, SUB)).reshape(4 * SUB)
-
-    def whole(v):
-        return v[:, :SUB].reshape(4 * SUB, QUARTER).T.astype(F32)
-
     return (
-        layer_out.reshape(4 * ROWS, QUARTER),
-        input_grad.reshape(4 * ROWS, QUARTER),
-        mine[0],
-        mine[1],
-        wao[0:3].reshape(3 * SUB, QUARTER).T.astype(F32),
-        heads(qf[:, 0]),
-        heads(qf[:, 1]),
-        wao[3].T.astype(F32),
-        mine[4],
-        mine[2],
-        mine[3],
-        whole(ffo[0]),
-        fcp,
-        whole(ffo[1]),
-        mine[5],
+        layer_out.T,
+        input_grad.T.astype(F32),
+        vsum[0],
+        vsum[1],
+        gwa[:, : 3 * SUB].astype(F32),
+        qsum[0],
+        qsum[1],
+        gwa[:, 3 * SUB :].astype(F32),
+        vsum[4],
+        vsum[2],
+        vsum[3],
+        gfc.astype(F32),
+        fsum[0],
+        got.astype(F32),
+        vsum[5],
     )
 
 

time: 344 us -> 318 us (0.924)
  Pallas kernels: 311 us -> 295 us
  local copies, waits for them, and re-layouts: 20.9 us -> 7.24 us
  other arithmetic: 5.25 us -> 9.23 us
    pallas_call x1, Pallas kernels: 311 us -> 295 us  [layer(): pl.pallas_call(layer_kernel, out_shape=[jax.ShapeDtypeStruct((QUARTER, 4...]
    convert_element_type x4 -> x5, other arithmetic: 0.76 us -> 7.27 us  [the longest x1 2.06 us: per_device(): gwa[:, :3 * SUB].astype(F32)]
    convert_element_type x3 -> x0, local copies, waits for them, and re-layouts: 4.55 us -> none  [the longest x2 3.22 us: whole(): return v[:, :SUB].reshape(4 * SUB, QUARTER).T.astype(F32)]
    unnamed x38 -> x9, local copies, waits for them, and re-layouts: 5.27 us -> 0.77 us
where the time goes in v3:
time: 318 us; the launch traced here: 312 us
  Pallas kernels  295 us (93%)
  other arithmetic  9.23 us (3%)
  local copies, waits for them, and re-layouts  7.24 us (2%)
    pallas_call x1, Pallas kernels, layer(): pl.pallas_call(layer_kernel, out_shape=[jax.ShapeDtypeStruct((QUARTER, 4...  295 us

profile of v3, /device:TPU:27, one launch (start us, length us, event | category | flops | bytes accessed | tf_op | source)
XLA Modules:
  0.0 311.9 jit_solution(2384745878770779447)
XLA Ops:
  0.6 0.7 stack.44
  1.3 0.7 stack.45
  2.0 0.7 pad.4
  2.7 0.6 pad_maximum_fusion.bias
  3.4 1.4 stack.43.vec
  4.8 294.6 %layer.1 = (bf16[400,512]{1,0:T(8,128)(2,1)}, bf16[400,512]{1,0:T(8,128)(2,1)}, bf16[400,800]{1,0:T(8,128)(2,1)}, bf16[400,800]{1,0:T(8,128)(2,1)}, bf16[400,800...) custom-call(s32[1,128]{1,0:T(1,128)} %segs.1, ...), custom_call_target="tpu_custom_call" | custom-call | tf_op jit(solution)/shard_map/layer/pallas_call | solution.py:1136
  299.4 0.0 copy-start.3
  299.4 1.3 reduce.2
  300.7 1.5 fusion
  302.3 0.0 copy-start.1
  302.3 1.4 slice_reduce_fusion
  303.7 1.8 slice_convert_fusion.1
  305.5 2.1 slice_convert_fusion
  307.6 0.0 copy-done.3
  307.6 0.0 copy-start
  307.6 1.0 convert_bitcast_fusion
  308.6 0.0 copy-done.1
  308.6 0.0 copy-start.2
  308.6 1.2 convert_element_type.24
  309.8 0.0 copy-done
  309.8 1.2 convert_element_type.25
  311.0 0.0 copy-done.2
  311.0 0.8 copy.32
  (2 shorter events, 0.0 us)
Async XLA Ops:
  299.4 8.2 %copy-start.3 = (bf16[400,512]{1,0:T(8,128)(2,1)S(1)}, bf16[400,512]{1,0:T(8,128)(2,1)}, u32[]{:S(2)}) copy-start(bf16[400,512]{1,0:T(8,128)(2,1)} %get-tuple-element.24) | copy-start | bytes 1228804
  302.3 6.3 %copy-start.1 = (bf16[400,800]{1,0:T(8,128)(2,1)S(1)}, bf16[400,800]{1,0:T(8,128)(2,1)}, u32[]{:S(2)}) copy-start(bf16[400,800]{1,0:T(8,128)(2,1)} %get-tuple-element.28) | copy-start | bytes 1920004
  307.6 2.2 copy-start
  308.6 2.4 copy-start.2

commit v4 on v3

--- a/solution.py
+++ b/solution.py
@@ -172,8 +172,11 @@
     def row(self, dx):
         return (lax.rem(self.h.x + 4 + dx, 4) * 2 + self.h.c) * ROWS
 
+    def ref(self, dx, half):
+        return self.buf.at[cut(self.row(dx), ROWS) if half is None else cut(self.row(dx) + 64 * half, 64)]
+
     def go(self, dx, d, half=None):
-        ref = self.buf.at[cut(self.row(dx), ROWS) if half is None else cut(self.row(dx) + 64 * half, 64)]
+        ref = self.ref(dx, half)
         return self.net.send(ref, ref, d)
 
     def start(self):
@@ -184,6 +187,14 @@
         self.r[1] = self.go(0, self.right, 1)
         self.l[0] = self.go(0, self.left, 0)
         self.own = self.go(0, self.sib)
+        self.rr = None
+
+    def relays(self):
+        if self.rr is None:
+            self.r[0].got()
+            self.rr = self.go(-1, self.right, 0)
+            self.l[1].got()
+            self.ll = self.go(1, self.left, 1)
 
     def chip(self, s):
         return lax.rem(self.h.x + (0, 3, 1, 2)[s], 4)
@@ -194,10 +205,7 @@
             self.own.got()
             return h.x
         if s == 1:
-            self.r[0].got()
-            self.rr = self.go(-1, self.right, 0)
-            self.l[1].got()
-            self.ll = self.go(1, self.left, 1)
+            self.relays()
             self.r[1].got()
             self.f1 = self.go(-1, self.sib)
             self.l[0].got()
@@ -218,6 +226,20 @@
         return lax.rem(h.x + 2, 4)
 
 
+def raw_at(p, half=None):
+    rows, lanes = QUARTER * (p // 3), 512 * (p % 3 if isinstance(p, int) else lax.rem(p, 3))
+    if isinstance(p, int):
+        return slice(rows, rows + QUARTER), slice(lanes, lanes + 512)
+    if half is None:
+        return cut(rows, QUARTER), pl.ds(pl.multiple_of(lanes, 256), 512)
+    return cut(rows, QUARTER), pl.ds(pl.multiple_of(lanes + 256 * half, 256), 256)
+
+
+class RawGather(Gather):
+    def ref(self, dx, half):
+        return self.buf.at[raw_at(lax.rem(self.h.x + 4 + dx, 4) * 2 + self.h.c, half)]
+
+
 class Scatter:
     @staticmethod
     def scratch():
@@ -333,16 +355,16 @@
 
 
 def layer_kernel(
-    segs, tok, grd, wq, wp, fcw, otw, vec, bias,
-    layer_out, input_grad, gwa, gfc, got_, vsum, qsum, fsum, ffo, saved,
+    segs, tok, grd, wq, wp, fcw, otw, g1, c1, pb, g2, c2, ob, qbias, vbias, fbias,
+    layer_out, input_grad, gwa, gfc, got_, small, ffo, saved,
     *refs,
 ):
     (
         fs, ga, ba, wt, fw, qkv, att, gat, masks, hid, gpre, dk, dv,
         a0, a1, a2, a3, b0, b1, b2, b3,
-        rt, rg, rwa, rff, frames, tsend, trecv, scr, t32, stage, fbuf, rv, vecs, seg, fcb, fcbs,
+        rt, rg, vec, rwa, rff, frames, tsend, trecv, scr, t32, stage, fbuf, rv, vecs, seg, fcb, fcbs,
         res, gsave, rows, yr, s2, wx, tl, v0, vy, vz, vx,
-        ss, rs, rsw, rsx, rseg, rsm, rsn, rst, loc, hz, hb, hy, ho,
+        ss, rs, rsw, rsx, rseg, rsm, rsn, rst, loc, hz, hb, hy, ho, hx,
     ) = refs
     h = Here()
     net = Net(ss, rs)
@@ -364,6 +386,12 @@
     def _():
         pltpu.make_async_copy(otw, stage, loc.at[0]).start()
 
+    mine_raw = fw.at[raw_at(h.p)]
+    tok_own = pltpu.make_async_copy(tok, mine_raw, loc.at[2])
+    tok_own.start()
+    vec[...] = jnp.concatenate(
+        [v[...].reshape(1, QUARTER) for v in (g1, c1, pb, g2, c2, ob)] + [jnp.zeros((2, QUARTER), F32)], axis=0
+    )
     t32[0 : 3 * SUB] = jnp.transpose(wq[...]).astype(F32)
     t32[3 * SUB : 4 * SUB] = jnp.transpose(wp[...]).astype(F32)
 
@@ -407,6 +435,20 @@
 
     for i in (1, 2):
         frame(i, sub_tail(i - 1))
+
+    @pl.when(par == 0)
+    def _():
+        pltpu.make_async_copy(fcw, stage, loc.at[0]).wait()
+
+    @pl.when(par == 1)
+    def _():
+        pltpu.make_async_copy(otw, stage, loc.at[0]).wait()
+
+    turned = jnp.transpose(stage[...]).astype(F32)
+    blank = jnp.zeros((FPAD - SUB, QUARTER), F32)
+    for g in range(4):
+        fbuf[g] = jnp.concatenate([turned[SUB * g : SUB * (g + 1)], blank], axis=0).astype(BF)
+    tok_own.wait()
     pl.semaphore_wait(barrier, len(everyone))
 
     tail = net.send(tsend, trecv, (h.z, h.gx, lax.rem(h.gy + 1, 8)))
@@ -417,12 +459,11 @@
     def by_gx(src, dst):
         return [net.send(src(h.gx ^ d), dst(h.gx), h.gxd(d)) for d in (1, 2, 3)]
 
-    toks = by_gx(lambda g: tok.at[:, lanes_of(g)], lambda g: rt.at[g])
     for i in (1, 2):
         send_frame(i)
+    gather = RawGather(h, net, fw)
+    gather.start()
     vgot = [net.send(vec, rv.at[h.gx], h.gxd(d)) for d in (1, 2, 3)]
-    tok_own = pltpu.make_async_copy(tok.at[:, lanes_of(h.gx)], rt.at[h.gx], loc.at[2])
-    tok_own.start()
     rv[h.gx] = vec[...]
     at_zero = h.gy == 0
     alone = at_zero & (h.gx == 0)
@@ -441,54 +482,27 @@
             out = jnp.where(index == k + 1, v, out)
         return out
 
-    for c in vgot:
-        c.got()
-    vecs[...] = join([rv[g] for g in range(4)])
-    for c in toks:
-        c.got()
-    tok_own.wait()
-
-    def turn(ref):
-        return jnp.transpose(jnp.concatenate([ref[g] for g in range(4)], axis=0))
-
-    x = turn(rt)
-    rows[...] = x
-    normed, _ = stats(x.astype(F32))
-    my_rows = cut(ROWS * h.p, ROWS)
-    fs[my_rows] = (normed * vecs[0:1] + vecs[1:2]).astype(BF)
     tail.got()
     for i in (0, 3):
         frame(i, trecv[i // 3].astype(F32))
         send_frame(i)
 
-    gather = Gather(h, net, fs)
-    gather.start()
-
-    @pl.when(par == 0)
-    def _():
-        pltpu.make_async_copy(fcw, stage, loc.at[0]).wait()
-
-    @pl.when(par == 1)
-    def _():
-        pltpu.make_async_copy(otw, stage, loc.at[0]).wait()
-
-    t32[...] = jnp.transpose(stage[...]).astype(F32)
-    blank = jnp.zeros((FPAD - SUB, QUARTER), F32)
-    for g in range(4):
-        fbuf[g] = jnp.concatenate([t32[SUB * g : SUB * (g + 1)], blank], axis=0).astype(BF)
-    ffs = by_gx(lambda g: fbuf.at[g], lambda g: rff.at[g])
-    rff[h.gx] = fbuf[h.gx]
-
-    low_bias = pick([bias[2:3, SUB * g : SUB * (g + 1)] for g in range(4)], h.gx)
+    my_rows = cut(ROWS * h.p, ROWS)
+
+    def turn(ref):
+        return jnp.transpose(jnp.concatenate([ref[g] for g in range(4)], axis=0))
+
+    fbias1 = fbias[...].reshape(1, 4 * SUB)
+    low_bias = pick([fbias1[:, SUB * g : SUB * (g + 1)] for g in range(4)], h.gx)
     fcb[...] = jnp.broadcast_to(join([low_bias, jnp.zeros((1, FPAD - SUB), F32)]), (8, FPAD))
     fgot = [net.send(fcb, fcbs.at[h.y], d) for d in ys]
     fcbs[h.y] = fcb[...]
     lane = lax.broadcasted_iota(jnp.int32, (1, FRAME), 1)
     qb, vb = (
         jnp.where(
-            (lane < 192) | last, pick([bias[k : k + 1, 192 * p : 192 * p + FRAME] for p in range(8)], h.p), 0.0
+            (lane < 192) | last, pick([v[:, 192 * p : 192 * p + FRAME] for p in range(8)], h.p), 0.0
         )
-        for k in (0, 1)
+        for v in (qbias[...].reshape(1, D), vbias[...].reshape(1, D))
     )
     qkvb = (qb, jnp.zeros_like(qb), vb)
 
@@ -560,23 +574,49 @@
             ref = wt.at[wrow(kind, start + off, size // 2)]
             by_z.setdefault(kind, []).append(net.send(ref, ref, d, send_if=cond, recv_if=cond))
 
+    gather.relays()
     for kind in range(3):
         take_frames(kind)
         pass_y(kind)
     gather.ready(0)
     gather.ready(1)
+    ffs = by_gx(lambda g: fbuf.at[g], lambda g: rff.at[g])
+    rff[h.gx] = fbuf[h.gx]
     for kind in range(3):
         pass_z(kind, 0)
+    gather.ready(2)
+    gather.ready(3)
     grds = by_gx(lambda g: grd.at[:, lanes_of(g)], lambda g: rg.at[g])
     grd_own = pltpu.make_async_copy(grd.at[:, lanes_of(h.gx)], rg.at[h.gx], loc.at[3])
     grd_own.start()
+    for c in vgot:
+        c.got()
+    vecs[...] = join([rv[g] for g in range(4)])
+
+    for xh in range(2):
+
+        @pl.loop(0, 4)
+        def _(j, xh=xh):
+            blocks = []
+            for g in range(4):
+                r, l = raw_at(4 * xh + g)
+                blocks.append(fw[r, pl.ds(pl.multiple_of(l.start + ROWS * j, ROWS), ROWS)])
+            x = jnp.transpose(jnp.concatenate(blocks, axis=0))
+            normed, _ = stats(x.astype(F32))
+            fs[cut(512 * xh + ROWS * j, ROWS)] = (normed * vecs[0:1] + vecs[1:2]).astype(BF)
+
+            @pl.when(h.p == 4 * xh + j)
+            def _():
+                rows[...] = x
+
+    for d in ys + [zm, zp]:
+        pl.semaphore_signal(hx, inc=1, device_id=d, device_id_type=MESH)
     for k in (1, 2):
         for kind in range(3):
             pass_z(kind, k)
-    gather.ready(2)
-    gather.ready(3)
     take_frames(3)
     pass_y(3)
+    pl.semaphore_wait(hx, 5)
 
     for c in ffs:
         c.got()
@@ -691,8 +731,6 @@
     sa = Scatter(h, net, (a0, a1, a2, a3))
     for j in range(4):
         sa.term(j, total(hid, 1))
-    sb.relayed()
-
     one = {}
     for d in (2, 1, 3, 0):
         y = lax.rem(h.y + d, 4)
@@ -704,6 +742,8 @@
             net.send(fw.at[cut(base + off, size)], land.at[pl.ds(off, size)], to)
             for off, size, to in ((0, A_ROWS, zm), (A_ROWS, B_ROWS, zp))
         ]
+        if d == 2:
+            sb.relayed()
 
     load = pltpu.make_async_copy(saved, fs, loc.at[1])
     load.start()
@@ -1049,11 +1089,11 @@
     total_v = vx[0]
     for p in range(1, 8):
         total_v = total_v + vx[p]
-    vsum[...] = pick([total_v[:, QUARTER * g : QUARTER * (g + 1)] for g in range(4)], h.gx)
+    small[0:8, 0:QUARTER] = pick([total_v[:, QUARTER * g : QUARTER * (g + 1)] for g in range(4)], h.gx)
     for k in (0, 1):
         parts = [vx[p, k : k + 1, 1664 : 1664 + (FRAME if p == 7 else 192)] for p in range(8)]
-        qsum[k : k + 1] = join(parts)
-    fsum[...] = join([vx[4 * h.xh + g, pl.ds(2 + h.y, 1), 1664 : 1664 + SUB] for g in range(4)])
+        small[8 + k : 9 + k] = join(parts)
+    small[10:11, 0 : 4 * SUB] = join([vx[4 * h.xh + g, pl.ds(2 + h.y, 1), 1664 : 1664 + SUB] for g in range(4)])
     for i in range(4):
         p, _ = h.unit(i)
         for c in wfive[i]:
@@ -1074,7 +1114,7 @@
     net.finish()
 
 
-def layer(segs, tok, grd, wq, wp, fcw, otw, vec, bias):
+def layer(*args):
     any_ = pl.BlockSpec(memory_space=pl.ANY)
     scratch = [
         pltpu.VMEM((SEQ, D), BF),
@@ -1094,6 +1134,7 @@
         *Scatter.scratch(),
         pltpu.VMEM((4, QUARTER, ROWS), BF),
         pltpu.VMEM((4, QUARTER, ROWS), BF),
+        pltpu.VMEM((8, QUARTER), F32),
         pltpu.VMEM((2, 4, HALF + EXTRA, QUARTER), BF),
         pltpu.VMEM((4, FPAD, QUARTER), BF),
         pltpu.VMEM((4, FRAME, QUARTER), BF),
@@ -1132,6 +1173,7 @@
         pltpu.SemaphoreType.REGULAR,
         pltpu.SemaphoreType.REGULAR,
         pltpu.SemaphoreType.REGULAR,
+        pltpu.SemaphoreType.REGULAR,
     ]
     return pl.pallas_call(
         layer_kernel,
@@ -1141,50 +1183,45 @@
             jax.ShapeDtypeStruct((QUARTER, 4 * SUB), BF),
             jax.ShapeDtypeStruct((QUARTER, 4 * SUB), BF),
             jax.ShapeDtypeStruct((QUARTER, 4 * SUB), BF),
-            jax.ShapeDtypeStruct((8, QUARTER), F32),
-            jax.ShapeDtypeStruct((2, D), F32),
-            jax.ShapeDtypeStruct((1, 4 * SUB), F32),
+            jax.ShapeDtypeStruct((16, D), F32),
             jax.ShapeDtypeStruct((2, 4, FPAD, QUARTER), BF),
             jax.ShapeDtypeStruct((SEQ, D), BF),
         ],
-        in_specs=[VMEM, any_, any_, VMEM, VMEM, any_, any_, VMEM, VMEM],
-        out_specs=[any_, any_, any_, any_, any_, VMEM, VMEM, VMEM, any_, any_],
+        in_specs=[VMEM, any_, any_, VMEM, VMEM, any_, any_] + [VMEM] * 9,
+        out_specs=[any_, any_, any_, any_, any_, VMEM, any_, any_],
         scratch_shapes=scratch,
         compiler_params=pltpu.CompilerParams(
             collective_id=0, has_side_effects=True, vmem_limit_bytes=64 * 2**20 - 2**16
         ),
         name="layer",
-    )(segs, tok, grd, wq, wp, fcw, otw, vec, bias)
+    )(*args)
 
 
 def per_device(
     tokens_in, segments, norm1_gain, norm1_bias, qkv_weight, query_bias, value_bias, proj_weight,
     proj_bias, norm2_gain, norm2_bias, fc_weight, fc_bias, out_weight, out_bias, out_grad,
 ):
-    zero = jnp.zeros_like(norm1_gain)
-    vec = jnp.stack(
-        [norm1_gain, norm1_bias, proj_bias, norm2_gain, norm2_bias, out_bias, zero, zero]
-    )
-    bias = jnp.stack([query_bias, value_bias, jnp.pad(fc_bias, (0, D - 4 * SUB))])
-    layer_out, input_grad, gwa, gfc, got, vsum, qsum, fsum, _, _ = layer(
-        segments, tokens_in.T, out_grad.T, qkv_weight, proj_weight, fc_weight, out_weight, vec, bias
+    layer_out, input_grad, gwa, gfc, got, small, _, _ = layer(
+        segments, tokens_in.T, out_grad.T, qkv_weight, proj_weight, fc_weight, out_weight,
+        norm1_gain, norm1_bias, proj_bias, norm2_gain, norm2_bias, out_bias,
+        query_bias, value_bias, fc_bias,
     )
     return (
         layer_out.T,
         input_grad.T.astype(F32),
-        vsum[0],
-        vsum[1],
+        small[0, :QUARTER],
+        small[1, :QUARTER],
         gwa[:, : 3 * SUB].astype(F32),
-        qsum[0],
-        qsum[1],
+        small[8],
+        small[9],
         gwa[:, 3 * SUB :].astype(F32),
-        vsum[4],
-        vsum[2],
-        vsum[3],
+        small[4, :QUARTER],
+        small[2, :QUARTER],
+        small[3, :QUARTER],
         gfc.astype(F32),
-        fsum[0],
+        small[10, : 4 * SUB],
         got.astype(F32),
-        vsum[5],
+        small[5, :QUARTER],
     )
 
 

time: 318 us -> 309 us (0.972)
  Pallas kernels: 295 us -> 291 us
    pallas_call x1, Pallas kernels: 295 us -> 291 us  [layer(): pl.pallas_call(layer_kernel, out_shape=[jax.ShapeDtypeStruct((QUARTER, 4...]
where the time goes in v4:
time: 309 us; the launch traced here: 304 us
  Pallas kernels  291 us (94%)
  other arithmetic  7.34 us (2%)
  local copies, waits for them, and re-layouts  5.23 us (2%)
    pallas_call x1, Pallas kernels, layer(): pl.pallas_call(layer_kernel, out_shape=[jax.ShapeDtypeStruct((QUARTER, 4...  291 us

profile of v4, /device:TPU:27, one launch (start us, length us, event | category | flops | bytes accessed | tf_op | source)
XLA Modules:
  0.0 304.2 jit_solution(5475311308435142591)
XLA Ops:
  0.7 290.8 %layer.1 = (bf16[400,512]{1,0:T(8,128)(2,1)}, bf16[400,512]{1,0:T(8,128)(2,1)}, bf16[400,800]{1,0:T(8,128)(2,1)}, bf16[400,800]{1,0:T(8,128)(2,1)}, bf16[400,800...) custom-call(s32[1,128]{1,0:T(1,128)} %segs.1, ...), custom_call_target="tpu_custom_call" | custom-call | tf_op jit(solution)/shard_map/layer/pallas_call | solution.py:1178
  291.4 0.0 copy-start.3
  291.4 1.4 slice_reduce_fusion.2
  292.8 1.5 fusion
  294.4 1.5 slice_reduce_fusion
  295.9 0.0 copy-start.1
  295.9 1.9 slice_convert_fusion.1
  297.8 2.1 slice_convert_fusion
  299.9 0.0 copy-done.3
  299.9 0.0 copy-start
  299.9 1.0 convert_bitcast_fusion
  300.9 0.0 copy-done.1
  300.9 0.0 copy-start.2
  300.9 1.2 convert_element_type.22
  302.1 0.0 copy-done
  302.1 1.2 convert_element_type.23
  303.3 0.0 copy-done.2
  303.3 0.8 copy.32
Async XLA Ops:
  291.4 8.5 %copy-start.3 = (bf16[400,512]{1,0:T(8,128)(2,1)S(1)}, bf16[400,512]{1,0:T(8,128)(2,1)}, u32[]{:S(2)}) copy-start(bf16[400,512]{1,0:T(8,128)(2,1)} %get-tuple-element.22) | copy-start | bytes 1228804
  295.9 5.0 %copy-start.1 = (bf16[400,800]{1,0:T(8,128)(2,1)S(1)}, bf16[400,800]{1,0:T(8,128)(2,1)}, u32[]{:S(2)}) copy-start(bf16[400,800]{1,0:T(8,128)(2,1)} %get-tuple-element.25) | copy-start | bytes 1920004
  299.9 2.2 copy-start
  300.9 2.4 copy-start.2

commit v5 on v4

--- a/solution.py
+++ b/solution.py
@@ -226,18 +226,32 @@
         return lax.rem(h.x + 2, 4)
 
 
-def raw_at(p, half=None):
-    rows, lanes = QUARTER * (p // 3), 512 * (p % 3 if isinstance(p, int) else lax.rem(p, 3))
-    if isinstance(p, int):
+def raw_at(g, half=None):
+    if isinstance(g, int):
+        rows, lanes = QUARTER * (g // 3), 512 * (g % 3)
         return slice(rows, rows + QUARTER), slice(lanes, lanes + 512)
+    rows, lanes = QUARTER * (g // 3), 512 * lax.rem(g, 3)
     if half is None:
         return cut(rows, QUARTER), pl.ds(pl.multiple_of(lanes, 256), 512)
     return cut(rows, QUARTER), pl.ds(pl.multiple_of(lanes + 256 * half, 256), 256)
 
 
 class RawGather(Gather):
-    def ref(self, dx, half):
-        return self.buf.at[raw_at(lax.rem(self.h.x + 4 + dx, 4) * 2 + self.h.c, half)]
+    def go(self, dx, d, half=None):
+        x = lax.rem(self.h.x + 4 + dx, 4)
+        where = raw_at(lax.rem(x, 2) * 2 + self.h.c, half)
+        copies = []
+        for xh in range(2):
+            ref = self.buf[xh].at[where]
+            i = self.net.n
+            c = self.net.make(ref, ref, d)
+            if xh:
+                self.net.n -= 1
+                self.net.copies.pop()
+                c.desc = push(ref, ref, self.net.ss.at[i - 1], self.net.rs.at[i - 1], d)
+            pl.when(x // 2 == xh)(c.desc.start)
+            copies.append(c)
+        return copies[0]
 
 
 class Scatter:
@@ -364,7 +378,7 @@
         a0, a1, a2, a3, b0, b1, b2, b3,
         rt, rg, vec, rwa, rff, frames, tsend, trecv, scr, t32, stage, fbuf, rv, vecs, seg, fcb, fcbs,
         res, gsave, rows, yr, s2, wx, tl, v0, vy, vz, vx,
-        ss, rs, rsw, rsx, rseg, rsm, rsn, rst, loc, hz, hb, hy, ho, hx,
+        ss, rs, rsw, rsx, rseg, rsm, rsn, rst, loc, hz, hb, hy, ho,
     ) = refs
     h = Here()
     net = Net(ss, rs)
@@ -386,9 +400,13 @@
     def _():
         pltpu.make_async_copy(otw, stage, loc.at[0]).start()
 
-    mine_raw = fw.at[raw_at(h.p)]
-    tok_own = pltpu.make_async_copy(tok, mine_raw, loc.at[2])
-    tok_own.start()
+    raws = (ba, b0)
+    for k in range(2):
+
+        @pl.when(h.xh == k)
+        def _(k=k):
+            pltpu.make_async_copy(tok, raws[k].at[raw_at(h.gx)], loc.at[2]).start()
+
     vec[...] = jnp.concatenate(
         [v[...].reshape(1, QUARTER) for v in (g1, c1, pb, g2, c2, ob)] + [jnp.zeros((2, QUARTER), F32)], axis=0
     )
@@ -448,7 +466,12 @@
     blank = jnp.zeros((FPAD - SUB, QUARTER), F32)
     for g in range(4):
         fbuf[g] = jnp.concatenate([turned[SUB * g : SUB * (g + 1)], blank], axis=0).astype(BF)
-    tok_own.wait()
+    for k in range(2):
+
+        @pl.when(h.xh == k)
+        def _(k=k):
+            pltpu.make_async_copy(tok, raws[k].at[raw_at(h.gx)], loc.at[2]).wait()
+
     pl.semaphore_wait(barrier, len(everyone))
 
     tail = net.send(tsend, trecv, (h.z, h.gx, lax.rem(h.gy + 1, 8)))
@@ -461,7 +484,7 @@
 
     for i in (1, 2):
         send_frame(i)
-    gather = RawGather(h, net, fw)
+    gather = RawGather(h, net, raws)
     gather.start()
     vgot = [net.send(vec, rv.at[h.gx], h.gxd(d)) for d in (1, 2, 3)]
     rv[h.gx] = vec[...]
@@ -584,39 +607,17 @@
     rff[h.gx] = fbuf[h.gx]
     for kind in range(3):
         pass_z(kind, 0)
+
     gather.ready(2)
     gather.ready(3)
     grds = by_gx(lambda g: grd.at[:, lanes_of(g)], lambda g: rg.at[g])
     grd_own = pltpu.make_async_copy(grd.at[:, lanes_of(h.gx)], rg.at[h.gx], loc.at[3])
     grd_own.start()
-    for c in vgot:
-        c.got()
-    vecs[...] = join([rv[g] for g in range(4)])
-
-    for xh in range(2):
-
-        @pl.loop(0, 4)
-        def _(j, xh=xh):
-            blocks = []
-            for g in range(4):
-                r, l = raw_at(4 * xh + g)
-                blocks.append(fw[r, pl.ds(pl.multiple_of(l.start + ROWS * j, ROWS), ROWS)])
-            x = jnp.transpose(jnp.concatenate(blocks, axis=0))
-            normed, _ = stats(x.astype(F32))
-            fs[cut(512 * xh + ROWS * j, ROWS)] = (normed * vecs[0:1] + vecs[1:2]).astype(BF)
-
-            @pl.when(h.p == 4 * xh + j)
-            def _():
-                rows[...] = x
-
-    for d in ys + [zm, zp]:
-        pl.semaphore_signal(hx, inc=1, device_id=d, device_id_type=MESH)
     for k in (1, 2):
         for kind in range(3):
             pass_z(kind, k)
     take_frames(3)
     pass_y(3)
-    pl.semaphore_wait(hx, 5)
 
     for c in ffs:
         c.got()
@@ -634,6 +635,25 @@
         for off, size, to in ((0, A_ROWS, zm), (A_ROWS, B_ROWS, zp)):
             ref = fw.at[cut(base + off, size)]
             ff_z.append(net.send(ref, ref, to))
+    for c in vgot:
+        c.got()
+    vecs[...] = join([rv[g] for g in range(4)])
+
+    for xh in range(2):
+
+        @pl.loop(0, 4)
+        def _(j, xh=xh):
+            blocks = []
+            for g in range(4):
+                r, l = raw_at(g)
+                blocks.append(raws[xh][r, pl.ds(pl.multiple_of(l.start + ROWS * j, ROWS), ROWS)])
+            x = jnp.transpose(jnp.concatenate(blocks, axis=0))
+            normed, _ = stats(x.astype(F32))
+            fs[cut(512 * xh + ROWS * j, ROWS)] = (normed * vecs[0:1] + vecs[1:2]).astype(BF)
+
+            @pl.when(h.p == 4 * xh + j)
+            def _():
+                rows[...] = x
 
     @pl.when(jnp.logical_not(alone))
     def _():
@@ -947,19 +967,6 @@
     three.gone()
 
     spans = ((HALF * par, half_own, 0, HALF, None), (192 + EXTRA * par, extra_own, HALF, EXTRA, last))
-    for c in vys:
-        c.got()
-    vz[h.z] = (vy[0] + vy[1]) + (vy[2] + vy[3])
-    vzs = [net.send(vz.at[h.z], vz.at[h.z], h.rel(dz=d)) for d in (1, 2, 3)]
-
-    ffo_own.wait()
-    for c in four:
-        c.got()
-    five = []
-    for at, size, to in ((0, A_ROWS, zm), (A_ROWS, B_ROWS, zp)):
-        ref = ffo.at[par, :, pl.ds(at, size)]
-        five.append(net.send(ref, ref, to))
-
     pl.semaphore_wait(ho, 1)
     wthree = {}
     for kind in range(4):
@@ -982,6 +989,19 @@
                     s2.at[pl.ds(low_at, size)], wx.at[pl.ds(low_at, size)], zo, send_if=ok, recv_if=ok
                 )
             )
+
+    for c in vys:
+        c.got()
+    vz[h.z] = (vy[0] + vy[1]) + (vy[2] + vy[3])
+    vzs = [net.send(vz.at[h.z], vz.at[h.z], h.rel(dz=d)) for d in (1, 2, 3)]
+
+    ffo_own.wait()
+    for c in four:
+        c.got()
+    five = []
+    for at, size, to in ((0, A_ROWS, zm), (A_ROWS, B_ROWS, zp)):
+        ref = ffo.at[par, :, pl.ds(at, size)]
+        five.append(net.send(ref, ref, to))
 
     for c in vzs:
         c.got()
@@ -1173,7 +1193,6 @@
         pltpu.SemaphoreType.REGULAR,
         pltpu.SemaphoreType.REGULAR,
         pltpu.SemaphoreType.REGULAR,
-        pltpu.SemaphoreType.REGULAR,
     ]
     return pl.pallas_call(
         layer_kernel,

time: 309 us -> 308 us (level)
  no operation moved by 1% of the time
where the time goes in v5:
time: 308 us; the launch traced here: 305 us
  Pallas kernels  292 us (95%)
  other arithmetic  7.34 us (2%)
  local copies, waits for them, and re-layouts  5.23 us (2%)
    pallas_call x1, Pallas kernels, layer(): pl.pallas_call(layer_kernel, out_shape=[jax.ShapeDtypeStruct((QUARTER, 4...  292 us

profile of v5, /device:TPU:27, one launch (start us, length us, event | category | flops | bytes accessed | tf_op | source)
XLA Modules:
  0.0 305.3 jit_solution(16895634152750760225)
XLA Ops:
  0.7 291.8 %layer.1 = (bf16[400,512]{1,0:T(8,128)(2,1)}, bf16[400,512]{1,0:T(8,128)(2,1)}, bf16[400,800]{1,0:T(8,128)(2,1)}, bf16[400,800]{1,0:T(8,128)(2,1)}, bf16[400,800...) custom-call(s32[1,128]{1,0:T(1,128)} %segs.1, ...), custom_call_target="tpu_custom_call" | custom-call | tf_op jit(solution)/shard_map/layer/pallas_call | solution.py:1197
  292.5 0.0 copy-start.3
  292.5 1.4 slice_reduce_fusion.2
  293.9 1.5 fusion
  295.4 1.5 slice_reduce_fusion
  297.0 0.0 copy-start.1
  297.0 1.9 slice_convert_fusion.1
  298.9 2.1 slice_convert_fusion
  300.9 0.0 copy-done.3
  300.9 0.0 copy-start
  300.9 1.0 convert_bitcast_fusion
  301.9 0.0 copy-done.1
  301.9 0.0 copy-start.2
  301.9 1.2 convert_element_type.22
  303.1 0.0 copy-done
  303.1 1.2 convert_element_type.23
  304.3 0.0 copy-done.2
  304.3 0.8 copy.32
Async XLA Ops:
  292.5 8.5 %copy-start.3 = (bf16[400,512]{1,0:T(8,128)(2,1)S(1)}, bf16[400,512]{1,0:T(8,128)(2,1)}, u32[]{:S(2)}) copy-start(bf16[400,512]{1,0:T(8,128)(2,1)} %get-tuple-element.22) | copy-start | bytes 1228804
  297.0 5.0 %copy-start.1 = (bf16[400,800]{1,0:T(8,128)(2,1)S(1)}, bf16[400,800]{1,0:T(8,128)(2,1)}, u32[]{:S(2)}) copy-start(bf16[400,800]{1,0:T(8,128)(2,1)} %get-tuple-element.25) | copy-start | bytes 1920004
  300.9 2.2 copy-start
  301.9 2.4 copy-start.2
